TPU v7x, 32 devices: a whole 2x2x4 slice. The times are simulated.
32 devices in a mesh: batch: 8 (over z, y), tensor: 4 (over x, core).
Axes of the slice: x: 2, y: 2, z: 4, core: 2. Of those that a mesh axis runs over, the one named last changes fastest.
Arguments:
- tokens: bfloat16 [16384, 768], P(('batch', 'tensor')), may hold values from -6 to 6
- out_cotangent: bfloat16 [16384, 768], P(('batch', 'tensor')), may hold values from -6 to 6
- ln_gain: bfloat16 [768], replicated, may hold values from 0.25 to 1.75
- qkv_weight: bfloat16 [768, 2304], P(None, 'tensor'), may hold values from -0.21875 to 0.21875
- q_gain: bfloat16 [768], P('tensor'), may hold values from 0.099609375 to 1.8984375
- k_gain: bfloat16 [768], P('tensor'), may hold values from 0.099609375 to 1.8984375
- attn_out: bfloat16 [768, 768], P('tensor'), may hold values from -1.75 to 1.75
- mlp_in: bfloat16 [768, 3072], P(None, 'tensor'), may hold values from -0.21875 to 0.21875
- mlp_bias: bfloat16 [3072], P('tensor'), may hold values from -3 to 3
- mlp_out: bfloat16 [3072, 768], P('tensor'), may hold values from -0.109375 to 0.109375
- out_bias: bfloat16 [768], replicated, may hold values from -3 to 3
- image_len: int32 [80], replicated, may hold values from 0 to 1024, as said below
- image_group: int32 [80], replicated, may hold values from 0 to 7, as said below
Outputs:
- output: bfloat16 [16384, 768], P(('batch', 'tensor'))
- input_grad: bfloat16 [16384, 768], P(('batch', 'tensor'))
- ln_gain_grad: float32 [768], replicated
- qkv_grad: float32 [768, 2304], P(None, 'tensor')
- q_gain_grad: float32 [768], P('tensor')
- k_gain_grad: float32 [768], P('tensor')
- attn_out_grad: float32 [768, 768], P('tensor')
- mlp_in_grad: float32 [768, 3072], P(None, 'tensor')
- mlp_bias_grad: float32 [3072], P('tensor')
- mlp_out_grad: float32 [3072, 768], P('tensor')
- out_bias_grad: float32 [768], replicated
Inputs may be any that keep to these rules, and one draw needn't show every extreme that they name: `image_len`: each entry is 0, 196 or 1024; every draw holds an image of 1024 tokens; the entries of one group never total more than 2048. `image_group`: each group index is named by exactly 10 entries.
All inputs are finite; a program needn't handle non-finite values.
Results may differ from a plain program's by a relative error of at most 0.015.
Values may be sent and summed in bfloat16 or wider, within the bound.
A program may use at most 128 MiB of HBM per device.

v0:
```python
import functools

import jax
import jax.numpy as jnp
from jax import lax
from jax.experimental import pallas as pl
from jax.experimental.pallas import tpu as pltpu
from jax.sharding import PartitionSpec as P

DH = 64
LANES = 128
WIN = 64
LOG2E = 1.4426950408889634
epsilon = 1e-06
F32 = jnp.float32
BF16 = jnp.bfloat16
VMEM = pl.BlockSpec(memory_space=pltpu.VMEM)
SMEM = pl.BlockSpec(memory_space=pltpu.SMEM)
ANY = pl.BlockSpec(memory_space=pl.ANY)


def nn(left, right):
    return lax.dot_general(left, right, (((1,), (0,)), ((), ())), preferred_element_type=F32)


def nt(left, right):
    return lax.dot_general(left, right, (((1,), (1,)), ((), ())), preferred_element_type=F32)


def tn(left, right):
    return lax.dot_general(left, right, (((0,), (0,)), ((), ())), preferred_element_type=F32)


def find_segments(len_ref, group_ref, seg_ref, strips, tok_dev):
    group = lax.axis_index("batch")

    def entry(i, carry):
        count, run = carry
        rows = jnp.where(group_ref[i] == group, len_ref[i] // strips, 0)

        @pl.when(rows > 0)
        def _():
            seg_ref[0, count] = run
            seg_ref[1, count] = run + rows

        return count + jnp.where(rows > 0, 1, 0), run + rows

    count, run = lax.fori_loop(0, len_ref.shape[0], entry, (jnp.int32(0), jnp.int32(0)))

    @pl.when(run < tok_dev)
    def _():
        seg_ref[0, count] = run
        seg_ref[1, count] = tok_dev

    return count + jnp.where(run < tok_dev, 1, 0)


def window(start, end, first, i, tok_dev):
    nominal = first + WIN * i
    at = pl.multiple_of(jnp.minimum(nominal, tok_dev - WIN), 16)
    return at, jnp.maximum(start, nominal) - at, jnp.minimum(end, nominal + WIN) - at


def row_mask(low, high, strips, width=LANES):
    j = lax.broadcasted_iota(jnp.int32, (strips, WIN, width), 1).reshape(strips * WIN, width)
    return (j >= low) & (j < high)


def tile(ref, at, h):
    strips = ref.shape[0]
    return ref[:, pl.ds(at, WIN), h * LANES : (h + 1) * LANES].reshape(strips * WIN, LANES)


def put_tile(ref, at, h, mask, value, width=LANES):
    strips = ref.shape[0]
    where = (slice(None), pl.ds(at, WIN), slice(h * LANES, h * LANES + width))
    old = ref[where].reshape(strips * WIN, width)
    ref[where] = jnp.where(mask, value.astype(ref.dtype), old).reshape(strips, WIN, width)


def attn_fwd_body(
    heads, len_ref, group_ref, qa, ka, va, do, attn_out, mlp_part_hbm, call_hbm,
    qb, dob, give, keep, attn_grad, seg, acc, ho, mlp_part, call, out_pad, grad_acc, sems,
):
    strips, tok_dev = qa.shape[0], qa.shape[1]
    loads = [pltpu.make_async_copy(mlp_part_hbm, mlp_part, sems.at[0]), pltpu.make_async_copy(call_hbm, call, sems.at[1])]
    for load in loads:
        load.start()
    count = find_segments(len_ref, group_ref, seg, strips, tok_dev)
    lane = lax.broadcasted_iota(jnp.int32, (strips * WIN, LANES), 1)
    left = lane < DH

    def finish(h, at, low, high, total):
        mask = row_mask(low, high, strips)
        rows_sum = jnp.where(left, pltpu.roll(total, DH, 1), total)
        out = jnp.where(left, total / rows_sum, 0.0)
        log_sum = jnp.log2(rows_sum)
        d_out = tile(do, at, h).astype(F32)
        out_low = out.astype(BF16)
        delta = jnp.sum(out * d_out, axis=-1, keepdims=True)
        log_hi = log_sum.astype(BF16).astype(F32)
        delta_hi = delta.astype(BF16).astype(F32)
        q = tile(qa, at, h).astype(F32)
        q = jnp.where(lane == DH, -log_hi, jnp.where(lane == DH + 1, log_hi - log_sum, q))
        d_out = jnp.where(lane == DH, -delta_hi, jnp.where(lane == DH + 1, delta_hi - delta, d_out))
        put_tile(ho, at, h, mask, out_low)
        put_tile(qb, at, h, mask, q)
        put_tile(dob, at, h, mask, d_out)

    def product(h, at_q, at_k, k_mask):
        scores = nt(tile(qa, at_q, h), tile(ka, at_k, h))
        weights = jnp.exp2(scores).astype(BF16)
        return nn(weights, jnp.where(k_mask, tile(va, at_k, h), jnp.zeros((), BF16)))

    def segment(index, _):
        start, end = seg[0, index], seg[1, index]
        first = (start // 16) * 16
        windows = (end - first + WIN - 1) // WIN

        @pl.when(windows == 1)
        def _():
            at, low, high = window(start, end, first, 0, tok_dev)
            mask = row_mask(low, high, strips)
            for h in range(heads):
                finish(h, at, low, high, product(h, at, at, mask))

        @pl.when(windows > 1)
        def _():
            def q_window(i, _):
                at_q, low_q, high_q = window(start, end, first, i, tok_dev)
                acc[...] = jnp.zeros_like(acc)

                def k_window(k, _):
                    at_k, low_k, high_k = window(start, end, first, k, tok_dev)
                    mask = row_mask(low_k, high_k, strips)
                    for h in range(heads):
                        acc[h] += product(h, at_q, at_k, mask)
                    return 0

                lax.fori_loop(0, windows, k_window, 0)
                for h in range(heads):
                    finish(h, at_q, low_q, high_q, acc[h])
                return 0

            lax.fori_loop(0, windows, q_window, 0)

        return 0

    lax.fori_loop(0, count, segment, 0)

    for h in range(heads):
        out_pad[h * LANES : h * LANES + DH, :] = attn_out[h * DH : (h + 1) * DH, :]
        out_pad[h * LANES + DH : (h + 1) * LANES, :] = jnp.zeros((DH, out_pad.shape[1]), BF16)
    for load in loads:
        load.wait()
    me = lax.axis_index("tensor")
    rows = 256
    per_strip = tok_dev // rows
    grad_acc[...] = jnp.zeros_like(grad_acc)

    def project(i, _):
        strip = i // per_strip
        at = pl.ds(pl.multiple_of(i % per_strip * rows, rows), rows)
        heads_rows = ho[strip, at]
        out = (nn(heads_rows, out_pad[...]) + mlp_part[strip, at].astype(F32)).astype(BF16)
        own = jnp.where(strip // 2 == me // 2, 1, 0)

        @pl.when(strip % 2 == me % 2)
        def _():
            keep[own, at] = out

        @pl.when(strip % 2 != me % 2)
        def _():
            give[own, at] = out

        grad_acc[...] += tn(heads_rows, call[strip, at])
        return 0

    lax.fori_loop(0, strips * per_strip, project, 0)
    for h in range(heads):
        attn_grad[h * DH : (h + 1) * DH, :] = grad_acc[h * LANES : h * LANES + DH, :].astype(BF16)


def attn_fwd(image_len, image_group, qa, ka, va, do, attn_out, mlp_part, call):
    strips, tok_dev, width = qa.shape
    heads = width // LANES
    features = call.shape[2]
    like = jax.ShapeDtypeStruct(qa.shape, BF16)
    half = jax.ShapeDtypeStruct((strips // 2, tok_dev, features), BF16)
    return pl.pallas_call(
        functools.partial(attn_fwd_body, heads),
        out_shape=(like, like, half, half, jax.ShapeDtypeStruct(attn_out.shape, BF16)),
        in_specs=[SMEM, SMEM] + [VMEM] * 5 + [ANY] * 2,
        out_specs=(VMEM,) * 5,
        scratch_shapes=[
            pltpu.SMEM((2, image_len.shape[0] + 1), jnp.int32),
            pltpu.VMEM((heads, strips * WIN, LANES), F32),
            pltpu.VMEM(qa.shape, BF16),
            pltpu.VMEM(call.shape, BF16),
            pltpu.VMEM(call.shape, BF16),
            pltpu.VMEM((width, features), BF16),
            pltpu.VMEM((width, features), F32),
            pltpu.SemaphoreType.DMA((2,)),
        ],
        compiler_params=pltpu.CompilerParams(vmem_limit_bytes=56 << 20),
        cost_estimate=pl.CostEstimate(flops=8 * 10**9, bytes_accessed=30 * 10**6, transcendentals=8 * 10**6),
        name="attention_forward",
    )(image_len, image_group, qa, ka, va, do, attn_out, mlp_part, call)


def attn_bwd_body(
    heads, len_ref, group_ref, qb, ka, va, dob, uq, uk, gq, gk,
    d_qkv, gain_grad, seg, k_turned, dq_turned, dk_acc, dv_acc, dq, dk, dv,
):
    strips, tok_dev = qb.shape[0], qb.shape[1]
    count = find_segments(len_ref, group_ref, seg, strips, tok_dev)
    zero = jnp.zeros((), BF16)

    def products(h, at_q, at_k, q_mask, k_turned_h):
        q = tile(qb, at_q, h)
        d_out = jnp.where(q_mask, tile(dob, at_q, h), zero)
        weights = jnp.exp2(nt(tile(ka, at_k, h), q))
        d_weights = nt(tile(va, at_k, h), d_out)
        d_scores = (weights * d_weights).astype(BF16)
        return nn(k_turned_h, d_scores), nn(d_scores, q), nn(weights.astype(BF16), d_out)

    def turned(h, at_k, mask):
        return jnp.where(mask, tile(ka, at_k, h), zero).T[:DH]

    def segment(index, _):
        start, end = seg[0, index], seg[1, index]
        first = (start // 16) * 16
        windows = (end - first + WIN - 1) // WIN

        @pl.when(windows == 1)
        def _():
            at, low, high = window(start, end, first, 0, tok_dev)
            mask = row_mask(low, high, strips)
            half = row_mask(low, high, strips, DH)
            for h in range(heads):
                dq_t, dk_new, dv_new = products(h, at, at, mask, turned(h, at, mask))
                put_tile(dq, at, h, half, dq_t.T, DH)
                put_tile(dk, at, h, mask, dk_new)
                put_tile(dv, at, h, mask, dv_new)

        @pl.when(windows > 1)
        def _():
            def clear(i, _):
                for h in range(heads):
                    dq_turned[h, i] = jnp.zeros(dq_turned.shape[2:], F32)
                return 0

            lax.fori_loop(0, windows, clear, 0)

            def k_window(k, _):
                at_k, low_k, high_k = window(start, end, first, k, tok_dev)
                mask_k = row_mask(low_k, high_k, strips)
                for h in range(heads):
                    k_turned[h] = turned(h, at_k, mask_k)
                dk_acc[...] = jnp.zeros_like(dk_acc)
                dv_acc[...] = jnp.zeros_like(dv_acc)

                def q_window(i, _):
                    at_q, low_q, high_q = window(start, end, first, i, tok_dev)
                    mask_q = row_mask(low_q, high_q, strips)
                    for h in range(heads):
                        dq_t, dk_new, dv_new = products(h, at_q, at_k, mask_q, k_turned[h])
                        dq_turned[h, i] += dq_t
                        dk_acc[h] += dk_new
                        dv_acc[h] += dv_new
                    return 0

                lax.fori_loop(0, windows, q_window, 0)
                for h in range(heads):
                    put_tile(dk, at_k, h, mask_k, dk_acc[h])
                    put_tile(dv, at_k, h, mask_k, dv_acc[h])
                return 0

            lax.fori_loop(0, windows, k_window, 0)

            def q_out(i, _):
                at_q, low_q, high_q = window(start, end, first, i, tok_dev)
                half = row_mask(low_q, high_q, strips, DH)
                for h in range(heads):
                    put_tile(dq, at_q, h, half, dq_turned[h, i].T, DH)
                return 0

            lax.fori_loop(0, windows, q_out, 0)

        return 0

    lax.fori_loop(0, count, segment, 0)

    rows = strips * WIN
    lane = lax.broadcasted_iota(jnp.int32, (rows, LANES), 1)
    left = lane < DH

    def norm_back(d_rows, u_ref, gain, at, h):
        u = tile(u_ref, at, h).astype(F32)
        rstd = pltpu.roll(u, DH, 1)
        d_rows = jnp.where(left, d_rows, 0.0)
        scaled = d_rows * gain
        mean = jnp.sum(scaled, axis=-1, keepdims=True) * (1.0 / DH)
        mean_u = jnp.sum(scaled * u, axis=-1, keepdims=True) * (1.0 / DH)
        return (scaled - mean - u * mean_u) * rstd, jnp.sum(d_rows * u, axis=0, keepdims=True)

    gain_grad[...] = jnp.zeros_like(gain_grad)

    def chunk(i, _):
        at = pl.multiple_of(i * WIN, WIN)
        parts = []
        for h in range(heads):
            cols = slice(h * LANES, (h + 1) * LANES)
            d_q, g_q = norm_back(tile(dq, at, h), uq, gq[:, cols], at, h)
            d_k, g_k = norm_back(tile(dk, at, h) * (1.0 / LOG2E), uk, gk[:, cols], at, h)
            gain_grad[0:1, cols] += g_q * DH ** (-0.5)
            gain_grad[1:2, cols] += g_k
            parts += [d_q, d_k, tile(dv, at, h)]
        if len(parts) % 2:
            parts.append(jnp.zeros_like(parts[0]))
        for b in range(len(parts) // 2):
            block = jnp.where(left, parts[2 * b], pltpu.roll(parts[2 * b + 1], DH, 1))
            d_qkv[:, pl.ds(at, WIN), b * LANES : (b + 1) * LANES] = block.astype(BF16).reshape(strips, WIN, LANES)
        return 0

    lax.fori_loop(0, tok_dev // WIN, chunk, 0)


def attn_bwd(image_len, image_group, qb, ka, va, dob, uq, uk, gq, gk):
    strips, tok_dev, width = qb.shape
    heads = width // LANES
    blocks = (3 * heads + 1) // 2
    rows = strips * WIN
    windows = tok_dev // WIN + 1
    full = pltpu.VMEM((strips, tok_dev, width), F32)
    return pl.pallas_call(
        functools.partial(attn_bwd_body, heads),
        out_shape=(
            jax.ShapeDtypeStruct((strips, tok_dev, blocks * LANES), BF16),
            jax.ShapeDtypeStruct((8, width), F32),
        ),
        in_specs=[SMEM, SMEM] + [VMEM] * 8,
        out_specs=(VMEM, VMEM),
        scratch_shapes=[
            pltpu.SMEM((2, image_len.shape[0] + 1), jnp.int32),
            pltpu.VMEM((heads, DH, rows), BF16),
            pltpu.VMEM((heads, windows, DH, rows), F32),
            pltpu.VMEM((heads, rows, LANES), F32),
            pltpu.VMEM((heads, rows, LANES), F32),
            full, full, full,
        ],
        compiler_params=pltpu.CompilerParams(vmem_limit_bytes=56 << 20),
        cost_estimate=pl.CostEstimate(flops=16 * 10**9, bytes_accessed=30 * 10**6, transcendentals=8 * 10**6),
        name="attention_backward",
    )(image_len, image_group, qb, ka, va, dob, uq, uk, gq, gk)


CHUNKS = 4


def remote(src, dst, send, recv, device):
    return pltpu.make_async_remote_copy(
        src_ref=src, dst_ref=dst, send_sem=send, recv_sem=recv, device_id=device, device_id_type=pl.DeviceIdType.MESH
    )


def front_body(
    heads, tokens, cot, ln_gain, qkv_weight, gq, gk, attn_out, mlp_in, mlp_bias, mlp_out,
    qa_out, ka_out, va_out, do_out, uq_out, uk_out, mlp_part_out, dn_part_out, nall_out, call_out,
    g_in_out, g_out_out, rows_out,
    both, wide, narrow, qkv_pad, mlp_out_t, mlp_in_t, attn_out_t, g_in, g_out,
    send_sem, recv_sem, save_sem,
):
    batch, me = lax.axis_index("batch"), lax.axis_index("tensor")
    sibling = me + 1 - 2 * (me % 2)
    across = (me + 2) % 4
    chip, far_chip = me // 2, 1 - me // 2
    tok_dev = tokens.shape[0]
    step = tok_dev // CHUNKS
    rows = 2 * step
    features = tokens.shape[1]
    heads_wide = heads * LANES

    def rows_of(c):
        return pl.ds(pl.multiple_of(c * step, step), step)

    def move(kind, route, c, strip, to):
        part = both.at[kind, strip, rows_of(c)]
        return remote(part, part, send_sem.at[kind, route, c], recv_sem.at[kind, route, c], (batch, to))

    barrier = pltpu.get_barrier_semaphore()
    for other in (sibling, across):
        pl.semaphore_signal(barrier, inc=1, device_id=(batch, other), device_id_type=pl.DeviceIdType.MESH)
    gain = ln_gain[...].astype(F32)

    def norm_chunk(c):
        both[0, me, rows_of(c)] = cot[rows_of(c)]
        x = tokens[rows_of(c)].astype(F32)
        centred = x - jnp.mean(x, axis=-1, keepdims=True)
        variance = jnp.mean(centred * centred, axis=-1, keepdims=True)
        both[1, me, rows_of(c)] = (centred * lax.rsqrt(variance + epsilon) * gain).astype(BF16)

    norm_chunk(0)
    pl.semaphore_wait(barrier, 2)

    def first_sends(c, _):
        for kind in range(2):
            move(kind, 1, c, me, across).start()
            move(kind, 0, c, me, sibling).start()

        @pl.when(c + 1 < CHUNKS)
        def _():
            norm_chunk(c + 1)

        return 0

    lax.fori_loop(0, CHUNKS, first_sends, 0)

    g_in[...] = jnp.zeros_like(g_in)
    g_out[...] = jnp.zeros_like(g_out)
    rows_out[...] = jnp.zeros_like(rows_out)
    total = jnp.zeros((1, features), F32)
    for c in range(CHUNKS):
        total += jnp.sum(cot[c * step : (c + 1) * step].astype(F32), axis=0, keepdims=True)
    rows_out[1:2, :] = total
    width = qkv_weight.shape[1]
    qkv_pad[:, width // LANES * LANES :] = jnp.zeros((features, qkv_pad.shape[1] - width // LANES * LANES), BF16)
    qkv_pad[:, :width] = qkv_weight[...]
    mlp_out_t[...] = mlp_out[...].T
    mlp_in_t[...] = mlp_in[...].T
    for h in range(heads):
        part = attn_out[h * DH : (h + 1) * DH, :]
        attn_out_t[:, h * LANES : (h + 1) * LANES] = jnp.concatenate([part, jnp.zeros_like(part)], axis=0).T

    lane = lax.broadcasted_iota(jnp.int32, (rows, LANES), 1)
    left = lane < DH
    bias = mlp_bias[...].astype(F32)

    def saves(c, at_chip):
        strips = pl.ds(2 * at_chip, 2)
        where = rows_of(c)
        index = at_chip * CHUNKS + c
        pairs = [(narrow.at[a, strips, where], ref.at[strips, where]) for a, ref in enumerate(
            (qa_out, ka_out, va_out, do_out, uq_out, uk_out))]
        pairs += [(wide.at[a, strips, where], ref.at[strips, where]) for a, ref in enumerate(
            (mlp_part_out, dn_part_out))]
        pairs += [(both.at[1, strips, where], nall_out.at[strips, where]), (both.at[0, strips, where], call_out.at[strips, where])]
        return [pltpu.make_async_copy(a, b, save_sem.at[n, index]) for n, (a, b) in enumerate(pairs)]

    def unit(i, _):
        far = i >= CHUNKS
        c = i % CHUNKS
        at_chip = jnp.where(far, far_chip, chip)

        @pl.when(jnp.logical_not(far))
        def _():
            for kind in range(2):
                move(kind, 0, c, sibling, sibling).wait_recv()

        def pass_on(k):
            for kind in range(2):
                move(kind, 1, k, across, across).wait_recv()
                move(kind, 2, k, across, sibling).start()

        @pl.when(i == CHUNKS - 1)
        def _():
            pass_on(0)

        @pl.when(i == CHUNKS)
        def _():
            pass_on(1)

        @pl.when(i > CHUNKS + 1)
        def _():
            pass_on(c)

        @pl.when(far)
        def _():
            for kind in range(2):
                move(kind, 2, c, across + 1 - 2 * (across % 2), sibling).wait_recv()

        strips = pl.ds(2 * at_chip, 2)
        where = rows_of(c)
        n = both[1, strips, where].reshape(rows, features)
        d = both[0, strips, where].reshape(rows, features)

        def save(ref, a, h, value):
            ref[a, strips, where, h * LANES : (h + 1) * LANES] = value.astype(BF16).reshape(2, step, LANES)

        qkv = nn(n, qkv_pad[...])

        def part(p):
            block = qkv[:, p // 2 * LANES : p // 2 * LANES + LANES]
            return pltpu.roll(block, DH, 1) if p % 2 else block

        def unit_norm(x):
            x = jnp.where(left, x, 0.0)
            centred = jnp.where(left, x - jnp.sum(x, axis=-1, keepdims=True) * (1.0 / DH), 0.0)
            rstd = lax.rsqrt(jnp.sum(centred * centred, axis=-1, keepdims=True) * (1.0 / DH) + epsilon)
            return centred * rstd, rstd

        for h in range(heads):
            cols = slice(h * LANES, (h + 1) * LANES)
            u, rstd = unit_norm(part(3 * h))
            save(narrow, 0, h, u * gq[:, cols])
            save(narrow, 4, h, jnp.where(left, u, rstd))
            u, rstd = unit_norm(part(3 * h + 1))
            save(narrow, 1, h, jnp.where(left, u * gk[:, cols], 1.0))
            save(narrow, 5, h, jnp.where(left, u, rstd))
            save(narrow, 2, h, jnp.where(left, part(3 * h + 2), 1.0))
        narrow[3, strips, where] = nn(d, attn_out_t[...]).astype(BF16).reshape(2, step, heads_wide)

        hidden = nn(n, mlp_in[...]) + bias
        cdf = 0.5 + 0.5 * lax.erf(hidden * 0.7071067811865476)
        act = (hidden * cdf).astype(BF16)
        slope = cdf + hidden * (0.3989422804014327 * jnp.exp(hidden * hidden * -0.5))
        wide[0, strips, where] = nn(act, mlp_out[...]).astype(BF16).reshape(2, step, features)
        d_hidden = nn(d, mlp_out_t[...]) * slope
        d_low = d_hidden.astype(BF16)
        rows_out[0:1, :] += jnp.sum(d_low.astype(F32), axis=0, keepdims=True)
        wide[1, strips, where] = nn(d_low, mlp_in_t[...]).astype(BF16).reshape(2, step, features)
        g_out[...] += tn(act, d)
        g_in[...] += tn(n, d_low)
        for copy in saves(c, at_chip):
            copy.start()
        return 0

    lax.fori_loop(0, 2 * CHUNKS, unit, 0)

    g_in_out[...] = g_in[...].astype(BF16)
    g_out_out[...] = g_out[...].astype(BF16)

    def finish(i, _):
        for copy in saves(i % CHUNKS, i // CHUNKS):
            copy.wait()
        return 0

    lax.fori_loop(0, 2 * CHUNKS, finish, 0)

    def sent(c, _):
        for kind in range(2):
            move(kind, 0, c, me, sibling).wait_send()
            move(kind, 1, c, me, across).wait_send()
            move(kind, 2, c, across, sibling).wait_send()
        return 0

    lax.fori_loop(0, CHUNKS, sent, 0)


def front(strips, tokens, cot, ln_gain, qkv_weight, gq, gk, attn_out, mlp_in, mlp_bias, mlp_out):
    tok_dev, features = tokens.shape
    width = gq.shape[1]
    heads = width // LANES
    hidden = mlp_in.shape[1]
    blocks = (3 * heads + 1) // 2
    like = jax.ShapeDtypeStruct((strips, tok_dev, width), BF16)
    rows = jax.ShapeDtypeStruct((strips, tok_dev, features), BF16)
    return pl.pallas_call(
        functools.partial(front_body, heads),
        out_shape=(like,) * 6 + (rows,) * 4 + (
            jax.ShapeDtypeStruct((features, hidden), BF16),
            jax.ShapeDtypeStruct((hidden, features), BF16),
            jax.ShapeDtypeStruct((8, features), F32),
        ),
        in_specs=[VMEM] * 10,
        out_specs=(ANY,) * 10 + (VMEM,) * 3,
        scratch_shapes=[
            pltpu.VMEM((2, strips, tok_dev, features), BF16),
            pltpu.VMEM((2, strips, tok_dev, features), BF16),
            pltpu.VMEM((6, strips, tok_dev, width), BF16),
            pltpu.VMEM((features, blocks * LANES), BF16),
            pltpu.VMEM((features, hidden), BF16),
            pltpu.VMEM((hidden, features), BF16),
            pltpu.VMEM((features, width), BF16),
            pltpu.VMEM((features, hidden), F32),
            pltpu.VMEM((hidden, features), F32),
            pltpu.SemaphoreType.DMA((2, 3, CHUNKS)),
            pltpu.SemaphoreType.DMA((2, 3, CHUNKS)),
            pltpu.SemaphoreType.DMA((10, 2 * CHUNKS)),
        ],
        compiler_params=pltpu.CompilerParams(collective_id=0, has_side_effects=True, vmem_limit_bytes=60 << 20),
        name="gather_and_project",
    )(tokens, cot, ln_gain, qkv_weight, gq, gk, attn_out, mlp_in, mlp_bias, mlp_out)


def layer_norm(inputs, gain):
    row_mean = jnp.mean(inputs, axis=-1, keepdims=True)
    centred = inputs - row_mean
    variance = jnp.mean(centred * centred, axis=-1, keepdims=True)
    return centred * lax.rsqrt(variance + epsilon) * gain


SIBLINGS = [(0, 1), (1, 0), (2, 3), (3, 2)]
ACROSS = [(0, 2), (1, 3), (2, 0), (3, 1)]


def on_device(
    tokens, out_cotangent, ln_gain, qkv_weight, q_gain, k_gain, attn_out,
    mlp_in, mlp_bias, mlp_out, out_bias, image_len, image_group,
):
    tok_dev, features = tokens.shape
    strips = lax.axis_size("tensor")
    cap = tok_dev * strips
    heads = q_gain.shape[0] // DH
    head_width = heads * DH
    qkv_cols = qkv_weight.shape[1]

    def pad_gain(g, factor):
        g = g.astype(F32).reshape(heads, DH) * factor
        return jnp.concatenate([g, jnp.zeros_like(g)], axis=-1).reshape(1, heads * LANES)

    scale = DH ** (-0.5)
    gq, gk = pad_gain(q_gain, scale), pad_gain(k_gain, 1.0)
    (qa, ka, va, do, uq, uk, mlp_part, dn_part, nall, call, g_in, g_out, rows_out) = front(
        strips, tokens, out_cotangent, ln_gain.reshape(1, -1), qkv_weight, gq * LOG2E, gk,
        attn_out, mlp_in, mlp_bias.reshape(1, -1), mlp_out,
    )

    def over_batch(grad):
        return lax.psum(grad.astype(BF16), "batch").astype(F32)

    mlp_in_grad, mlp_out_grad, mlp_bias_grad = over_batch(g_in), over_batch(g_out), over_batch(rows_out[0])
    qb, dob, give, keep, attn_grad = attn_fwd(image_len, image_group, qa, ka, va, do, attn_out, mlp_part, call)
    got = lax.ppermute(give, "tensor", SIBLINGS)
    mine = (keep.astype(F32) + got.astype(F32)).astype(BF16)
    got = lax.ppermute(mine[0], "tensor", ACROSS)
    output = (
        tokens.astype(F32) + mine[1].astype(F32) + got.astype(F32) + out_bias.astype(F32)
    ).astype(BF16)

    d_qkv, gain_grad = attn_bwd(image_len, image_group, qb, ka, va, dob, uq, uk, gq, gk)
    gain_grad = gain_grad.reshape(8, heads, LANES)[:, :, :DH].reshape(8, head_width)
    d_qkv = d_qkv.reshape(cap, -1)[:, :qkv_cols]
    qkv_grad = tn(nall.reshape(cap, features), d_qkv)
    d_normed = lax.psum_scatter(
        (nt(d_qkv, qkv_weight) + dn_part.reshape(cap, features).astype(F32)).astype(BF16),
        "tensor", scatter_dimension=0, tiled=True,
    )
    _, ln_pull = jax.vjp(layer_norm, tokens.astype(F32), ln_gain.astype(F32))
    d_x, ln_gain_part = ln_pull(d_normed.astype(F32))
    input_grad = (out_cotangent.astype(F32) + d_x).astype(BF16)
    ln_gain_grad, out_bias_grad = lax.psum((ln_gain_part, rows_out[1]), ("batch", "tensor"))
    return (
        output,
        input_grad,
        ln_gain_grad,
        over_batch(qkv_grad),
        over_batch(gain_grad[0]),
        over_batch(gain_grad[1]),
        over_batch(attn_grad),
        mlp_in_grad,
        mlp_bias_grad,
        mlp_out_grad,
        out_bias_grad,
    )


def solution(mesh):
    rows, cols, first = P(("batch", "tensor"), None), P(None, "tensor"), P("tensor", None)
    return jax.shard_map(
        on_device,
        mesh=mesh,
        in_specs=(rows, rows, P(), cols, P("tensor"), P("tensor"), first, cols, P("tensor"), first, P(), P(), P()),
        out_specs=(rows, rows, P(), cols, P("tensor"), P("tensor"), first, cols, P("tensor"), first, P()),
        check_vma=False,
    )
```

profile of v0, /device:TPU:0, one launch (start us, length us, event | category | flops | bytes accessed | tf_op | source)
XLA Modules:
  0.0 352.0 jit_solution(14810027447367896980)
XLA Ops:
  8.0 0.0 copy-start.8
  8.0 0.0 copy-start.10
  8.0 0.0 all-reduce.7.cloned.1.call-start
  8.1 0.7 convert_multiply_fusion.2
  8.7 0.1 mul.67
  8.8 0.6 broadcast_multiply_fusion.1
  9.4 0.7 reshape.108
  10.1 0.5 copy.35
  10.7 2.2 copy.25.qkv_weight
  12.9 0.0 copy-done.8
  12.9 0.6 reshape.106.ln_gain
  13.5 0.0 copy-done.10
  13.5 0.6 reshape.111.mlp_bias
  14.1 47.4 %gather_and_project.1 = (bf16[4,512,384]{2,1,0:T(8,128)(2,1)}, bf16[4,512,384]{2,1,0:T(8,128)(2,1)}, bf16[4,512,384]{2,1,0:T(8,128)(2,1)}, bf16[4,512,384]{2,1,0...) custom-call(bf16[512,768]{1,0:T(8,128)(2,1)} %tokens.1, ...), custom_call_target="tpu_custom_call" | custom-call | tf_op jit(solution)/shard_map/gather_and_project/pallas_call | solution.py:558
  61.5 25.3 %attention_forward.1 = (bf16[4,512,384]{2,1,0:T(8,128)(2,1)}, bf16[4,512,384]{2,1,0:T(8,128)(2,1)}, bf16[2,512,768]{2,1,0:T(8,128)(2,1)}, bf16[2,512,768]{2,1,0:T(8,128)(2,1)}, bf16[192,768]{1,0:T(8,128)(2,1)}) custom-call(s32[80]{0:T(128)} %len_ref.3, s32[80]{0:T(128)} %group_ref.3, bf16[4,512,384]{2,1,0:T(8,128)(2,1)} %get-tuple-element.31.qa, ...), custom_call_target="tpu_custom_call" | custom-call | flops 8000000000 | bytes 30000000 | tf_op jit(solution)/shard_map/attention_forward/pallas_call | solution.py:190
  86.8 0.0 copy-start.11
  86.8 24.9 %attention_backward.1 = (bf16[4,512,640]{2,1,0:T(8,128)(2,1)}, f32[8,384]{1,0:T(8,128)}) custom-call(s32[80]{0:T(128)} %len_ref.3, s32[80]{0:T(128)} %group_ref.3, bf16[4,512,384]{2,1,0:T(8,128)(2,1)} %get-tuple-element.39.qb, bf16[4,512,384]{2,1,0:T(8,128)(2,1)} %get-tuple-element.32.ka, bf16[4,512,384]{2,1,0:T(8,128)(2,1)} %get-tuple-element.33.va, ...), custom_call_target="tpu_custom_call" | custom-call | flops 16000000000 | bytes 30000000 | tf_op jit(solution)/shard_map/attention_backward/pallas_call | solution.py:336
  111.7 0.0 copy-done.11
  111.7 4.7 %fusion.15 = bf16[768,576]{0,1:T(8,128)(2,1)} fusion(bf16[2048,768]{1,0:T(8,128)(2,1)S(1)} %bitcast.30, bf16[2048,640]{1,0:T(8,128)(2,1)} %bitcast.31), kind=kOutput, calls=%fused_computation.24 | convolution fusion | flops 1812381696 | bytes 6651904 | tf_op jit(solution)/shard_map/dot_general | solution.py:31
  116.4 0.0 copy-start.4
  116.4 0.0 all-reduce.7.cloned.1.call-update
  116.4 0.0 reduce-scatter.2.cloned.1.call-start
  116.5 1.1 copy-done.4
  117.6 7.0 %fusion = bf16[2048,768]{1,0:T(8,128)(2,1)} fusion(bf16[2048,768]{1,0:T(8,128)(2,1)} %bitcast.29, bf16[768,576]{0,1:T(8,128)(2,1)S(1)} %copy-done.4, bf16[2048,640]{1,0:T(8,128)(2,1)} %bitcast.32), kind=kOutput, calls=%fused_computation.1 | convolution fusion | flops 1816657920 | bytes 9797632 | tf_op jit(solution)/shard_map/dot_general | solution.py:27
  124.6 0.0 copy-start.7
  124.6 0.0 copy-start.9
  124.6 0.0 copy-start
  124.6 0.0 reduce-scatter.2.cloned.1.call-update
  124.6 0.8 collective-permute-start
  125.4 0.0 copy-done.7
  125.4 0.1 convert_element_type.108
  125.5 0.1 convert_element_type.110
  125.6 0.8 fusion.19
  126.4 56.2 %all-reduce.3 = (bf16[192]{0:T(256)(128)(2,1)S(1)}, bf16[192]{0:T(256)(128)(2,1)S(1)}, bf16[768]{0:T(1024)(128)(2,1)S(1)}) all-reduce(bf16[192]{0:T(256)(128)(2,1)S(1)} %convert_element_type.108, bf16[192]{0:T(256)(128)(2,1)S(1)} %convert_element_type.110, bf16[768]{0:T(1024)(128)(2,1)S(1)} %fusion.19), channel_id=1, replica_groups=mesh['batch'=8,'tensor'=4] {'batch'}, use_global_device_ids=true, to_apply=%region_8.0 | all-reduce | flops 1152 | bytes 4608 | tf_op jit(solution)/shard_map/psum | solution.py:620
  182.6 0.6 convert_element_type.115
  183.2 0.6 convert_element_type.109
  183.7 0.6 convert_element_type.111
  184.3 0.0 copy-done.9
  184.3 0.8 slice_reduce_fusion
  185.1 0.0 copy-done
  185.1 0.2 convert_reduce_fusion
  185.3 0.0 collective-permute-done
  185.3 0.0 copy-start.2
  185.3 1.1 copy-done.2
  186.4 2.3 add_convert_fusion
  188.7 0.9 slice_bitcast_fusion
  189.7 1.3 collective-permute-start.1
  191.0 101.5 %all-reduce.7.cloned.1.call-done = (bf16[768,576]{0,1:T(8,128)(2,1)}, bf16[192,768]{1,0:T(8,128)(2,1)}, bf16[768,768]{1,0:T(8,128)(2,1)}, bf16[768,768]{1,0:T(8,128)(2,1)}) async-done(((bf16[768,576]{0,1:T(8,128)(2,1)}, bf16[192,768]{1,0:T(8,128)(2,1)}, bf16[768,768]{1,0:T(8,128)(2,1)}, bf16[768,768]{1,0:T(8,128)(2,1)}), (bf16[768,576]{0,1:T(8,128)(2,1)}, bf16[192,768]{1,0:T(8,128)(2,1)}, ...) | async-done | bytes 3538960 | tf_op jit(solution)/shard_map/psum | solution.py:620
  292.4 0.0 copy-start.3
  292.4 2.9 convert_element_type.113
  295.4 0.0 copy-done.3
  295.4 1.6 convert_element_type.116
  297.0 0.0 copy-start.6
  297.0 0.0 copy-done.5
  297.0 1.3 convert_element_type.107
  298.3 0.0 copy-done.6
  298.3 0.9 convert_element_type.112
  299.2 0.0 reduce-scatter.2.cloned.1.call-done
  299.2 1.8 fusion.10
  301.0 0.0 copy-done.1
  301.0 0.9 fusion.9
  302.0 39.2 %all-reduce.2 = (f32[768]{0:T(1024)}, f32[768]{0:T(1024)}) all-reduce(f32[768]{0:T(1024)S(1)} %get-tuple-element.51, f32[768]{0:T(1024)S(1)} %slice_reduce_fusion), channel_id=1, replica_groups=mesh['batch'=8,'tensor'=4] {'batch','tensor'}, use_global_device_ids=true, to_apply=%region_6.0 | all-reduce | flops 1536 | bytes 12288 | tf_op jit(solution)/shard_map/psum | solution.py:642
  341.2 0.0 collective-permute-done.1
  341.2 3.3 add_convert_fusion.1
  (11 shorter events, 0.1 us)
Async XLA Ops:
  8.0 4.9 %copy-start.8 = (bf16[768]{0:T(1024)(128)(2,1)S(1)}, bf16[768]{0:T(1024)(128)(2,1)}, u32[]{:S(2)}) copy-start(bf16[768]{0:T(1024)(128)(2,1)} %param.15) | copy-start | bytes 4612
  8.0 5.5 %copy-start.10 = (bf16[768]{0:T(1024)(128)(2,1)S(1)}, bf16[768]{0:T(1024)(128)(2,1)}, u32[]{:S(2)}) copy-start(bf16[768]{0:T(1024)(128)(2,1)} %param.21) | copy-start | bytes 4612
  8.0 284.4 %all-reduce.7.cloned.1.call-start = ((), (), s32[]{:S(2)}) async-start(), calls=%async_computation.2 | async-start | bytes 7077888 | tf_op jit(solution)/shard_map/psum | solution.py:620
  86.8 24.9 %copy-start.11 = (bf16[4,512,768]{2,1,0:T(8,128)(2,1)S(1)}, bf16[4,512,768]{2,1,0:T(8,128)(2,1)}, u32[]{:S(2)}) copy-start(bf16[4,512,768]{2,1,0:T(8,128)(2,1)} %get-tuple-element.45) | copy-start | bytes 9437188
  116.4 1.2 copy-start.4
  116.4 182.7 %reduce-scatter.2.cloned.1.call-start = ((), (), s32[]{:S(2)}) async-start(), calls=%async_computation.1 | async-start | bytes 3932160 | tf_op jit(solution)/shard_map/reduce_scatter | solution.py:635
  124.6 0.8 copy-start.7
  124.6 59.7 %copy-start.9 = (bf16[768]{0:T(1024)(128)(2,1)S(1)}, bf16[768]{0:T(1024)(128)(2,1)}, u32[]{:S(2)}) copy-start(bf16[768]{0:T(1024)(128)(2,1)} %param.23) | copy-start | bytes 4612
  124.6 60.5 %copy-start = (bf16[512,768]{1,0:T(8,128)(2,1)S(1)}, bf16[512,768]{1,0:T(8,128)(2,1)}, u32[]{:S(2)}) copy-start(bf16[512,768]{1,0:T(8,128)(2,1)} %tokens.1) | copy-start | bytes 2359300
  124.6 60.7 %collective-permute-start = (bf16[2,512,768]{2,1,0:T(8,128)(2,1)}, bf16[2,512,768]{2,1,0:T(8,128)(2,1)S(1)}, u32[]{:S(2)}, u32[]{:S(2)}) collective-permute-start(bf16[2,512,768]{2,1,0:T(8,128)(2,1)} %get-tuple-element.38), channel_id=1, source_target_pairs={{0,1},{1,0},{2,3},{3,2},{4,5},{5,4},{6,7},{7,6},{8,9},{9,8},{10,11... | collective-permute-start | bytes 4718600 | tf_op jit(solution)/shard_map/ppermute | solution.py:624
  185.3 1.1 copy-start.2
  189.7 151.5 %collective-permute-start.1 = (bf16[512,768]{1,0:T(8,128)(2,1)}, bf16[512,768]{1,0:T(8,128)(2,1)}, u32[]{:S(2)}, u32[]{:S(2)}) collective-permute-start(bf16[512,768]{1,0:T(8,128)(2,1)} %slice_bitcast_fusion), channel_id=1, source_target_pairs={{0,2},{1,3},{2,0},{3,1},{4,6},{5,7},{6,4},{7,5},{8,10},{9,11},{10,... | collective-permute-start | bytes 2359304 | tf_op jit(solution)/shard_map/ppermute | solution.py:626
  292.4 2.9 copy-start.3
  295.4 1.6 copy-start.5
  297.0 1.3 copy-start.6
  299.2 1.8 copy-start.1
Sparse Core Ops, SparseCore 0:
  116.5 175.8 all-reduce.6
Sparse Core Ops, SparseCore 1:
  124.7 78.6 reduce-scatter.1
where the time goes:
time: 351 us; the launch traced here: 352 us
  waiting for transfers between devices  101 us (29%)
  Pallas kernels  97.6 us (28%)
  blocking collectives  95.4 us (27%)
  other arithmetic  18.3 us (5%)
  between operations  15.6 us (4%)
  matrix products  11.7 us (3%)
  local copies, waits for them, and re-layouts  9.63 us (3%)
    psum x1, waiting for transfers between devices, over_batch(): return lax.psum(grad.astype(BF16), 'batch').astype(F32)  101 us
    psum x1, blocking collectives, over_batch(): return lax.psum(grad.astype(BF16), 'batch').astype(F32)  56.2 us
    pallas_call x1, Pallas kernels, front(): pl.pallas_call(functools.partial(front_body, heads), out_shape=(like,) *...  47.4 us
    psum x1, blocking collectives, on_device(): lax.psum((ln_gain_part, rows_out[1]), ('batch', 'tensor'))  39.2 us
    pallas_call x1, Pallas kernels, attn_fwd(): pl.pallas_call(functools.partial(attn_fwd_body, heads), out_shape=(like,...  25.3 us
    pallas_call x1, Pallas kernels, attn_bwd(): pl.pallas_call(functools.partial(attn_bwd_body, heads), out_shape=(jax.Sh...  24.9 us
    convert_element_type x7, other arithmetic, over_batch(): return lax.psum(grad.astype(BF16), 'batch').astype(F32)  8.43 us
  transfers between devices with their start and end apart: 4, of which 1 were waited for; matrix products, arithmetic and copies ran while one was open for 7% of the time, Pallas kernels for 0%

commit v1 on v0

--- a/solution.py
+++ b/solution.py
@@ -80,7 +80,7 @@
 
 def attn_fwd_body(
     heads, len_ref, group_ref, qa, ka, va, do, attn_out, mlp_part_hbm, call_hbm,
-    qb, dob, give, keep, attn_grad, seg, acc, ho, mlp_part, call, out_pad, grad_acc, sems,
+    qb, dob, give, keep, attn_t, seg, acc, ho, mlp_part, call, out_pad, grad_acc, sems,
 ):
     strips, tok_dev = qa.shape[0], qa.shape[1]
     loads = [pltpu.make_async_copy(mlp_part_hbm, mlp_part, sems.at[0]), pltpu.make_async_copy(call_hbm, call, sems.at[1])]
@@ -177,8 +177,7 @@
         return 0
 
     lax.fori_loop(0, strips * per_strip, project, 0)
-    for h in range(heads):
-        attn_grad[h * DH : (h + 1) * DH, :] = grad_acc[h * LANES : h * LANES + DH, :].astype(BF16)
+    attn_t[...] = grad_acc[...].T.astype(BF16)
 
 
 def attn_fwd(image_len, image_group, qa, ka, va, do, attn_out, mlp_part, call):
@@ -189,7 +188,7 @@
     half = jax.ShapeDtypeStruct((strips // 2, tok_dev, features), BF16)
     return pl.pallas_call(
         functools.partial(attn_fwd_body, heads),
-        out_shape=(like, like, half, half, jax.ShapeDtypeStruct(attn_out.shape, BF16)),
+        out_shape=(like, like, half, half, jax.ShapeDtypeStruct((features, width), BF16)),
         in_specs=[SMEM, SMEM] + [VMEM] * 5 + [ANY] * 2,
         out_specs=(VMEM,) * 5,
         scratch_shapes=[
@@ -367,10 +366,11 @@
 def front_body(
     heads, tokens, cot, ln_gain, qkv_weight, gq, gk, attn_out, mlp_in, mlp_bias, mlp_out,
     qa_out, ka_out, va_out, do_out, uq_out, uk_out, mlp_part_out, dn_part_out, nall_out, call_out,
-    g_in_out, g_out_out, rows_out,
-    both, wide, narrow, qkv_pad, mlp_out_t, mlp_in_t, attn_out_t, g_in, g_out,
-    send_sem, recv_sem, save_sem,
+    *rest,
 ):
+    (rows_out, both, wide, narrow, qkv_pad, mlp_out_t, mlp_in_t, attn_out_t, g_in, g_out,
+     send_sem, recv_sem, save_sem) = rest[-13:]
+    grad_outs = rest[:-13]
     batch, me = lax.axis_index("batch"), lax.axis_index("tensor")
     sibling = me + 1 - 2 * (me % 2)
     across = (me + 2) % 4
@@ -527,8 +527,26 @@
 
     lax.fori_loop(0, 2 * CHUNKS, unit, 0)
 
-    g_in_out[...] = g_in[...].astype(BF16)
-    g_out_out[...] = g_out[...].astype(BF16)
+    n_lo = len(grad_outs)
+    n_hi, chunk_rows = grad_outs[0].shape[0], grad_outs[0].shape[1]
+    hi, lo = batch // n_lo, batch % n_lo
+    per_grad = features // chunk_rows
+    for o in range(n_hi * n_lo):
+        source = (g_in, g_out)[o // per_grad]
+        row = o % per_grad * chunk_rows
+        low = source[row : row + chunk_rows, :].astype(BF16)
+        at_hi = (o // n_lo - hi + n_hi) % n_hi
+        at_lo = (o % n_lo - lo + n_lo) % n_lo
+        for m in range(n_lo):
+
+            @pl.when(at_lo == m)
+            def _():
+                grad_outs[m][at_hi] = low
+
+    grown = g_in[...] * mlp_in[...].astype(F32)
+    grown_hi = grown.astype(BF16)
+    ones = jnp.ones((8, grown.shape[1]), BF16)
+    rows_out[2:3, :] = (nt(ones, grown_hi) + nt(ones, (grown - grown_hi.astype(F32)).astype(BF16)))[0:1]
 
     def finish(i, _):
         for copy in saves(i % CHUNKS, i // CHUNKS):
@@ -547,23 +565,22 @@
     lax.fori_loop(0, CHUNKS, sent, 0)
 
 
-def front(strips, tokens, cot, ln_gain, qkv_weight, gq, gk, attn_out, mlp_in, mlp_bias, mlp_out):
+def front(strips, n_batch, tokens, cot, ln_gain, qkv_weight, gq, gk, attn_out, mlp_in, mlp_bias, mlp_out):
     tok_dev, features = tokens.shape
     width = gq.shape[1]
     heads = width // LANES
     hidden = mlp_in.shape[1]
     blocks = (3 * heads + 1) // 2
+    n_hi, n_lo = levels(n_batch)
     like = jax.ShapeDtypeStruct((strips, tok_dev, width), BF16)
     rows = jax.ShapeDtypeStruct((strips, tok_dev, features), BF16)
     return pl.pallas_call(
         functools.partial(front_body, heads),
         out_shape=(like,) * 6 + (rows,) * 4 + (
-            jax.ShapeDtypeStruct((features, hidden), BF16),
-            jax.ShapeDtypeStruct((hidden, features), BF16),
-            jax.ShapeDtypeStruct((8, features), F32),
-        ),
+            jax.ShapeDtypeStruct((n_hi, 2 * features // n_batch, features), BF16),
+        ) * n_lo + (jax.ShapeDtypeStruct((8, features), F32),),
         in_specs=[VMEM] * 10,
-        out_specs=(ANY,) * 10 + (VMEM,) * 3,
+        out_specs=(ANY,) * 10 + (VMEM,) * (n_lo + 1),
         scratch_shapes=[
             pltpu.VMEM((2, strips, tok_dev, features), BF16),
             pltpu.VMEM((2, strips, tok_dev, features), BF16),
@@ -583,11 +600,334 @@
     )(tokens, cot, ln_gain, qkv_weight, gq, gk, attn_out, mlp_in, mlp_bias, mlp_out)
 
 
-def layer_norm(inputs, gain):
-    row_mean = jnp.mean(inputs, axis=-1, keepdims=True)
-    centred = inputs - row_mean
-    variance = jnp.mean(centred * centred, axis=-1, keepdims=True)
-    return centred * lax.rsqrt(variance + epsilon) * gain
+def back_body(
+    heads, n_hi, n_lo, d_qkv_hbm, nall_hbm, dn_part_hbm, qkv_weight, tokens, cot, ln_gain, attn_t, mlp_own, front_rows,
+    gain_rows, input_grad, mlp_all_out, joint_all_out, rows_out,
+    d_qkv, nall, dn_part, weight_t, acc, joint, joint_low, joint_got, joint_sum, joint_got_hi, joint_all, mlp_all,
+    near, core_give, core_got, x_give, x_got, vec, vec_lo, vec_hi, vec_pair,
+    load_sem, mlp_s, mlp_r, joint_s, joint_r, hi_s, hi_r, all_s, all_r, core_s, core_r, x_s, x_r, vec_s, vec_r, save_sem,
+):
+    batch, me = lax.axis_index("batch"), lax.axis_index("tensor")
+    hi, lo = batch // n_lo, batch % n_lo
+    sibling = me + 1 - 2 * (me % 2)
+    across = (me + 2) % 4
+    chip, core = me // 2, me % 2
+    tok_dev, features = tokens.shape
+    step = tok_dev // CHUNKS
+    chunk_rows, chunk_cols = joint.shape[2], joint.shape[3]
+    half_cols = chunk_cols
+
+    loads = [
+        pltpu.make_async_copy(a, b, load_sem.at[i])
+        for i, (a, b) in enumerate(((d_qkv_hbm, d_qkv), (nall_hbm, nall), (dn_part_hbm, dn_part)))
+    ]
+    for load in loads:
+        load.start()
+
+    def hi_peer(k):
+        return (hi + k + n_hi) % n_hi
+
+    def lo_peer(m):
+        return (lo + m + n_lo) % n_lo
+
+    def to_hi(k):
+        return (hi_peer(k) * n_lo + lo, me)
+
+    def to_lo(m):
+        return (hi * n_lo + lo_peer(m), me)
+
+    barrier = pltpu.get_barrier_semaphore()
+    peers = [to_hi(k) for k in range(1, n_hi)] + [to_lo(m) for m in range(1, n_lo)] + [(batch, sibling), (batch, across)]
+    for peer in peers:
+        pl.semaphore_signal(barrier, inc=1, device_id=peer, device_id_type=pl.DeviceIdType.MESH)
+    mlp_all[hi, lo] = mlp_own[...]
+    pl.semaphore_wait(barrier, len(peers))
+
+    def gather_hi(buf, sends, recvs, k, back=0):
+        part = buf.at[hi_peer(back), lo]
+        return remote(part, part, sends.at[0, k], recvs.at[0, k], to_hi(k))
+
+    def gather_lo(buf, sends, recvs, m, k, back=0):
+        part = buf.at[hi_peer(-k), lo_peer(back)]
+        return remote(part, part, sends.at[m, k], recvs.at[m, k], to_lo(m))
+
+    def gather_start(buf, sends, recvs):
+        for k in range(1, n_hi):
+            gather_hi(buf, sends, recvs, k).start()
+        for m in range(1, n_lo):
+            gather_lo(buf, sends, recvs, m, 0).start()
+
+    def gather_pass(buf, sends, recvs, k):
+        gather_hi(buf, sends, recvs, k, -k).wait_recv()
+        for m in range(1, n_lo):
+            gather_lo(buf, sends, recvs, m, k).start()
+
+    def gather_end(buf, sends, recvs):
+        for m in range(1, n_lo):
+            for k in range(n_hi):
+                gather_lo(buf, sends, recvs, m, k, -m).wait_recv()
+        for k in range(1, n_hi):
+            gather_hi(buf, sends, recvs, k).wait_send()
+        for m in range(1, n_lo):
+            for k in range(n_hi):
+                gather_lo(buf, sends, recvs, m, k).wait_send()
+
+    gather_start(mlp_all, mlp_s, mlp_r)
+
+    loads[0].wait()
+    loads[1].wait()
+    acc[...] = jnp.zeros_like(acc)
+
+    def add_strip(i, _):
+        acc[...] += tn(nall[i], d_qkv[i])
+        return 0
+
+    lax.fori_loop(0, nall.shape[0], add_strip, 0)
+    width = qkv_weight.shape[1]
+    whole = width // LANES * LANES
+    left = lax.broadcasted_iota(jnp.int32, (features, LANES), 1) < DH
+    joint_low[:, :whole] = acc[:, :whole].astype(BF16)
+    parts = [attn_t[:, h * LANES : (h + 1) * LANES].astype(F32) for h in range(heads)]
+    if width % LANES:
+        parts = [acc[:, whole : whole + LANES]] + parts
+    for b in range(len(parts) // 2):
+        block = jnp.where(left, parts[2 * b], pltpu.roll(parts[2 * b + 1], DH, 1))
+        joint_low[:, whole + b * LANES : whole + (b + 1) * LANES] = block.astype(BF16)
+    per_half = features // chunk_rows
+    for o in range(n_hi * n_lo):
+        row = o % per_half * chunk_rows
+        col = o // per_half * half_cols
+        joint[o // n_lo, o % n_lo] = joint_low[row : row + chunk_rows, col : col + half_cols]
+
+    def joint_move(m, k, back=0):
+        return remote(
+            joint.at[hi_peer(k), lo_peer(m)], joint_got.at[lo_peer(back), hi_peer(k)],
+            joint_s.at[m, k], joint_r.at[m, k], to_lo(m),
+        )
+
+    for k in list(range(1, n_hi)) + [0]:
+        for m in range(1, n_lo):
+            joint_move(m, k).start()
+
+    weight = qkv_weight[...].astype(F32)
+    grown = acc[:, :width] * weight
+    grown_hi = grown.astype(BF16)
+    ones = jnp.ones((8, width), BF16)
+    ln_row = (nt(ones, grown_hi) + nt(ones, (grown - grown_hi.astype(F32)).astype(BF16)))[0:1]
+    vec_lo[lo] = front_rows[...]
+    vec_lo[lo, 2:3, :] = (front_rows[2:3, :] + ln_row) / ln_gain[...].astype(F32)
+    vec_lo[lo, 3:5, 0 : heads * LANES] = gain_rows[0:2, :]
+
+    def vec_lo_move(m, back=0):
+        part = vec_lo.at[lo_peer(back)]
+        return remote(part, part, vec_s.at[m], vec_r.at[m], to_lo(m))
+
+    def vec_hi_move(k, back=0):
+        part = vec_hi.at[hi_peer(back)]
+        return remote(part, part, vec_s.at[n_lo + k], vec_r.at[n_lo + k], to_hi(k))
+
+    def vec_pair_move(i, to):
+        return remote(vec.at[i], vec_pair.at[i], vec_s.at[n_lo + n_hi + i], vec_r.at[n_lo + n_hi + i], (batch, to))
+
+    for m in range(1, n_lo):
+        vec_lo_move(m).start()
+
+    weight_t[...] = jnp.zeros_like(weight_t)
+    weight_t[:width, :] = qkv_weight[...].T
+    loads[2].wait()
+
+    def rows_of(c):
+        return pl.ds(pl.multiple_of(c * step, step), step)
+
+    def partial_rows(strip, c):
+        return nn(d_qkv[strip, rows_of(c)], weight_t[...]) + dn_part[strip, rows_of(c)].astype(F32)
+
+    def core_move(side, c):
+        return remote(
+            core_give.at[side, rows_of(c)], core_got.at[side, rows_of(c)], core_s.at[side, c], core_r.at[side, c], (batch, sibling)
+        )
+
+    def x_move(c):
+        return remote(x_give.at[rows_of(c)], x_got.at[rows_of(c)], x_s.at[c], x_r.at[c], (batch, across))
+
+    def give_far(c, _):
+        core_give[0, rows_of(c)] = partial_rows(across + sibling - me, c).astype(BF16)
+        core_move(0, c).start()
+        return 0
+
+    def send_far(c, _):
+        mine = partial_rows(across, c)
+        core_move(0, c).wait_recv()
+        x_give[rows_of(c)] = (mine + core_got[0, rows_of(c)].astype(F32)).astype(BF16)
+        x_move(c).start()
+        return 0
+
+    def give_near(c, _):
+        core_give[1, rows_of(c)] = partial_rows(sibling, c).astype(BF16)
+        core_move(1, c).start()
+        return 0
+
+    def keep_near(c, _):
+        mine = partial_rows(me, c)
+        core_move(1, c).wait_recv()
+        near[rows_of(c)] = mine + core_got[1, rows_of(c)].astype(F32)
+        return 0
+
+    for loop in (give_far, send_far, give_near, keep_near):
+        lax.fori_loop(0, CHUNKS, loop, 0)
+
+    for m in range(1, n_lo):
+        vec_lo_move(m, -m).wait_recv()
+    total = vec_lo[0]
+    for i in range(1, n_lo):
+        total = total + vec_lo[i]
+    vec_hi[hi] = total
+    for k in range(1, n_hi):
+        vec_hi_move(k).start()
+
+    def hi_move(k, back=0):
+        return remote(joint_sum.at[hi_peer(k)], joint_got_hi.at[hi_peer(back)], hi_s.at[k], hi_r.at[k], to_hi(k))
+
+    for k in list(range(1, n_hi)) + [0]:
+        for m in range(1, n_lo):
+            joint_move(m, k, -m).wait_recv()
+        where = hi_peer(k)
+        total = joint[where, lo].astype(F32)
+        for m in range(1, n_lo):
+            total = total + joint_got[lo_peer(m), where].astype(F32)
+        joint_sum[where] = total.astype(BF16)
+        if k:
+            hi_move(k).start()
+
+    for k in range(1, n_hi):
+        vec_hi_move(k, -k).wait_recv()
+    total = vec_hi[0]
+    for i in range(1, n_hi):
+        total = total + vec_hi[i]
+    vec[0] = total
+    vec_pair_move(0, sibling).start()
+
+    gain = ln_gain[...].astype(F32)
+
+    def last_rows(c, _):
+        x_move(c).wait_recv()
+        d_normed = near[rows_of(c)] + x_got[rows_of(c)].astype(F32)
+        x = tokens[rows_of(c)].astype(F32)
+        centred = x - jnp.mean(x, axis=-1, keepdims=True)
+        r = lax.rsqrt(jnp.mean(centred * centred, axis=-1, keepdims=True) + epsilon)
+        xhat = centred * r
+        e = d_normed * gain
+        d_x = r * (e - jnp.mean(e, axis=-1, keepdims=True) - xhat * jnp.mean(e * xhat, axis=-1, keepdims=True))
+        input_grad[rows_of(c)] = (cot[rows_of(c)].astype(F32) + d_x).astype(BF16)
+        return 0
+
+    for k in range(1, n_hi):
+        gather_pass(mlp_all, mlp_s, mlp_r, k)
+    lax.fori_loop(0, CHUNKS, last_rows, 0)
+
+    vec_pair_move(0, sibling).wait_recv()
+    vec[1] = vec[0] + vec_pair[0]
+    vec_pair_move(1, across).start()
+
+    total = joint_sum[hi].astype(F32)
+    for k in range(1, n_hi):
+        hi_move(k, -k).wait_recv()
+        total = total + joint_got_hi[hi_peer(-k)].astype(F32)
+    joint_all[hi, lo] = total.astype(BF16)
+    gather_start(joint_all, all_s, all_r)
+
+    vec_pair_move(1, across).wait_recv()
+    rows_out[...] = vec[0]
+    rows_out[1:3, :] = vec[1, 1:3, :] + vec_pair[1, 1:3, :]
+
+    for k in range(1, n_hi):
+        gather_pass(joint_all, all_s, all_r, k)
+    gather_end(mlp_all, mlp_s, mlp_r)
+    save_mlp = pltpu.make_async_copy(mlp_all, mlp_all_out, save_sem.at[0])
+    save_mlp.start()
+
+    for m in range(1, n_lo):
+        for k in range(n_hi):
+            joint_move(m, k).wait_send()
+        vec_lo_move(m).wait_send()
+    for k in range(1, n_hi):
+        hi_move(k).wait_send()
+        vec_hi_move(k).wait_send()
+    vec_pair_move(0, sibling).wait_send()
+    vec_pair_move(1, across).wait_send()
+
+    def sent(c, _):
+        core_move(0, c).wait_send()
+        core_move(1, c).wait_send()
+        x_move(c).wait_send()
+        return 0
+
+    lax.fori_loop(0, CHUNKS, sent, 0)
+    gather_end(joint_all, all_s, all_r)
+    save_joint = pltpu.make_async_copy(joint_all, joint_all_out, save_sem.at[1])
+    save_joint.start()
+    save_mlp.wait()
+    save_joint.wait()
+
+
+def levels(n_batch):
+    lo = 2 if n_batch <= 8 else 4
+    return n_batch // lo, lo
+
+
+def back(n_batch, d_qkv, nall, dn_part, qkv_weight, tokens, cot, ln_gain, attn_t, mlp_own, front_rows, gain_rows):
+    n_hi, n_lo = levels(n_batch)
+    strips, tok_dev, features = nall.shape
+    wide = d_qkv.shape[2]
+    heads = attn_t.shape[1] // LANES
+    chunk = (2 * features // n_batch, features // 2)
+    dma = pltpu.SemaphoreType.DMA
+    rows = pltpu.VMEM((8, features), F32)
+    return pl.pallas_call(
+        functools.partial(back_body, heads, n_hi, n_lo),
+        out_shape=(
+            jax.ShapeDtypeStruct(tokens.shape, BF16),
+            jax.ShapeDtypeStruct((n_hi, n_lo) + mlp_own.shape, BF16),
+            jax.ShapeDtypeStruct((n_hi, n_lo) + chunk, BF16),
+            jax.ShapeDtypeStruct((8, features), F32),
+        ),
+        in_specs=[ANY] * 3 + [VMEM] * 8,
+        out_specs=(VMEM, ANY, ANY, VMEM),
+        scratch_shapes=[
+            pltpu.VMEM(d_qkv.shape, BF16),
+            pltpu.VMEM(nall.shape, BF16),
+            pltpu.VMEM(dn_part.shape, BF16),
+            pltpu.VMEM((wide, features), BF16),
+            pltpu.VMEM((features, wide), F32),
+            pltpu.VMEM((n_hi, n_lo) + chunk, BF16),
+            pltpu.VMEM((features, features), BF16),
+            pltpu.VMEM((n_lo, n_hi) + chunk, BF16),
+            pltpu.VMEM((n_hi,) + chunk, BF16),
+            pltpu.VMEM((n_hi,) + chunk, BF16),
+            pltpu.VMEM((n_hi, n_lo) + chunk, BF16),
+            pltpu.VMEM((n_hi, n_lo) + mlp_own.shape, BF16),
+            pltpu.VMEM(tokens.shape, F32),
+            pltpu.VMEM((2,) + tokens.shape, BF16),
+            pltpu.VMEM((2,) + tokens.shape, BF16),
+            pltpu.VMEM(tokens.shape, BF16),
+            pltpu.VMEM(tokens.shape, BF16),
+            pltpu.VMEM((2, 8, features), F32),
+            pltpu.VMEM((n_lo, 8, features), F32),
+            pltpu.VMEM((n_hi, 8, features), F32),
+            pltpu.VMEM((2, 8, features), F32),
+            dma((3,)),
+            dma((n_lo, n_hi)), dma((n_lo, n_hi)),
+            dma((n_lo, n_hi)), dma((n_lo, n_hi)),
+            dma((n_hi,)), dma((n_hi,)),
+            dma((n_lo, n_hi)), dma((n_lo, n_hi)),
+            dma((2, CHUNKS)), dma((2, CHUNKS)),
+            dma((CHUNKS,)), dma((CHUNKS,)),
+            dma((n_lo + n_hi + 2,)), dma((n_lo + n_hi + 2,)),
+            dma((2,)),
+        ],
+        compiler_params=pltpu.CompilerParams(collective_id=1, has_side_effects=True, vmem_limit_bytes=60 << 20),
+        name="reduce_gradients",
+    )(d_qkv, nall, dn_part, qkv_weight, tokens, cot, ln_gain, attn_t, mlp_own, front_rows, gain_rows)
 
 
 SIBLINGS = [(0, 1), (1, 0), (2, 3), (3, 2)]
@@ -600,9 +940,9 @@
 ):
     tok_dev, features = tokens.shape
     strips = lax.axis_size("tensor")
-    cap = tok_dev * strips
+    n_batch = lax.axis_size("batch")
+    n_hi, n_lo = levels(n_batch)
     heads = q_gain.shape[0] // DH
-    head_width = heads * DH
     qkv_cols = qkv_weight.shape[1]
 
     def pad_gain(g, factor):
@@ -611,47 +951,61 @@
 
     scale = DH ** (-0.5)
     gq, gk = pad_gain(q_gain, scale), pad_gain(k_gain, 1.0)
-    (qa, ka, va, do, uq, uk, mlp_part, dn_part, nall, call, g_in, g_out, rows_out) = front(
-        strips, tokens, out_cotangent, ln_gain.reshape(1, -1), qkv_weight, gq * LOG2E, gk,
+    ln_row = ln_gain.reshape(1, -1)
+    (qa, ka, va, do, uq, uk, mlp_part, dn_part, nall, call, *mlp_grad, front_rows) = front(
+        strips, n_batch, tokens, out_cotangent, ln_row, qkv_weight, gq * LOG2E, gk,
         attn_out, mlp_in, mlp_bias.reshape(1, -1), mlp_out,
     )
 
-    def over_batch(grad):
-        return lax.psum(grad.astype(BF16), "batch").astype(F32)
-
-    mlp_in_grad, mlp_out_grad, mlp_bias_grad = over_batch(g_in), over_batch(g_out), over_batch(rows_out[0])
-    qb, dob, give, keep, attn_grad = attn_fwd(image_len, image_group, qa, ka, va, do, attn_out, mlp_part, call)
-    got = lax.ppermute(give, "tensor", SIBLINGS)
-    mine = (keep.astype(F32) + got.astype(F32)).astype(BF16)
-    got = lax.ppermute(mine[0], "tensor", ACROSS)
+    def along_lo(x, m):
+        pairs = [(h * n_lo + i, h * n_lo + (i + m) % n_lo) for h in range(n_hi) for i in range(n_lo)]
+        return lax.ppermute(x, "batch", pairs)
+
+    def along_hi(x, k):
+        pairs = [(h * n_lo + i, (h + k) % n_hi * n_lo + i) for h in range(n_hi) for i in range(n_lo)]
+        return lax.ppermute(x, "batch", pairs)
+
+    def add(first, others):
+        total = first.astype(F32)
+        for other in others:
+            total = total + other.astype(F32)
+        return total.astype(BF16)
+
+    lo_got = [along_lo(mlp_grad[m], m) for m in range(1, n_lo)]
+    qb, dob, give, keep, attn_t = attn_fwd(image_len, image_group, qa, ka, va, do, attn_out, mlp_part, call)
+    lo_sum = [add(mlp_grad[0][k], [got[k] for got in lo_got]) for k in range(n_hi)]
+    core_got = lax.ppermute(give, "tensor", SIBLINGS)
+    hi_got = [along_hi(lo_sum[k], k) for k in range(1, n_hi)]
+    mine = add(keep, [core_got])
+    x_got = lax.ppermute(mine[0], "tensor", ACROSS)
+    d_qkv, gain_rows = attn_bwd(image_len, image_group, qb, ka, va, dob, uq, uk, gq, gk)
     output = (
-        tokens.astype(F32) + mine[1].astype(F32) + got.astype(F32) + out_bias.astype(F32)
+        tokens.astype(F32) + mine[1].astype(F32) + x_got.astype(F32) + out_bias.astype(F32)
     ).astype(BF16)
-
-    d_qkv, gain_grad = attn_bwd(image_len, image_group, qb, ka, va, dob, uq, uk, gq, gk)
-    gain_grad = gain_grad.reshape(8, heads, LANES)[:, :, :DH].reshape(8, head_width)
-    d_qkv = d_qkv.reshape(cap, -1)[:, :qkv_cols]
-    qkv_grad = tn(nall.reshape(cap, features), d_qkv)
-    d_normed = lax.psum_scatter(
-        (nt(d_qkv, qkv_weight) + dn_part.reshape(cap, features).astype(F32)).astype(BF16),
-        "tensor", scatter_dimension=0, tiled=True,
+    mlp_own = add(lo_sum[0], hi_got)
+    input_grad, mlp_all, joint_all, rows = back(
+        n_batch, d_qkv, nall, dn_part, qkv_weight, tokens, out_cotangent, ln_row, attn_t, mlp_own, front_rows, gain_rows
     )
-    _, ln_pull = jax.vjp(layer_norm, tokens.astype(F32), ln_gain.astype(F32))
-    d_x, ln_gain_part = ln_pull(d_normed.astype(F32))
-    input_grad = (out_cotangent.astype(F32) + d_x).astype(BF16)
-    ln_gain_grad, out_bias_grad = lax.psum((ln_gain_part, rows_out[1]), ("batch", "tensor"))
+    mlp_all = mlp_all.reshape(-1, features).astype(F32)
+    joint = joint_all.reshape(2, features, features // 2).astype(F32)
+    hidden = mlp_in.shape[1]
+    left_cols = features // 2
+
+    def gain_grad(row):
+        return row[: heads * LANES].reshape(heads, LANES)[:, :DH].reshape(heads * DH)
+
     return (
         output,
         input_grad,
-        ln_gain_grad,
-        over_batch(qkv_grad),
-        over_batch(gain_grad[0]),
-        over_batch(gain_grad[1]),
-        over_batch(attn_grad),
-        mlp_in_grad,
-        mlp_bias_grad,
-        mlp_out_grad,
-        out_bias_grad,
+        rows[2],
+        jnp.concatenate([joint[0], joint[1][:, : qkv_cols - left_cols]], axis=1),
+        gain_grad(rows[3]),
+        gain_grad(rows[4]),
+        joint[1][:, qkv_cols - left_cols :].T,
+        mlp_all[:features],
+        rows[0],
+        mlp_all[features:],
+        rows[1],
     )
 
 

time: 351 us -> 242 us (0.69)
  blocking collectives: 95.4 us -> 0 us
  waiting for transfers between devices: 101 us -> 6.32 us
  Pallas kernels: 97.6 us -> 190 us
  starting transfers between devices: 2.2 us -> 19.8 us
  between operations: 15.6 us -> 0.78 us
  matrix products: 11.7 us -> 0 us
  other arithmetic: 18.3 us -> 7.01 us
  local copies, waits for them, and re-layouts: 9.63 us -> 18.8 us
    psum x1 -> x0, waiting for transfers between devices: 101 us -> none  [over_batch(): return lax.psum(grad.astype(BF16), 'batch').astype(F32)]
    psum x2 -> x0, blocking collectives: 95.4 us -> none  [the longest x1 56.2 us: over_batch(): return lax.psum(grad.astype(BF16), 'batch').astype(F32)]
    pallas_call x0 -> x1, Pallas kernels: none -> 92 us  [back(): pl.pallas_call(functools.partial(back_body, heads, n_hi, n_lo), out_shape...]
    ppermute x2 -> x6, starting transfers between devices: 2.12 us -> 19.8 us  [the longest x3 16.6 us: along_hi(): return lax.ppermute(x, 'batch', pairs)]
    dot_general x2 -> x0, matrix products: 11.7 us -> none  [the longest x1 7.01 us: nt(): lax.dot_general(left, right, (((1,), (1,)), ((), ())), preferred_element_...]
    convert_element_type x10 -> x4, other arithmetic: 14.1 us -> 3.89 us  [the longest x1 2.37 us: on_device(): output = (tokens.astype(F32) + mine[1].astype(F32) + x_got.astype(F32) +...]
    ppermute x2 -> x6, waiting for transfers between devices: 0.01 us -> 6.32 us  [the longest x1 4.98 us: on_device(): x_got = lax.ppermute(mine[0], 'tensor', ACROSS)]
    slice x3 -> x5, local copies, waits for them, and re-layouts: 1.53 us -> 7.7 us  [the longest x1 2.6 us: on_device(): mlp_all[features:]]
  transfers between devices with their start and end apart: 4 -> 6, of which waited for: 1 -> 2; matrix products, arithmetic and copies ran while one was open for 7% -> 7% of each run, Pallas kernels for 0% -> 59%
where the time goes in v1:
time: 242 us; the launch traced here: 243 us
  Pallas kernels  190 us (79%)
  starting transfers between devices  19.8 us (8%)
  local copies, waits for them, and re-layouts  18.8 us (8%)
  other arithmetic  7.01 us (3%)
  waiting for transfers between devices  6.32 us (3%)
    pallas_call x1, Pallas kernels, back(): pl.pallas_call(functools.partial(back_body, heads, n_hi, n_lo), out_shape...  92 us
    pallas_call x1, Pallas kernels, front(): pl.pallas_call(functools.partial(front_body, heads), out_shape=(like,) *...  47.8 us
    pallas_call x1, Pallas kernels, attn_fwd(): pl.pallas_call(functools.partial(attn_fwd_body, heads), out_shape=(like,...  25.4 us
    pallas_call x1, Pallas kernels, attn_bwd(): pl.pallas_call(functools.partial(attn_bwd_body, heads), out_shape=(jax.Sh...  24.8 us
    ppermute x3, starting transfers between devices, along_hi(): return lax.ppermute(x, 'batch', pairs)  16.6 us
    unnamed x26, local copies, waits for them, and re-layouts  5.9 us
    ppermute x1, waiting for transfers between devices, on_device(): x_got = lax.ppermute(mine[0], 'tensor', ACROSS)  4.98 us
  transfers between devices with their start and end apart: 6, of which 2 were waited for; matrix products, arithmetic and copies ran while one was open for 7% of the time, Pallas kernels for 59%

profile of v1, /device:TPU:0, one launch (start us, length us, event | category | flops | bytes accessed | tf_op | source)
XLA Modules:
  0.0 242.7 jit_solution(9619983991407262832)
XLA Ops:
  0.6 0.0 copy-start.8
  0.7 0.0 copy-start.9
  0.7 0.0 copy-start.6
  0.7 0.0 copy-start.7
  0.7 2.3 copy.24.qkv_weight
  2.9 0.0 copy-done.8
  2.9 0.1 mul.17
  3.0 0.6 broadcast_multiply_fusion
  3.6 0.0 copy-done.9
  3.6 0.1 reshape.104
  3.7 0.6 copy.36
  4.3 0.0 copy-done.6
  4.3 0.6 reshape.102.ln_gain
  4.9 0.0 copy-done.7
  4.9 0.6 reshape.107.mlp_bias
  5.5 47.8 %gather_and_project.1 = (bf16[4,512,384]{2,1,0:T(8,128)(2,1)}, bf16[4,512,384]{2,1,0:T(8,128)(2,1)}, bf16[4,512,384]{2,1,0:T(8,128)(2,1)}, bf16[4,512,384]{2,1,0...) custom-call(bf16[512,768]{1,0:T(8,128)(2,1)} %tokens.3, ...), custom_call_target="tpu_custom_call" | custom-call | tf_op jit(solution)/shard_map/gather_and_project/pallas_call | solution.py:577
  53.3 1.2 collective-permute-start.2
  54.5 0.0 copy-start.3
  54.5 25.4 %attention_forward.1 = (bf16[4,512,384]{2,1,0:T(8,128)(2,1)}, bf16[4,512,384]{2,1,0:T(8,128)(2,1)}, bf16[2,512,768]{2,1,0:T(8,128)(2,1)}, bf16[2,512,768]{2,1,0:T(8,128)(2,1)}, bf16[768,384]{1,0:T(8,128)(2,1)}) custom-call(s32[80]{0:T(128)} %len_ref.3, s32[80]{0:T(128)} %group_ref.3, bf16[4,512,384]{2,1,0:T(8,128)(2,1)} %get-tuple-element.35.qa, ...), custom_call_target="tpu_custom_call" | custom-call | flops 8000000000 | bytes 30000000 | tf_op jit(solution)/shard_map/attention_forward/pallas_call | solution.py:189
  80.0 0.9 collective-permute-start
  80.8 1.3 collective-permute-done.2
  82.2 0.0 copy-done.3
  82.2 0.2 fusion.7
  82.4 1.4 collective-permute-start.3
  83.8 12.3 %collective-permute-start.4 = (bf16[192,768]{1,0:T(8,128)(2,1)S(1)}, bf16[192,768]{1,0:T(8,128)(2,1)S(1)}, u32[]{:S(2)}, u32[]{:S(2)}) collective-permute-start(bf16[192,768]{1,0:T(8,128)(2,1)S(1)} %get-tuple-element.70), channel_id=1, source_target_pairs={{0,16},{4,20},{8,24},{12,28},{16,0},{20,4},{24,8},{28,12},{1,17},{... | collective-permute-start | bytes 884744 | tf_op jit(solution)/shard_map/ppermute | solution.py:966
  96.1 2.8 %collective-permute-start.5 = (bf16[192,768]{1,0:T(8,128)(2,1)S(1)}, bf16[192,768]{1,0:T(8,128)(2,1)S(1)}, u32[]{:S(2)}, u32[]{:S(2)}) collective-permute-start(bf16[192,768]{1,0:T(8,128)(2,1)S(1)} %get-tuple-element.69), channel_id=1, source_target_pairs={{0,24},{4,28},{8,0},{12,4},{16,8},{20,12},{24,16},{28,20},{1,25},{... | collective-permute-start | bytes 884744 | tf_op jit(solution)/shard_map/ppermute | solution.py:966
  99.0 0.0 copy-start.5
  99.0 24.8 %attention_backward.1 = (bf16[4,512,640]{2,1,0:T(8,128)(2,1)}, f32[8,384]{1,0:T(8,128)}) custom-call(s32[80]{0:T(128)} %len_ref.3, s32[80]{0:T(128)} %group_ref.3, bf16[4,512,384]{2,1,0:T(8,128)(2,1)} %get-tuple-element.43.qb, bf16[4,512,384]{2,1,0:T(8,128)(2,1)} %get-tuple-element.36.ka, bf16[4,512,384]{2,1,0:T(8,128)(2,1)} %get-tuple-element.37.va, ...), custom_call_target="tpu_custom_call" | custom-call | flops 16000000000 | bytes 30000000 | tf_op jit(solution)/shard_map/attention_backward/pallas_call | solution.py:335
  123.7 0.0 copy-done.5
  123.8 0.0 collective-permute-done.3
  123.8 0.0 collective-permute-done.4
  123.8 0.0 collective-permute-done.5
  123.8 0.9 fusion.5.mlp_own
  124.7 92.0 %reduce_gradients.1 = (bf16[512,768]{1,0:T(8,128)(2,1)}, bf16[4,2,192,768]{3,2,1,0:T(8,128)(2,1)}, bf16[4,2,192,384]{3,2,1,0:T(8,128)(2,1)}, f32[8,768]{1,0:T(8,128)}) custom-call(bf16[4,512,640]{2,1,0:T(8,128)(2,1)} %get-tuple-element.47.d_qkv_hbm, bf16[4,512,768]{2,1,0:T(8,128)(2,1)} %get-tuple-element.48.nall_hbm, ...), custom_call_target="tpu_custom_call" | custom-call | tf_op jit(solution)/shard_map/reduce_gradients/pallas_call | solution.py:886
  216.7 0.0 copy-start.2
  216.7 2.5 %fusion.12 = (f32[2,2,192,384]{3,2,1,0:T(8,128)}, f32[2,2,192,384]{3,2,1,0:T(8,128)S(1)}) fusion(bf16[4,2,192,384]{3,2,1,0:T(8,128)(2,1)} %get-tuple-element.57), kind=kLoop, calls=%fused_computation.33 | loop fusion | bytes 4718592 | tf_op jit(solution)/shard_map/slice | solution.py:1001
  219.3 0.0 collective-permute-done
  219.3 0.0 copy-done.2
  219.3 0.4 add_convert_fusion
  219.7 0.9 slice_bitcast_fusion
  220.6 1.1 collective-permute-start.1
  221.7 0.3 fusion.11
  222.0 1.1 copy.29
  223.0 1.6 copy.27
  224.7 1.1 copy.30
  225.8 0.8 slice_reduce_fusion.3
  226.6 0.6 reshape.109
  227.2 0.6 reshape.111
  227.8 1.5 slice_reduce_fusion
  229.3 0.0 copy-start
  229.3 2.5 %pad_maximum_fusion = f32[768,576]{0,1:T(8,128)} fusion(f32[768,192]{0,1:T(8,128)} %copy.29, f32[768,384]{0,1:T(8,128)S(1)} %copy.27), kind=kLoop, calls=%fused_computation.1 | loop fusion | flops 442368 | bytes 3538944 | tf_op jit(solution)/shard_map/concatenate | solution.py:1001
  231.9 0.0 copy-done
  231.9 0.0 copy-start.1
  231.9 2.6 %fusion.10 = (f32[2,2,192,768]{3,2,1,0:T(8,128)}, f32[2,2,192,768]{3,2,1,0:T(8,128)}) fusion(bf16[4,2,192,768]{3,2,1,0:T(8,128)(2,1)S(1)} %copy-done), kind=kLoop, calls=%fused_computation.31 | loop fusion | bytes 9437184 | tf_op jit(solution)/shard_map/slice | solution.py:1007
  234.5 0.0 copy-start.4
  234.5 5.0 %collective-permute-done.1 = bf16[512,768]{1,0:T(8,128)(2,1)} collective-permute-done((bf16[512,768]{1,0:T(8,128)(2,1)}, bf16[512,768]{1,0:T(8,128)(2,1)}, u32[]{:S(2)}, u32[]{:S(2)}) %collective-permute-start.1) | collective-permute-done | bytes 786464 | tf_op jit(solution)/shard_map/ppermute | solution.py:980
  239.5 0.0 copy-done.1
  239.5 2.4 fusion.2
  241.8 0.0 copy-done.4
  241.8 0.9 copy.38
  (4 shorter events, 0.0 us)
Async XLA Ops:
  0.6 2.3 copy-start.8
  0.7 3.0 %copy-start.9 = (bf16[192]{0:T(256)(128)(2,1)S(1)}, bf16[192]{0:T(256)(128)(2,1)}, u32[]{:S(2)}) copy-start(bf16[192]{0:T(256)(128)(2,1)} %param.18) | copy-start | bytes 1156
  0.7 3.6 %copy-start.6 = (bf16[768]{0:T(1024)(128)(2,1)S(1)}, bf16[768]{0:T(1024)(128)(2,1)}, u32[]{:S(2)}) copy-start(bf16[768]{0:T(1024)(128)(2,1)} %param.15) | copy-start | bytes 4612
  0.7 4.2 %copy-start.7 = (bf16[768]{0:T(1024)(128)(2,1)S(1)}, bf16[768]{0:T(1024)(128)(2,1)}, u32[]{:S(2)}) copy-start(bf16[768]{0:T(1024)(128)(2,1)} %param.21) | copy-start | bytes 4612
  53.3 28.9 %collective-permute-start.2 = (bf16[4,192,768]{2,1,0:T(8,128)(2,1)}, bf16[4,192,768]{2,1,0:T(8,128)(2,1)S(1)}, u32[]{:S(2)}, u32[]{:S(2)}) collective-permute-start(bf16[4,192,768]{2,1,0:T(8,128)(2,1)} %get-tuple-element.52), channel_id=1, source_target_pairs={{0,4},{4,0},{8,12},{12,8},{16,20},{20,16},{24,28},{28,24},{1,5},{5... | collective-permute-start | bytes 3538952 | tf_op jit(solution)/shard_map/ppermute | solution.py:962
  54.5 27.6 %copy-start.3 = (bf16[4,192,768]{2,1,0:T(8,128)(2,1)S(1)}, bf16[4,192,768]{2,1,0:T(8,128)(2,1)}, u32[]{:S(2)}) copy-start(bf16[4,192,768]{2,1,0:T(8,128)(2,1)} %get-tuple-element.51) | copy-start | bytes 3538948
  80.0 139.3 %collective-permute-start = (bf16[2,512,768]{2,1,0:T(8,128)(2,1)}, bf16[2,512,768]{2,1,0:T(8,128)(2,1)S(1)}, u32[]{:S(2)}, u32[]{:S(2)}) collective-permute-start(bf16[2,512,768]{2,1,0:T(8,128)(2,1)} %get-tuple-element.42), channel_id=1, source_target_pairs={{0,1},{1,0},{2,3},{3,2},{4,5},{5,4},{6,7},{7,6},{8,9},{9,8},{10,11... | collective-permute-start | bytes 4718600 | tf_op jit(solution)/shard_map/ppermute | solution.py:977
  82.4 41.4 %collective-permute-start.3 = (bf16[192,768]{1,0:T(8,128)(2,1)S(1)}, bf16[192,768]{1,0:T(8,128)(2,1)S(1)}, u32[]{:S(2)}, u32[]{:S(2)}) collective-permute-start(bf16[192,768]{1,0:T(8,128)(2,1)S(1)} %get-tuple-element.68), channel_id=1, source_target_pairs={{0,8},{4,12},{8,16},{12,20},{16,24},{20,28},{24,0},{28,4},{1,9},{5... | collective-permute-start | bytes 884744 | tf_op jit(solution)/shard_map/ppermute | solution.py:966
  83.8 40.0 %collective-permute-start.4 = (bf16[192,768]{1,0:T(8,128)(2,1)S(1)}, bf16[192,768]{1,0:T(8,128)(2,1)S(1)}, u32[]{:S(2)}, u32[]{:S(2)}) collective-permute-start(bf16[192,768]{1,0:T(8,128)(2,1)S(1)} %get-tuple-element.70), channel_id=1, source_target_pairs={{0,16},{4,20},{8,24},{12,28},{16,0},{20,4},{24,8},{28,12},{1,17},{... | collective-permute-start | bytes 884744 | tf_op jit(solution)/shard_map/ppermute | solution.py:966
  96.1 27.6 %collective-permute-start.5 = (bf16[192,768]{1,0:T(8,128)(2,1)S(1)}, bf16[192,768]{1,0:T(8,128)(2,1)S(1)}, u32[]{:S(2)}, u32[]{:S(2)}) collective-permute-start(bf16[192,768]{1,0:T(8,128)(2,1)S(1)} %get-tuple-element.69), channel_id=1, source_target_pairs={{0,24},{4,28},{8,0},{12,4},{16,8},{20,12},{24,16},{28,20},{1,25},{... | collective-permute-start | bytes 884744 | tf_op jit(solution)/shard_map/ppermute | solution.py:966
  99.0 24.8 %copy-start.5 = (bf16[768]{0:T(1024)(128)(2,1)S(1)}, bf16[768]{0:T(1024)(128)(2,1)}, u32[]{:S(2)}) copy-start(bf16[768]{0:T(1024)(128)(2,1)} %param.23) | copy-start | bytes 4612
  216.7 2.5 %copy-start.2 = (bf16[2,512,768]{2,1,0:T(8,128)(2,1)S(1)}, bf16[2,512,768]{2,1,0:T(8,128)(2,1)}, u32[]{:S(2)}) copy-start(bf16[2,512,768]{2,1,0:T(8,128)(2,1)} %get-tuple-element.41) | copy-start | bytes 4718596
  220.6 18.8 %collective-permute-start.1 = (bf16[512,768]{1,0:T(8,128)(2,1)}, bf16[512,768]{1,0:T(8,128)(2,1)}, u32[]{:S(2)}, u32[]{:S(2)}) collective-permute-start(bf16[512,768]{1,0:T(8,128)(2,1)} %slice_bitcast_fusion), channel_id=1, source_target_pairs={{0,2},{1,3},{2,0},{3,1},{4,6},{5,7},{6,4},{7,5},{8,10},{9,11},{10,... | collective-permute-start | bytes 2359304 | tf_op jit(solution)/shard_map/ppermute | solution.py:980
  229.3 2.5 %copy-start = (bf16[4,2,192,768]{3,2,1,0:T(8,128)(2,1)S(1)}, bf16[4,2,192,768]{3,2,1,0:T(8,128)(2,1)}, u32[]{:S(2)}) copy-start(bf16[4,2,192,768]{3,2,1,0:T(8,128)(2,1)} %get-tuple-element.58) | copy-start | bytes 7077892
  231.9 7.6 %copy-start.1 = (bf16[512,768]{1,0:T(8,128)(2,1)S(1)}, bf16[512,768]{1,0:T(8,128)(2,1)}, u32[]{:S(2)}) copy-start(bf16[512,768]{1,0:T(8,128)(2,1)} %tokens.3) | copy-start | bytes 2359300
  234.5 7.4 %copy-start.4 = (bf16[512,768]{1,0:T(8,128)(2,1)S(1)}, bf16[512,768]{1,0:T(8,128)(2,1)}, u32[]{:S(2)}) copy-start(bf16[512,768]{1,0:T(8,128)(2,1)} %get-tuple-element.87) | copy-start | bytes 2359300

commit v2 on v1

v2 whole, which is shorter than its diff:
```python
import functools

import jax
import jax.numpy as jnp
from jax import lax
from jax.experimental import pallas as pl
from jax.experimental.pallas import tpu as pltpu
from jax.sharding import PartitionSpec as P

DH = 64
LANES = 128
WIN = 64
ALIGN = 16
LOG2E = 1.4426950408889634
epsilon = 1e-06
F32 = jnp.float32
BF16 = jnp.bfloat16
VMEM = pl.BlockSpec(memory_space=pltpu.VMEM)
SMEM = pl.BlockSpec(memory_space=pltpu.SMEM)
ANY = pl.BlockSpec(memory_space=pl.ANY)


def nn(left, right):
    return lax.dot_general(left, right, (((1,), (0,)), ((), ())), preferred_element_type=F32)


def nt(left, right):
    return lax.dot_general(left, right, (((1,), (1,)), ((), ())), preferred_element_type=F32)


def tn(left, right):
    return lax.dot_general(left, right, (((0,), (0,)), ((), ())), preferred_element_type=F32)


def row_of(vector):
    return vector[...].astype(F32).reshape(1, -1)


def pair_row(q_vector, k_vector, heads):
    q, k = row_of(q_vector), row_of(k_vector)
    parts = []
    for h in range(heads):
        parts += [q[:, h * DH : (h + 1) * DH], k[:, h * DH : (h + 1) * DH]]
    return jnp.concatenate(parts, axis=1)


def half_sums():
    row = lax.broadcasted_iota(jnp.int32, (LANES, LANES), 0) // DH
    col = lax.broadcasted_iota(jnp.int32, (LANES, LANES), 1) // DH
    return jnp.where(row == col, 1.0, 0.0).astype(BF16)


def left_half(rows):
    return lax.broadcasted_iota(jnp.int32, (rows, LANES), 1) < DH


def find_segments(len_ref, group_ref, seg_ref, strips, tok_dev):
    group = lax.axis_index("batch")

    def entry(i, carry):
        count, run = carry
        rows = jnp.where(group_ref[i] == group, len_ref[i] // strips, 0)

        @pl.when(rows > 0)
        def _():
            seg_ref[0, count] = run
            seg_ref[1, count] = run + rows

        return count + jnp.where(rows > 0, 1, 0), run + rows

    count, run = lax.fori_loop(0, len_ref.shape[0], entry, (jnp.int32(0), jnp.int32(0)))

    @pl.when(run < tok_dev)
    def _():
        seg_ref[0, count] = run
        seg_ref[1, count] = tok_dev

    return count + jnp.where(run < tok_dev, 1, 0)


def window(start, end, first, i, tok_dev):
    nominal = first + WIN * i
    at = pl.multiple_of(jnp.minimum(nominal, tok_dev - WIN), ALIGN)
    return at, jnp.maximum(start, nominal) - at, jnp.minimum(end, nominal + WIN) - at


def row_mask(low, high, strips, win=WIN, width=LANES):
    j = lax.broadcasted_iota(jnp.int32, (strips, win, width), 1).reshape(strips * win, width)
    return (j >= low) & (j < high)


def tile(ref, at, h, win=WIN):
    strips = ref.shape[0]
    return ref[:, pl.ds(at, win), h * LANES : (h + 1) * LANES].reshape(strips * win, LANES)


def put_tile(ref, at, h, mask, value, win=WIN, width=LANES):
    strips = ref.shape[0]
    where = (slice(None), pl.ds(at, win), slice(h * LANES, h * LANES + width))
    old = ref[where].reshape(strips * win, width)
    ref[where] = jnp.where(mask, value.astype(ref.dtype), old).reshape(strips, win, width)


def for_segments(len_ref, group_ref, seg, strips, tok_dev, small, middle, large):
    count = find_segments(len_ref, group_ref, seg, strips, tok_dev)
    big = middle_rows(tok_dev)

    def segment(index, _):
        start, end = seg[0, index], seg[1, index]
        first = (start // ALIGN) * ALIGN
        windows = (end - first + WIN - 1) // WIN
        fits = end - first <= big

        @pl.when(windows == 1)
        def _():
            small(*window(start, end, first, 0, tok_dev))

        @pl.when((windows > 1) & fits)
        def _():
            at = pl.multiple_of(jnp.minimum(first, tok_dev - big), ALIGN)
            middle(at, start - at, end - at)

        @pl.when(jnp.logical_not(fits))
        def _():
            large(start, end, first, windows)

        return 0

    lax.fori_loop(0, count, segment, 0)


def middle_rows(tok_dev):
    return min(tok_dev, tok_dev // 2 + ALIGN)


def attn_fwd_body(
    heads, len_ref, group_ref, qa, ka, va, do, attn_out, mlp_part_hbm, call_hbm,
    qb, dob, give, keep, attn_grad, seg, acc, ho, mlp_part, call, out_pad, grad_acc, sems,
):
    strips, tok_dev = qa.shape[0], qa.shape[1]
    loads = [pltpu.make_async_copy(mlp_part_hbm, mlp_part, sems.at[0]), pltpu.make_async_copy(call_hbm, call, sems.at[1])]
    for load in loads:
        load.start()
    zero = jnp.zeros((), BF16)
    big = middle_rows(tok_dev)

    def finish(at, low, high, totals, win=WIN):
        rows = strips * win
        mask = row_mask(low, high, strips, win)
        lane = lax.broadcasted_iota(jnp.int32, (rows, LANES), 1)
        left = lane < DH
        outs = []
        for h in range(heads):
            total = totals[h]
            rows_sum = jnp.where(left, pltpu.roll(total, DH, 1), total)
            out = jnp.where(left, total / rows_sum, 0.0)
            log_sum = jnp.log2(rows_sum)
            d_out = tile(do, at, h, win).astype(F32)
            delta = jnp.sum(out * d_out, axis=-1, keepdims=True)
            log_hi = log_sum.astype(BF16).astype(F32)
            delta_hi = delta.astype(BF16).astype(F32)
            q = tile(qa, at, h, win).astype(F32)
            q = jnp.where(lane == DH, -log_hi, jnp.where(lane == DH + 1, log_hi - log_sum, q))
            d_out = jnp.where(lane == DH, -delta_hi, jnp.where(lane == DH + 1, delta_hi - delta, d_out))
            put_tile(qb, at, h, mask, q, win)
            put_tile(dob, at, h, mask, d_out, win)
            outs.append(out)
        if heads % 2:
            outs.append(jnp.zeros_like(outs[0]))
        for b in range(len(outs) // 2):
            put_tile(ho, at, b, mask, jnp.where(left, outs[2 * b], pltpu.roll(outs[2 * b + 1], DH, 1)), win)

    def products(at_q, at_k, k_mask, win_q=WIN, win_k=WIN):
        scores = [nt(tile(qa, at_q, h, win_q), tile(ka, at_k, h, win_k)) for h in range(heads)]
        weights = [jnp.exp2(s).astype(BF16) for s in scores]
        return [nn(weights[h], jnp.where(k_mask, tile(va, at_k, h, win_k), zero)) for h in range(heads)]

    def small(at, low, high):
        finish(at, low, high, products(at, at, row_mask(low, high, strips)))

    def middle(at, low, high):
        def add(at_k, k_mask, win, first=False):
            for h, new in enumerate(products(at, at_k, k_mask, big, win)):
                acc[h] = new if first else acc[h] + new

        rest = big % WIN
        base = at + big - rest
        if rest:
            add(base, row_mask(low - (big - rest), high - (big - rest), strips, rest), rest, True)
        else:
            acc[...] = jnp.zeros_like(acc)

        def k_window(k, _):
            add(pl.multiple_of(at + k * WIN, ALIGN), row_mask(low - k * WIN, high - k * WIN, strips), WIN)
            return 0

        lax.fori_loop(0, big // WIN, k_window, 0)

        def total(h, offset, win):
            return acc[h].reshape(strips, big, LANES)[:, offset : offset + win].reshape(strips * win, LANES)

        for w in range(big // WIN):
            offset = w * WIN
            finish(
                pl.multiple_of(at + offset, ALIGN), low - offset, high - offset, [total(h, offset, WIN) for h in range(heads)]
            )
        if rest:
            offset = big - rest
            finish(base, low - offset, high - offset, [total(h, offset, rest) for h in range(heads)], rest)

    def large(start, end, first, windows):
        def q_window(i, _):
            at_q, low_q, high_q = window(start, end, first, i, tok_dev)
            rows = strips * WIN
            acc[:, :rows] = jnp.zeros((heads, rows, LANES), F32)

            def k_window(k, _):
                at_k, low_k, high_k = window(start, end, first, k, tok_dev)
                for h, new in enumerate(products(at_q, at_k, row_mask(low_k, high_k, strips))):
                    acc[h, :rows] += new
                return 0

            lax.fori_loop(0, windows, k_window, 0)
            finish(at_q, low_q, high_q, [acc[h, :rows] for h in range(heads)])
            return 0

        lax.fori_loop(0, windows, q_window, 0)

    for_segments(len_ref, group_ref, seg, strips, tok_dev, small, middle, large)

    width = attn_out.shape[0]
    out_pad[:width] = attn_out[...]
    out_pad[width:] = jnp.zeros((out_pad.shape[0] - width, out_pad.shape[1]), BF16)
    for load in loads:
        load.wait()
    me = lax.axis_index("tensor")
    grad_acc[...] = jnp.zeros_like(grad_acc)

    def project(strip, _):
        heads_rows = ho[strip]
        out = (nn(heads_rows, out_pad[...]) + mlp_part[strip].astype(F32)).astype(BF16)
        own = jnp.where(strip // 2 == me // 2, 1, 0)

        @pl.when(strip % 2 == me % 2)
        def _():
            keep[own] = out

        @pl.when(strip % 2 != me % 2)
        def _():
            give[own] = out

        grad_acc[...] += tn(heads_rows, call[strip])
        return 0

    lax.fori_loop(0, strips, project, 0)
    attn_grad[...] = grad_acc[:width].astype(BF16)


def attn_fwd(image_len, image_group, qa, ka, va, do, attn_out, mlp_part, call):
    strips, tok_dev, width = qa.shape
    heads = width // LANES
    features = call.shape[2]
    packed = (heads + 1) // 2 * LANES
    like = jax.ShapeDtypeStruct(qa.shape, BF16)
    half = jax.ShapeDtypeStruct((strips // 2, tok_dev, features), BF16)
    return pl.pallas_call(
        functools.partial(attn_fwd_body, heads),
        out_shape=(like, like, half, half, jax.ShapeDtypeStruct(attn_out.shape, BF16)),
        in_specs=[SMEM, SMEM] + [VMEM] * 5 + [ANY] * 2,
        out_specs=(VMEM,) * 5,
        scratch_shapes=[
            pltpu.SMEM((2, image_len.shape[0] + 1), jnp.int32),
            pltpu.VMEM((heads, strips * middle_rows(tok_dev), LANES), F32),
            pltpu.VMEM((strips, tok_dev, packed), BF16),
            pltpu.VMEM(call.shape, BF16),
            pltpu.VMEM(call.shape, BF16),
            pltpu.VMEM((packed, features), BF16),
            pltpu.VMEM((packed, features), F32),
            pltpu.SemaphoreType.DMA((2,)),
        ],
        compiler_params=pltpu.CompilerParams(vmem_limit_bytes=60 << 20),
        cost_estimate=pl.CostEstimate(flops=8 * 10**9, bytes_accessed=30 * 10**6, transcendentals=8 * 10**6),
        name="attention_forward",
    )(image_len, image_group, qa, ka, va, do, attn_out, mlp_part, call)


def attn_bwd_body(
    heads, len_ref, group_ref, qb, ka, va, dob, u_hbm, r_hbm, q_gain, k_gain,
    d_qkv, gain_grad, seg, k_turned, dq_turned, dk_acc, dv_acc, dq, dk, dv, u_rows, r_rows, sems,
):
    strips, tok_dev = qb.shape[0], qb.shape[1]
    loads = [pltpu.make_async_copy(u_hbm, u_rows, sems.at[0]), pltpu.make_async_copy(r_hbm, r_rows, sems.at[1])]
    for load in loads:
        load.start()
    zero = jnp.zeros((), BF16)
    big = middle_rows(tok_dev)

    def products(at_q, at_k, q_mask, k_turned_of, win_q=WIN, win_k=WIN):
        every = range(heads)
        qs = [tile(qb, at_q, h, win_q) for h in every]
        d_outs = [jnp.where(q_mask, tile(dob, at_q, h, win_q), zero) for h in every]
        scores = [nt(tile(ka, at_k, h, win_k), qs[h]) for h in every]
        d_weights = [nt(tile(va, at_k, h, win_k), d_outs[h]) for h in every]
        weights = [jnp.exp2(s) for s in scores]
        d_scores = [(weights[h] * d_weights[h]).astype(BF16) for h in every]
        dv_new = [nn(weights[h].astype(BF16), d_outs[h]) for h in every]
        dk_new = [nn(d_scores[h], qs[h]) for h in every]
        dq_new = [nn(k_turned_of(h), d_scores[h]) for h in every]
        return dq_new, dk_new, dv_new

    def turned(h, at_k, mask, win=WIN):
        return jnp.where(mask, tile(ka, at_k, h, win), zero).T[:DH]

    def small(at, low, high):
        mask = row_mask(low, high, strips)
        half = row_mask(low, high, strips, width=DH)
        dq_t, dk_new, dv_new = products(at, at, mask, lambda h: turned(h, at, mask))
        for h in range(heads):
            put_tile(dq, at, h, half, dq_t[h].T, width=DH)
            put_tile(dk, at, h, mask, dk_new[h])
            put_tile(dv, at, h, mask, dv_new[h])

    def middle(at, low, high):
        mask = row_mask(low, high, strips, big)
        for h in range(heads):
            k_turned[h] = turned(h, at, mask, big)

        def q_window(at_q, low_q, high_q, win, first=False):
            mask_q = row_mask(low_q, high_q, strips, win)
            half = row_mask(low_q, high_q, strips, win, DH)
            dq_t, dk_new, dv_new = products(at_q, at, mask_q, lambda h: k_turned[h], win, big)
            for h in range(heads):
                put_tile(dq, at_q, h, half, dq_t[h].T, win, DH)
                dk_acc[h] = dk_new[h] if first else dk_acc[h] + dk_new[h]
                dv_acc[h] = dv_new[h] if first else dv_acc[h] + dv_new[h]

        rest = big % WIN
        offset = big - rest
        if rest:
            q_window(at + offset, low - offset, high - offset, rest, True)
        else:
            dk_acc[...] = jnp.zeros_like(dk_acc)
            dv_acc[...] = jnp.zeros_like(dv_acc)

        def each(i, _):
            q_window(pl.multiple_of(at + i * WIN, ALIGN), low - i * WIN, high - i * WIN, WIN)
            return 0

        lax.fori_loop(0, big // WIN, each, 0)
        for h in range(heads):
            put_tile(dk, at, h, mask, dk_acc[h], big)
            put_tile(dv, at, h, mask, dv_acc[h], big)

    def large(start, end, first, windows):
        rows = strips * WIN

        def clear(i, _):
            for h in range(heads):
                dq_turned[h, i] = jnp.zeros(dq_turned.shape[2:], F32)
            return 0

        lax.fori_loop(0, windows, clear, 0)

        def k_window(k, _):
            at_k, low_k, high_k = window(start, end, first, k, tok_dev)
            mask_k = row_mask(low_k, high_k, strips)
            for h in range(heads):
                k_turned[h, :, :rows] = turned(h, at_k, mask_k)
            dk_acc[:, :rows] = jnp.zeros((heads, rows, LANES), F32)
            dv_acc[:, :rows] = jnp.zeros((heads, rows, LANES), F32)

            def q_window(i, _):
                at_q, low_q, high_q = window(start, end, first, i, tok_dev)
                mask_q = row_mask(low_q, high_q, strips)
                dq_t, dk_new, dv_new = products(at_q, at_k, mask_q, lambda h: k_turned[h, :, :rows])
                for h in range(heads):
                    dq_turned[h, i] += dq_t[h]
                    dk_acc[h, :rows] += dk_new[h]
                    dv_acc[h, :rows] += dv_new[h]
                return 0

            lax.fori_loop(0, windows, q_window, 0)
            for h in range(heads):
                put_tile(dk, at_k, h, mask_k, dk_acc[h, :rows])
                put_tile(dv, at_k, h, mask_k, dv_acc[h, :rows])
            return 0

        lax.fori_loop(0, windows, k_window, 0)

        def q_out(i, _):
            at_q, low_q, high_q = window(start, end, first, i, tok_dev)
            half = row_mask(low_q, high_q, strips, width=DH)
            for h in range(heads):
                put_tile(dq, at_q, h, half, dq_turned[h, i].T, width=DH)
            return 0

        lax.fori_loop(0, windows, q_out, 0)

    for_segments(len_ref, group_ref, seg, strips, tok_dev, small, middle, large)

    rows = strips * WIN
    left = left_half(rows)
    sums = half_sums()
    gains = pair_row(q_gain, k_gain, heads)
    for load in loads:
        load.wait()

    def chunk(i, totals):
        at = pl.multiple_of(i * WIN, WIN)
        scaled, new_totals, us = [], [], []
        for h in range(heads):
            cols = slice(h * LANES, (h + 1) * LANES)
            d_q, d_k = tile(dq, at, h), tile(dk, at, h) * (1.0 / LOG2E)
            both = jnp.where(left, d_q * DH ** (-0.5), pltpu.roll(d_k, DH, 1))
            u = tile(u_rows, at, h).astype(F32)
            new_totals.append(totals[h] + jnp.sum(both * u, axis=0, keepdims=True))
            scaled.append(both * gains[:, cols])
            us.append(u)
        stacked = [s.astype(BF16) for s in scaled] + [(scaled[h] * us[h]).astype(BF16) for h in range(heads)]
        means = nn(jnp.concatenate(stacked, axis=0), sums) * (1.0 / DH)
        parts = []
        for h in range(heads):
            mean = means[h * rows : (h + 1) * rows]
            mean_u = means[(heads + h) * rows : (heads + h + 1) * rows]
            parts.append((scaled[h] - mean - us[h] * mean_u) * tile(r_rows, at, h).astype(F32))
        values = [tile(dv, at, h) for h in range(heads)]
        if heads % 2:
            values.append(jnp.zeros_like(values[0]))
        for b in range(len(values) // 2):
            parts.append(jnp.where(left, values[2 * b], pltpu.roll(values[2 * b + 1], DH, 1)))
        for b, part in enumerate(parts):
            d_qkv[:, pl.ds(at, WIN), b * LANES : (b + 1) * LANES] = part.astype(BF16).reshape(strips, WIN, LANES)
        return tuple(new_totals)

    totals = lax.fori_loop(0, tok_dev // WIN, chunk, tuple(jnp.zeros((1, LANES), F32) for _ in range(heads)))
    gain_grad[...] = jnp.zeros_like(gain_grad)
    for h in range(heads):
        gain_grad[0:1, h * LANES : (h + 1) * LANES] = totals[h]


def attn_bwd(image_len, image_group, qb, ka, va, dob, u, r, q_gain, k_gain):
    strips, tok_dev, width = qb.shape
    heads = width // LANES
    blocks = heads + (heads + 1) // 2
    rows = strips * WIN
    big = strips * middle_rows(tok_dev)
    windows = tok_dev // WIN + 1
    full = pltpu.VMEM((strips, tok_dev, width), F32)
    return pl.pallas_call(
        functools.partial(attn_bwd_body, heads),
        out_shape=(
            jax.ShapeDtypeStruct((strips, tok_dev, blocks * LANES), BF16),
            jax.ShapeDtypeStruct((8, width), F32),
        ),
        in_specs=[SMEM, SMEM] + [VMEM] * 4 + [ANY] * 2 + [VMEM] * 2,
        out_specs=(VMEM, VMEM),
        scratch_shapes=[
            pltpu.SMEM((2, image_len.shape[0] + 1), jnp.int32),
            pltpu.VMEM((heads, DH, big), BF16),
            pltpu.VMEM((heads, windows, DH, rows), F32),
            pltpu.VMEM((heads, big, LANES), F32),
            pltpu.VMEM((heads, big, LANES), F32),
            full, full, full,
            pltpu.VMEM(u.shape, BF16),
            pltpu.VMEM(r.shape, BF16),
            pltpu.SemaphoreType.DMA((2,)),
        ],
        compiler_params=pltpu.CompilerParams(vmem_limit_bytes=60 << 20),
        cost_estimate=pl.CostEstimate(flops=16 * 10**9, bytes_accessed=30 * 10**6, transcendentals=8 * 10**6),
        name="attention_backward",
    )(image_len, image_group, qb, ka, va, dob, u, r, q_gain, k_gain)


CHUNKS = 4


def by_kind(weight_t, heads, rows):
    parts = [weight_t[3 * h * DH : (3 * h + 2) * DH, :] for h in range(heads)]
    parts += [weight_t[(3 * h + 2) * DH : (3 * h + 3) * DH, :] for h in range(heads)]
    spare = rows - weight_t.shape[0]
    if spare:
        parts.append(jnp.zeros((spare, weight_t.shape[1]), BF16))
    return jnp.concatenate(parts, axis=0)


def remote(src, dst, send, recv, device):
    return pltpu.make_async_remote_copy(
        src_ref=src, dst_ref=dst, send_sem=send, recv_sem=recv, device_id=device, device_id_type=pl.DeviceIdType.MESH
    )


def front_body(
    heads, tokens, cot, ln_gain, qkv_weight_t, q_gain, k_gain, attn_out, mlp_in, mlp_bias, mlp_out,
    qa_out, ka_out, va_out, do_out, u_out, r_out, mlp_part_out, dn_part_out, nall_out, call_out,
    *rest,
):
    (rows_out, both, wide, narrow, qkv_pad, mlp_out_t, mlp_in_t, attn_out_t, g_in, g_out,
     send_sem, recv_sem, save_sem) = rest[-13:]
    grad_outs = rest[:-13]
    batch, me = lax.axis_index("batch"), lax.axis_index("tensor")
    sibling = me + 1 - 2 * (me % 2)
    across = (me + 2) % 4
    chip, far_chip = me // 2, 1 - me // 2
    tok_dev = tokens.shape[0]
    step = tok_dev // CHUNKS
    rows = 2 * step
    features = tokens.shape[1]
    heads_wide = heads * LANES

    def rows_of(c):
        return pl.ds(pl.multiple_of(c * step, step), step)

    def move(kind, route, c, strip, to):
        part = both.at[kind, strip, rows_of(c)]
        return remote(part, part, send_sem.at[kind, route, c], recv_sem.at[kind, route, c], (batch, to))

    barrier = pltpu.get_barrier_semaphore()
    for other in (sibling, across):
        pl.semaphore_signal(barrier, inc=1, device_id=(batch, other), device_id_type=pl.DeviceIdType.MESH)
    gain = row_of(ln_gain)
    gains = pair_row(q_gain, k_gain, heads)

    def norm_chunk(c):
        both[0, me, rows_of(c)] = cot[rows_of(c)]
        x = tokens[rows_of(c)].astype(F32)
        centred = x - jnp.mean(x, axis=-1, keepdims=True)
        variance = jnp.mean(centred * centred, axis=-1, keepdims=True)
        both[1, me, rows_of(c)] = (centred * lax.rsqrt(variance + epsilon) * gain).astype(BF16)

    norm_chunk(0)
    pl.semaphore_wait(barrier, 2)

    def first_sends(c, _):
        for kind in range(2):
            move(kind, 1, c, me, across).start()
            move(kind, 0, c, me, sibling).start()

        @pl.when(c + 1 < CHUNKS)
        def _():
            norm_chunk(c + 1)

        return 0

    lax.fori_loop(0, CHUNKS, first_sends, 0)

    g_in[...] = jnp.zeros_like(g_in)
    g_out[...] = jnp.zeros_like(g_out)
    rows_out[...] = jnp.zeros_like(rows_out)
    total = jnp.zeros((1, features), F32)
    for c in range(CHUNKS):
        total += jnp.sum(cot[c * step : (c + 1) * step].astype(F32), axis=0, keepdims=True)
    rows_out[1:2, :] = total
    qkv_pad[...] = by_kind(qkv_weight_t, heads, qkv_pad.shape[1]).T
    mlp_out_t[...] = mlp_out[...].T
    mlp_in_t[...] = mlp_in[...].T
    for h in range(heads):
        part = attn_out[h * DH : (h + 1) * DH, :]
        attn_out_t[:, h * LANES : (h + 1) * LANES] = jnp.concatenate([part, jnp.zeros_like(part)], axis=0).T

    left = left_half(rows)
    sums = half_sums()
    bias = row_of(mlp_bias)

    def saves(c, at_chip):
        strips = pl.ds(2 * at_chip, 2)
        where = rows_of(c)
        index = at_chip * CHUNKS + c
        pairs = [(narrow.at[a, strips, where], ref.at[strips, where]) for a, ref in enumerate(
            (qa_out, ka_out, va_out, do_out, u_out, r_out))]
        pairs += [(wide.at[a, strips, where], ref.at[strips, where]) for a, ref in enumerate(
            (mlp_part_out, dn_part_out))]
        pairs += [(both.at[1, strips, where], nall_out.at[strips, where]), (both.at[0, strips, where], call_out.at[strips, where])]
        return [pltpu.make_async_copy(a, b, save_sem.at[n, index]) for n, (a, b) in enumerate(pairs)]

    def unit(i, _):
        far = i >= CHUNKS
        c = i % CHUNKS
        at_chip = jnp.where(far, far_chip, chip)

        @pl.when(jnp.logical_not(far))
        def _():
            for kind in range(2):
                move(kind, 0, c, sibling, sibling).wait_recv()

        def pass_on(k):
            for kind in range(2):
                move(kind, 1, k, across, across).wait_recv()
                move(kind, 2, k, across, sibling).start()

        @pl.when(i == CHUNKS - 1)
        def _():
            pass_on(0)

        @pl.when(i == CHUNKS)
        def _():
            pass_on(1)

        @pl.when(i > CHUNKS + 1)
        def _():
            pass_on(c)

        @pl.when(far)
        def _():
            for kind in range(2):
                move(kind, 2, c, across + 1 - 2 * (across % 2), sibling).wait_recv()

        strips = pl.ds(2 * at_chip, 2)
        where = rows_of(c)
        n = both[1, strips, where].reshape(rows, features)
        d = both[0, strips, where].reshape(rows, features)

        def save(ref, a, h, value):
            ref[a, strips, where, h * LANES : (h + 1) * LANES] = value.astype(BF16).reshape(2, step, LANES)

        qkv = nn(n, qkv_pad[...])

        def block(b):
            return qkv[:, b * LANES : (b + 1) * LANES]

        def stacked_means(parts):
            stacked = jnp.concatenate([p.astype(BF16) for p in parts], axis=0)
            means = nn(stacked, sums) * (1.0 / DH)
            return [means[h * rows : (h + 1) * rows] for h in range(heads)]

        pairs = [block(h) for h in range(heads)]
        means = stacked_means(pairs)
        centred = [pairs[h] - means[h] for h in range(heads)]
        variances = stacked_means([x * x for x in centred])
        for h in range(heads):
            rstd = lax.rsqrt(variances[h] + epsilon)
            u = centred[h] * rstd
            scaled = u * gains[:, h * LANES : (h + 1) * LANES]
            save(narrow, 0, h, jnp.where(left, scaled * (DH ** (-0.5) * LOG2E), 0.0))
            save(narrow, 1, h, jnp.where(left, pltpu.roll(scaled, DH, 1), 1.0))
            value = block(heads + h // 2)
            save(narrow, 2, h, jnp.where(left, pltpu.roll(value, DH, 1) if h % 2 else value, 1.0))
            save(narrow, 4, h, u)
            save(narrow, 5, h, rstd)
        narrow[3, strips, where] = nn(d, attn_out_t[...]).astype(BF16).reshape(2, step, heads_wide)

        hidden = nn(n, mlp_in[...]) + bias
        cdf = 0.5 + 0.5 * lax.erf(hidden * 0.7071067811865476)
        act = (hidden * cdf).astype(BF16)
        slope = cdf + hidden * (0.3989422804014327 * jnp.exp(hidden * hidden * -0.5))
        wide[0, strips, where] = nn(act, mlp_out[...]).astype(BF16).reshape(2, step, features)
        d_hidden = nn(d, mlp_out_t[...]) * slope
        d_low = d_hidden.astype(BF16)
        rows_out[0:1, :] += jnp.sum(d_low.astype(F32), axis=0, keepdims=True)
        wide[1, strips, where] = nn(d_low, mlp_in_t[...]).astype(BF16).reshape(2, step, features)
        g_out[...] += tn(act, d)
        g_in[...] += tn(n, d_low)
        for copy in saves(c, at_chip):
            copy.start()
        return 0

    lax.fori_loop(0, 2 * CHUNKS, unit, 0)

    n_lo = len(grad_outs)
    n_hi, chunk_rows = grad_outs[0].shape[0], grad_outs[0].shape[1]
    hi, lo = batch // n_lo, batch % n_lo
    per_grad = features // chunk_rows
    for o in range(n_hi * n_lo):
        source = (g_in, g_out)[o // per_grad]
        row = o % per_grad * chunk_rows
        low = source[row : row + chunk_rows, :].astype(BF16)
        at_hi = (o // n_lo - hi + n_hi) % n_hi
        at_lo = (o % n_lo - lo + n_lo) % n_lo
        for m in range(n_lo):

            @pl.when(at_lo == m)
            def _():
                grad_outs[m][at_hi] = low

    grown = g_in[...] * mlp_in[...].astype(F32)
    grown_hi = grown.astype(BF16)
    ones = jnp.ones((8, grown.shape[1]), BF16)
    rows_out[2:3, :] = (nt(ones, grown_hi) + nt(ones, (grown - grown_hi.astype(F32)).astype(BF16)))[0:1]

    def finish(i, _):
        for copy in saves(i % CHUNKS, i // CHUNKS):
            copy.wait()
        return 0

    lax.fori_loop(0, 2 * CHUNKS, finish, 0)

    def sent(c, _):
        for kind in range(2):
            move(kind, 0, c, me, sibling).wait_send()
            move(kind, 1, c, me, across).wait_send()
            move(kind, 2, c, across, sibling).wait_send()
        return 0

    lax.fori_loop(0, CHUNKS, sent, 0)


def front(strips, n_batch, tokens, cot, ln_gain, qkv_weight_t, q_gain, k_gain, attn_out, mlp_in, mlp_bias, mlp_out):
    tok_dev, features = tokens.shape
    heads = q_gain.shape[0] // DH
    width = heads * LANES
    hidden = mlp_in.shape[1]
    blocks = heads + (heads + 1) // 2
    n_hi, n_lo = levels(n_batch)
    like = jax.ShapeDtypeStruct((strips, tok_dev, width), BF16)
    rows = jax.ShapeDtypeStruct((strips, tok_dev, features), BF16)
    return pl.pallas_call(
        functools.partial(front_body, heads),
        out_shape=(like,) * 6 + (rows,) * 4 + (
            jax.ShapeDtypeStruct((n_hi, 2 * features // n_batch, features), BF16),
        ) * n_lo + (jax.ShapeDtypeStruct((8, features), F32),),
        in_specs=[VMEM] * 10,
        out_specs=(ANY,) * 10 + (VMEM,) * (n_lo + 1),
        scratch_shapes=[
            pltpu.VMEM((2, strips, tok_dev, features), BF16),
            pltpu.VMEM((2, strips, tok_dev, features), BF16),
            pltpu.VMEM((6, strips, tok_dev, width), BF16),
            pltpu.VMEM((features, blocks * LANES), BF16),
            pltpu.VMEM((features, hidden), BF16),
            pltpu.VMEM((hidden, features), BF16),
            pltpu.VMEM((features, width), BF16),
            pltpu.VMEM((features, hidden), F32),
            pltpu.VMEM((hidden, features), F32),
            pltpu.SemaphoreType.DMA((2, 3, CHUNKS)),
            pltpu.SemaphoreType.DMA((2, 3, CHUNKS)),
            pltpu.SemaphoreType.DMA((10, 2 * CHUNKS)),
        ],
        compiler_params=pltpu.CompilerParams(collective_id=0, has_side_effects=True, vmem_limit_bytes=60 << 20),
        name="gather_and_project",
    )(tokens, cot, ln_gain, qkv_weight_t, q_gain, k_gain, attn_out, mlp_in, mlp_bias, mlp_out)


def back_body(
    heads, n_hi, n_lo, d_qkv_hbm, nall_hbm, dn_part_hbm, give, keep, qkv_weight_t, tokens, cot, ln_gain, out_bias, attn_grad,
    mlp_own, front_rows, gain_rows, output, input_grad, mlp_all_out, joint_all_out, rows_out,
    d_qkv, nall, dn_part, weight_t, acc, joint, joint_low, joint_got, joint_sum, joint_got_hi, joint_all, mlp_all,
    near, core_give, core_got, x_give, x_got, out_got, out_give, out_far, vec, vec_lo, vec_hi, vec_pair,
    load_sem, mlp_s, mlp_r, joint_s, joint_r, hi_s, hi_r, all_s, all_r, core_s, core_r, x_s, x_r, out_core_s, out_core_r, out_x_s, out_x_r, vec_s, vec_r, save_sem,
):
    batch, me = lax.axis_index("batch"), lax.axis_index("tensor")
    hi, lo = batch // n_lo, batch % n_lo
    sibling = me + 1 - 2 * (me % 2)
    across = (me + 2) % 4
    chip, core = me // 2, me % 2
    tok_dev, features = tokens.shape
    step = tok_dev // CHUNKS
    chunk_rows, chunk_cols = joint.shape[2], joint.shape[3]
    half_cols = chunk_cols

    loads = [
        pltpu.make_async_copy(a, b, load_sem.at[i])
        for i, (a, b) in enumerate(((d_qkv_hbm, d_qkv), (nall_hbm, nall), (dn_part_hbm, dn_part)))
    ]
    for load in loads:
        load.start()

    def hi_peer(k):
        return (hi + k + n_hi) % n_hi

    def lo_peer(m):
        return (lo + m + n_lo) % n_lo

    def to_hi(k):
        return (hi_peer(k) * n_lo + lo, me)

    def to_lo(m):
        return (hi * n_lo + lo_peer(m), me)

    barrier = pltpu.get_barrier_semaphore()
    peers = [to_hi(k) for k in range(1, n_hi)] + [to_lo(m) for m in range(1, n_lo)] + [(batch, sibling), (batch, across)]
    for peer in peers:
        pl.semaphore_signal(barrier, inc=1, device_id=peer, device_id_type=pl.DeviceIdType.MESH)
    mlp_all[hi, lo] = mlp_own[...]
    pl.semaphore_wait(barrier, len(peers))

    def gather_hi(buf, sends, recvs, k, back=0):
        part = buf.at[hi_peer(back), lo]
        return remote(part, part, sends.at[0, k], recvs.at[0, k], to_hi(k))

    def gather_lo(buf, sends, recvs, m, k, back=0):
        part = buf.at[hi_peer(-k), lo_peer(back)]
        return remote(part, part, sends.at[m, k], recvs.at[m, k], to_lo(m))

    def gather_start(buf, sends, recvs):
        for k in range(1, n_hi):
            gather_hi(buf, sends, recvs, k).start()
        for m in range(1, n_lo):
            gather_lo(buf, sends, recvs, m, 0).start()

    def gather_pass(buf, sends, recvs, k):
        gather_hi(buf, sends, recvs, k, -k).wait_recv()
        for m in range(1, n_lo):
            gather_lo(buf, sends, recvs, m, k).start()

    def gather_end(buf, sends, recvs):
        for m in range(1, n_lo):
            for k in range(n_hi):
                gather_lo(buf, sends, recvs, m, k, -m).wait_recv()
        for k in range(1, n_hi):
            gather_hi(buf, sends, recvs, k).wait_send()
        for m in range(1, n_lo):
            for k in range(n_hi):
                gather_lo(buf, sends, recvs, m, k).wait_send()

    def rows_of(c):
        return pl.ds(pl.multiple_of(c * step, step), step)

    def out_core(c):
        where = rows_of(c)
        return remote(give.at[:, where], out_got.at[:, where], out_core_s.at[c], out_core_r.at[c], (batch, sibling))

    def out_across(c):
        return remote(out_give.at[rows_of(c)], out_far.at[rows_of(c)], out_x_s.at[c], out_x_r.at[c], (batch, across))

    def out_start(c, _):
        out_core(c).start()
        return 0

    def out_send(c, _):
        out_core(c).wait_recv()
        where = rows_of(c)
        out_give[where] = (keep[0, where].astype(F32) + out_got[0, where].astype(F32)).astype(BF16)
        out_across(c).start()
        return 0

    def out_rows(c, _):
        out_across(c).wait_recv()
        where = rows_of(c)
        total = keep[1, where].astype(F32) + out_got[1, where].astype(F32) + out_far[where].astype(F32)
        output[where] = (tokens[where].astype(F32) + total + bias).astype(BF16)
        return 0

    bias = row_of(out_bias)
    lax.fori_loop(0, CHUNKS, out_start, 0)
    gather_start(mlp_all, mlp_s, mlp_r)
    lax.fori_loop(0, CHUNKS, out_send, 0)

    weight_t[...] = by_kind(qkv_weight_t, heads, weight_t.shape[0])

    loads[0].wait()
    loads[1].wait()
    acc[...] = jnp.zeros_like(acc)

    def add_strip(i, _):
        acc[...] += tn(d_qkv[i], nall[i])
        return 0

    lax.fori_loop(0, nall.shape[0], add_strip, 0)
    width = qkv_weight_t.shape[0]
    joint_low[:width] = acc[:width].astype(BF16)
    joint_low[width:] = attn_grad[...]
    per_half = features // chunk_rows
    for o in range(n_hi * n_lo):
        row = o % per_half * chunk_rows
        col = o // per_half * half_cols
        joint[o // n_lo, o % n_lo] = joint_low[row : row + chunk_rows, col : col + half_cols]

    def joint_move(m, k, back=0):
        return remote(
            joint.at[hi_peer(k), lo_peer(m)], joint_got.at[lo_peer(back), hi_peer(k)],
            joint_s.at[m, k], joint_r.at[m, k], to_lo(m),
        )

    for k in list(range(1, n_hi)) + [0]:
        for m in range(1, n_lo):
            joint_move(m, k).start()

    ln_row = jnp.sum(acc[...] * weight_t[...].astype(F32), axis=0, keepdims=True)
    gain = row_of(ln_gain)
    vec_lo[lo] = front_rows[...]
    vec_lo[lo, 2:3, :] = (front_rows[2:3, :] + ln_row) / gain
    vec_lo[lo, 3:4, 0 : heads * LANES] = gain_rows[0:1, :]

    def vec_lo_move(m, back=0):
        part = vec_lo.at[lo_peer(back)]
        return remote(part, part, vec_s.at[m], vec_r.at[m], to_lo(m))

    def vec_hi_move(k, back=0):
        part = vec_hi.at[hi_peer(back)]
        return remote(part, part, vec_s.at[n_lo + k], vec_r.at[n_lo + k], to_hi(k))

    def vec_pair_move(i, to):
        return remote(vec.at[i], vec_pair.at[i], vec_s.at[n_lo + n_hi + i], vec_r.at[n_lo + n_hi + i], (batch, to))

    for m in range(1, n_lo):
        vec_lo_move(m).start()

    loads[2].wait()

    def partial_rows(strip, c):
        return nn(d_qkv[strip, rows_of(c)], weight_t[...]) + dn_part[strip, rows_of(c)].astype(F32)

    def core_move(side, c):
        return remote(
            core_give.at[side, rows_of(c)], core_got.at[side, rows_of(c)], core_s.at[side, c], core_r.at[side, c], (batch, sibling)
        )

    def x_move(c):
        return remote(x_give.at[rows_of(c)], x_got.at[rows_of(c)], x_s.at[c], x_r.at[c], (batch, across))

    def give_far(c, _):
        core_give[0, rows_of(c)] = partial_rows(across + sibling - me, c).astype(BF16)
        core_move(0, c).start()
        return 0

    def send_far(c, _):
        mine = partial_rows(across, c)
        core_move(0, c).wait_recv()
        x_give[rows_of(c)] = (mine + core_got[0, rows_of(c)].astype(F32)).astype(BF16)
        x_move(c).start()
        return 0

    def give_near(c, _):
        core_give[1, rows_of(c)] = partial_rows(sibling, c).astype(BF16)
        core_move(1, c).start()
        return 0

    def keep_near(c, _):
        mine = partial_rows(me, c)
        core_move(1, c).wait_recv()
        near[rows_of(c)] = mine + core_got[1, rows_of(c)].astype(F32)
        return 0

    for loop in (give_far, send_far, give_near, keep_near):
        lax.fori_loop(0, CHUNKS, loop, 0)

    for m in range(1, n_lo):
        vec_lo_move(m, -m).wait_recv()
    total = vec_lo[0]
    for i in range(1, n_lo):
        total = total + vec_lo[i]
    vec_hi[hi] = total
    for k in range(1, n_hi):
        vec_hi_move(k).start()

    def hi_move(k, back=0):
        return remote(joint_sum.at[hi_peer(k)], joint_got_hi.at[hi_peer(back)], hi_s.at[k], hi_r.at[k], to_hi(k))

    for k in list(range(1, n_hi)) + [0]:
        for m in range(1, n_lo):
            joint_move(m, k, -m).wait_recv()
        where = hi_peer(k)
        total = joint[where, lo].astype(F32)
        for m in range(1, n_lo):
            total = total + joint_got[lo_peer(m), where].astype(F32)
        joint_sum[where] = total.astype(BF16)
        if k:
            hi_move(k).start()

    for k in range(1, n_hi):
        vec_hi_move(k, -k).wait_recv()
    total = vec_hi[0]
    for i in range(1, n_hi):
        total = total + vec_hi[i]
    vec[0] = total
    vec_pair_move(0, sibling).start()

    def last_rows(c, _):
        x_move(c).wait_recv()
        d_normed = near[rows_of(c)] + x_got[rows_of(c)].astype(F32)
        x = tokens[rows_of(c)].astype(F32)
        centred = x - jnp.mean(x, axis=-1, keepdims=True)
        r = lax.rsqrt(jnp.mean(centred * centred, axis=-1, keepdims=True) + epsilon)
        xhat = centred * r
        e = d_normed * gain
        d_x = r * (e - jnp.mean(e, axis=-1, keepdims=True) - xhat * jnp.mean(e * xhat, axis=-1, keepdims=True))
        input_grad[rows_of(c)] = (cot[rows_of(c)].astype(F32) + d_x).astype(BF16)
        return 0

    for k in range(1, n_hi):
        gather_pass(mlp_all, mlp_s, mlp_r, k)
    lax.fori_loop(0, CHUNKS, out_rows, 0)
    lax.fori_loop(0, CHUNKS, last_rows, 0)

    vec_pair_move(0, sibling).wait_recv()
    vec[1] = vec[0] + vec_pair[0]
    vec_pair_move(1, across).start()

    total = joint_sum[hi].astype(F32)
    for k in range(1, n_hi):
        hi_move(k, -k).wait_recv()
        total = total + joint_got_hi[hi_peer(-k)].astype(F32)
    joint_all[hi, lo] = total.astype(BF16)
    gather_start(joint_all, all_s, all_r)

    vec_pair_move(1, across).wait_recv()
    rows_out[...] = vec[0]
    rows_out[1:3, :] = vec[1, 1:3, :] + vec_pair[1, 1:3, :]

    for k in range(1, n_hi):
        gather_pass(joint_all, all_s, all_r, k)
    gather_end(mlp_all, mlp_s, mlp_r)
    save_mlp = pltpu.make_async_copy(mlp_all, mlp_all_out, save_sem.at[0])
    save_mlp.start()

    for m in range(1, n_lo):
        for k in range(n_hi):
            joint_move(m, k).wait_send()
        vec_lo_move(m).wait_send()
    for k in range(1, n_hi):
        hi_move(k).wait_send()
        vec_hi_move(k).wait_send()
    vec_pair_move(0, sibling).wait_send()
    vec_pair_move(1, across).wait_send()

    def sent(c, _):
        core_move(0, c).wait_send()
        core_move(1, c).wait_send()
        x_move(c).wait_send()
        out_core(c).wait_send()
        out_across(c).wait_send()
        return 0

    lax.fori_loop(0, CHUNKS, sent, 0)
    gather_end(joint_all, all_s, all_r)
    save_joint = pltpu.make_async_copy(joint_all, joint_all_out, save_sem.at[1])
    save_joint.start()
    save_mlp.wait()
    save_joint.wait()


def levels(n_batch):
    lo = 2 if n_batch <= 8 else 4
    return n_batch // lo, lo


def back(n_batch, d_qkv, nall, dn_part, give, keep, qkv_weight_t, tokens, cot, ln_gain, out_bias, attn_grad,
    mlp_own, front_rows, gain_rows):
    n_hi, n_lo = levels(n_batch)
    strips, tok_dev, features = nall.shape
    wide = d_qkv.shape[2]
    heads = attn_grad.shape[0] // DH
    chunk = (2 * features // n_batch, features // 2)
    dma = pltpu.SemaphoreType.DMA
    rows = pltpu.VMEM((8, features), F32)
    return pl.pallas_call(
        functools.partial(back_body, heads, n_hi, n_lo),
        out_shape=(
            jax.ShapeDtypeStruct(tokens.shape, BF16),
            jax.ShapeDtypeStruct(tokens.shape, BF16),
            jax.ShapeDtypeStruct((n_hi, n_lo) + mlp_own.shape, BF16),
            jax.ShapeDtypeStruct((n_hi, n_lo) + chunk, BF16),
            jax.ShapeDtypeStruct((8, features), F32),
        ),
        in_specs=[ANY] * 3 + [VMEM] * 11,
        out_specs=(VMEM, VMEM, ANY, ANY, VMEM),
        scratch_shapes=[
            pltpu.VMEM(d_qkv.shape, BF16),
            pltpu.VMEM(nall.shape, BF16),
            pltpu.VMEM(dn_part.shape, BF16),
            pltpu.VMEM((wide, features), BF16),
            pltpu.VMEM((wide, features), F32),
            pltpu.VMEM((n_hi, n_lo) + chunk, BF16),
            pltpu.VMEM((features, features), BF16),
            pltpu.VMEM((n_lo, n_hi) + chunk, BF16),
            pltpu.VMEM((n_hi,) + chunk, BF16),
            pltpu.VMEM((n_hi,) + chunk, BF16),
            pltpu.VMEM((n_hi, n_lo) + chunk, BF16),
            pltpu.VMEM((n_hi, n_lo) + mlp_own.shape, BF16),
            pltpu.VMEM(tokens.shape, F32),
            pltpu.VMEM((2,) + tokens.shape, BF16),
            pltpu.VMEM((2,) + tokens.shape, BF16),
            pltpu.VMEM(tokens.shape, BF16),
            pltpu.VMEM(tokens.shape, BF16),
            pltpu.VMEM((2,) + tokens.shape, BF16),
            pltpu.VMEM(tokens.shape, BF16),
            pltpu.VMEM(tokens.shape, BF16),
            pltpu.VMEM((2, 8, features), F32),
            pltpu.VMEM((n_lo, 8, features), F32),
            pltpu.VMEM((n_hi, 8, features), F32),
            pltpu.VMEM((2, 8, features), F32),
            dma((3,)),
            dma((n_lo, n_hi)), dma((n_lo, n_hi)),
            dma((n_lo, n_hi)), dma((n_lo, n_hi)),
            dma((n_hi,)), dma((n_hi,)),
            dma((n_lo, n_hi)), dma((n_lo, n_hi)),
            dma((2, CHUNKS)), dma((2, CHUNKS)),
            dma((CHUNKS,)), dma((CHUNKS,)),
            dma((CHUNKS,)), dma((CHUNKS,)),
            dma((CHUNKS,)), dma((CHUNKS,)),
            dma((n_lo + n_hi + 2,)), dma((n_lo + n_hi + 2,)),
            dma((2,)),
        ],
        compiler_params=pltpu.CompilerParams(collective_id=1, has_side_effects=True, vmem_limit_bytes=60 << 20),
        name="reduce_gradients",
    )(d_qkv, nall, dn_part, give, keep, qkv_weight_t, tokens, cot, ln_gain, out_bias, attn_grad,
    mlp_own, front_rows, gain_rows)


def widen_body(heads, mlp_all, joint_all, rows, qkv_t, attn, mlp_in, mlp_out, ln_gain, q_gain, k_gain, mlp_bias, out_bias):
    features = rows.shape[1]
    chunks = mlp_all.shape[0]
    chunk_rows = mlp_all.shape[1]
    per_grad = features // chunk_rows
    width = qkv_t.shape[0]
    cols = joint_all.shape[2]
    for o in range(chunks):
        low = o % per_grad * chunk_rows
        (mlp_in, mlp_out)[o // per_grad][low : low + chunk_rows, :] = mlp_all[o].astype(F32)
    for half in range(2):
        at = slice(half * cols, (half + 1) * cols)
        kinds = [(3 * h + i) * DH for h in range(heads) for i in range(2)] + [(3 * h + 2) * DH for h in range(heads)]
        for i, to in enumerate(kinds):
            qkv_t[to : to + DH, at] = joint_all[half, i * DH : (i + 1) * DH].astype(F32)
        attn[:, at] = joint_all[half, width:].astype(F32)
    mlp_bias[...] = rows[0:1, :].reshape(features)
    out_bias[...] = rows[1:2, :].reshape(features)
    ln_gain[...] = rows[2:3, :].reshape(features)
    for offset, ref in ((0, q_gain), (DH, k_gain)):
        parts = [rows[3:4, h * LANES + offset : h * LANES + offset + DH] for h in range(heads)]
        ref[...] = jnp.concatenate(parts, axis=1).reshape(heads * DH)


def widen(heads, width, mlp_all, joint_all, rows):
    features = rows.shape[1]
    head_width = heads * DH

    def out(*shape):
        return jax.ShapeDtypeStruct(shape, F32)

    return pl.pallas_call(
        functools.partial(widen_body, heads),
        out_shape=(
            out(width, features), out(head_width, features), out(features, features), out(features, features),
            out(features), out(head_width), out(head_width), out(features), out(features),
        ),
        in_specs=[VMEM] * 3,
        out_specs=(VMEM,) * 9,
        compiler_params=pltpu.CompilerParams(vmem_limit_bytes=40 << 20),
        name="widen_gradients",
    )(mlp_all, joint_all, rows)


def on_device(
    tokens, out_cotangent, ln_gain, qkv_weight, q_gain, k_gain, attn_out,
    mlp_in, mlp_bias, mlp_out, out_bias, image_len, image_group,
):
    tok_dev, features = tokens.shape
    strips = lax.axis_size("tensor")
    n_batch = lax.axis_size("batch")
    n_hi, n_lo = levels(n_batch)
    heads = q_gain.shape[0] // DH
    qkv_cols = qkv_weight.shape[1]

    weight_t = qkv_weight.T
    (qa, ka, va, do, u, r, mlp_part, dn_part, nall, call, *mlp_grad, front_rows) = front(
        strips, n_batch, tokens, out_cotangent, ln_gain, weight_t, q_gain, k_gain, attn_out, mlp_in, mlp_bias, mlp_out
    )

    def along_lo(x, m):
        pairs = [(h * n_lo + i, h * n_lo + (i + m) % n_lo) for h in range(n_hi) for i in range(n_lo)]
        return lax.ppermute(x, "batch", pairs)

    def along_hi(x, k):
        pairs = [(h * n_lo + i, (h + k) % n_hi * n_lo + i) for h in range(n_hi) for i in range(n_lo)]
        return lax.ppermute(x, "batch", pairs)

    def add(first, others):
        total = first.astype(F32)
        for other in others:
            total = total + other.astype(F32)
        return total.astype(BF16)

    lo_got = [along_lo(mlp_grad[m], m) for m in range(1, n_lo)]
    qb, dob, give, keep, attn_grad = attn_fwd(image_len, image_group, qa, ka, va, do, attn_out, mlp_part, call)
    lo_sum = [add(mlp_grad[0][k], [got[k] for got in lo_got]) for k in range(n_hi)]
    hi_got = [along_hi(lo_sum[k], k) for k in range(1, n_hi)]
    d_qkv, gain_rows = attn_bwd(image_len, image_group, qb, ka, va, dob, u, r, q_gain, k_gain)
    mlp_own = add(lo_sum[0], hi_got)
    output, input_grad, mlp_all, joint_all, rows = back(
        n_batch, d_qkv, nall, dn_part, give, keep, weight_t, tokens, out_cotangent, ln_gain, out_bias, attn_grad,
        mlp_own, front_rows, gain_rows,
    )
    qkv_t, attn, mlp_in_grad, mlp_out_grad, ln, q, k, bias, out_bias_grad = widen(
        heads, qkv_cols, mlp_all.reshape((n_batch,) + mlp_all.shape[2:]), joint_all.reshape(2, features, -1), rows
    )
    return output, input_grad, ln, qkv_t.T, q, k, attn, mlp_in_grad, bias, mlp_out_grad, out_bias_grad


def solution(mesh):
    rows, cols, first = P(("batch", "tensor"), None), P(None, "tensor"), P("tensor", None)
    return jax.shard_map(
        on_device,
        mesh=mesh,
        in_specs=(rows, rows, P(), cols, P("tensor"), P("tensor"), first, cols, P("tensor"), first, P(), P(), P()),
        out_specs=(rows, rows, P(), cols, P("tensor"), P("tensor"), first, cols, P("tensor"), first, P()),
        check_vma=False,
    )
```

time: 242 us -> 192 us (0.79)
  Pallas kernels: 190 us -> 172 us
  starting transfers between devices: 19.8 us -> 6.6 us
  local copies, waits for them, and re-layouts: 18.8 us -> 5.96 us
  other arithmetic: 7.01 us -> 1.1 us
    ppermute x3, starting transfers between devices: 16.6 us -> 5.36 us  [along_hi(): return lax.ppermute(x, 'batch', pairs)]
    pallas_call x1, Pallas kernels: 92 us -> 81 us  [back(): pl.pallas_call(functools.partial(back_body, heads, n_hi, n_lo), out_shape...]
    pallas_call x1, Pallas kernels: 24.8 us -> 16.9 us  [attn_bwd(): pl.pallas_call(functools.partial(attn_bwd_body, heads), out_shape=(jax.Sh...]
    slice x5 -> x0, local copies, waits for them, and re-layouts: 7.7 us -> none  [the longest x1 2.6 us: on_device(): mlp_all[features:]]
    ppermute x2 -> x0, waiting for transfers between devices: 4.98 us -> none  [the longest x1 4.98 us: on_device(): x_got = lax.ppermute(mine[0], 'tensor', ACROSS)]
    ppermute x1, waiting for transfers between devices: 1.32 us -> 4.48 us  [along_lo(): return lax.ppermute(x, 'batch', pairs)]
    pallas_call x0 -> x1, Pallas kernels: none -> 3.01 us  [widen(): pl.pallas_call(functools.partial(widen_body, heads), out_shape=(out(width...]
    squeeze x2 -> x0, local copies, waits for them, and re-layouts: 2.56 us -> none  [the longest x1 1.63 us: on_device(): joint[0]]
  transfers between devices with their start and end apart: 6 -> 4, of which waited for: 2 -> 2; matrix products, arithmetic and copies ran while one was open for 7% -> 0% of each run, Pallas kernels for 59% -> 21%
where the time goes in v2:
time: 192 us
  Pallas kernels  172 us (90%)
  starting transfers between devices  6.6 us (3%)
  local copies, waits for them, and re-layouts  5.96 us (3%)
  waiting for transfers between devices  5.74 us (3%)
    pallas_call x1, Pallas kernels, back(): pl.pallas_call(functools.partial(back_body, heads, n_hi, n_lo), out_shape...  81 us
    pallas_call x1, Pallas kernels, front(): pl.pallas_call(functools.partial(front_body, heads), out_shape=(like,) *...  47.9 us
    pallas_call x1, Pallas kernels, attn_fwd(): pl.pallas_call(functools.partial(attn_fwd_body, heads), out_shape=(like,...  23.1 us
    pallas_call x1, Pallas kernels, attn_bwd(): pl.pallas_call(functools.partial(attn_bwd_body, heads), out_shape=(jax.Sh...  16.9 us
    unnamed x14, local copies, waits for them, and re-layouts  5.96 us
    ppermute x3, starting transfers between devices, along_hi(): return lax.ppermute(x, 'batch', pairs)  5.36 us
    ppermute x1, waiting for transfers between devices, along_lo(): return lax.ppermute(x, 'batch', pairs)  4.48 us
  transfers between devices with their start and end apart: 4, of which 2 were waited for; matrix products, arithmetic and copies ran while one was open for 0% of the time, Pallas kernels for 21%

profile of v2, /device:TPU:0, one launch (start us, length us, event | category | flops | bytes accessed | tf_op | source)
XLA Modules:
  0.0 192.1 jit_solution(14008690348349273737)
XLA Ops:
  0.6 47.9 %gather_and_project.1 = (bf16[4,512,384]{2,1,0:T(8,128)(2,1)}, bf16[4,512,384]{2,1,0:T(8,128)(2,1)}, bf16[4,512,384]{2,1,0:T(8,128)(2,1)}, bf16[4,512,384]{2,1,0...) custom-call(bf16[512,768]{1,0:T(8,128)(2,1)} %tokens.3, ...), custom_call_target="tpu_custom_call" | custom-call | tf_op jit(solution)/shard_map/gather_and_project/pallas_call | solution.py:705
  48.5 1.2 collective-permute-start
  49.8 0.0 copy-start.3
  49.8 23.1 %attention_forward.1 = (bf16[4,512,384]{2,1,0:T(8,128)(2,1)}, bf16[4,512,384]{2,1,0:T(8,128)(2,1)}, bf16[2,512,768]{2,1,0:T(8,128)(2,1)}, bf16[2,512,768]{2,1,0:T(8,128)(2,1)}, bf16[192,768]{1,0:T(8,128)(2,1)}) custom-call(s32[80]{0:T(128)} %len_ref.3, s32[80]{0:T(128)} %group_ref.3, bf16[4,512,384]{2,1,0:T(8,128)(2,1)} %get-tuple-element.45.qa, ...), custom_call_target="tpu_custom_call" | custom-call | flops 8000000000 | bytes 30000000 | tf_op jit(solution)/shard_map/attention_forward/pallas_call | solution.py:266
  72.9 4.5 %collective-permute-done = bf16[4,192,768]{2,1,0:T(8,128)(2,1)S(1)} collective-permute-done((bf16[4,192,768]{2,1,0:T(8,128)(2,1)}, bf16[4,192,768]{2,1,0:T(8,128)(2,1)S(1)}, u32[]{:S(2)}, u32[]{:S(2)}) %collective-permute-start) | collective-permute-done | bytes 1179680 | tf_op jit(solution)/shard_map/ppermute | solution.py:1150
  77.4 0.0 copy-done.3
  77.4 0.2 fusion.4
  77.6 1.4 collective-permute-start.1
  79.1 2.6 %collective-permute-start.2 = (bf16[192,768]{1,0:T(8,128)(2,1)S(1)}, bf16[192,768]{1,0:T(8,128)(2,1)S(1)}, u32[]{:S(2)}, u32[]{:S(2)}) collective-permute-start(bf16[192,768]{1,0:T(8,128)(2,1)S(1)} %get-tuple-element.81), channel_id=1, source_target_pairs={{0,16},{4,20},{8,24},{12,28},{16,0},{20,4},{24,8},{28,12},{1,17},{... | collective-permute-start | bytes 884744 | tf_op jit(solution)/shard_map/ppermute | solution.py:1154
  81.6 1.3 collective-permute-start.3
  83.0 16.9 %attention_backward.1 = (bf16[4,512,640]{2,1,0:T(8,128)(2,1)}, f32[8,384]{1,0:T(8,128)}) custom-call(s32[80]{0:T(128)} %len_ref.3, s32[80]{0:T(128)} %group_ref.3, bf16[4,512,384]{2,1,0:T(8,128)(2,1)} %get-tuple-element.51.qb, bf16[4,512,384]{2,1,0:T(8,128)(2,1)} %get-tuple-element.46.ka, bf16[4,512,384]{2,1,0:T(8,128)(2,1)} %get-tuple-element.47.va, ...), custom_call_target="tpu_custom_call" | custom-call | flops 16000000000 | bytes 30000000 | tf_op jit(solution)/shard_map/attention_backward/pallas_call | solution.py:449
  99.9 0.0 collective-permute-done.1
  99.9 1.3 collective-permute-done.2
  101.1 0.0 collective-permute-done.3
  101.1 0.9 fusion.2.mlp_own
  102.0 81.0 %reduce_gradients.1 = (bf16[512,768]{1,0:T(8,128)(2,1)}, bf16[512,768]{1,0:T(8,128)(2,1)}, bf16[4,2,192,768]{3,2,1,0:T(8,128)(2,1)}, bf16[4,2,192,384]{3,2,1,0:T(8,128)(2,1)}, f32[8,768]{1,0:T(8,128)}) custom-call(bf16[4,512,640]{2,1,0:T(8,128)(2,1)} %get-tuple-element.55.d_qkv_hbm, bf16[4,512,768]{2,1,0:T(8,128)(2,1)} %get-tuple-element.56.nall_hbm, ...), custom_call_target="tpu_custom_call" | custom-call | tf_op jit(solution)/shard_map/reduce_gradients/pallas_call | solution.py:1034
  183.1 0.0 copy-start
  183.1 1.7 copy-done
  184.7 0.0 copy-start.1
  184.7 1.3 copy-done.1
  186.0 0.0 copy-start.2
  186.0 0.7 copy-done.2
  186.7 0.0 copy-start.5
  186.7 3.0 %widen_gradients.1 = (f32[576,768]{1,0:T(8,128)}, f32[192,768]{1,0:T(8,128)}, f32[768,768]{1,0:T(8,128)}, f32[768,768]{1,0:T(8,128)}, f32[768]{0:T(1024)}, /*ind...) custom-call(bf16[8,192,768]{2,1,0:T(8,128)(2,1)S(1)} %bitcast.15, bf16[2,768,384]{2,1,0:T(8,128)(2,1)S(1)} %bitcast.16, ...), custom_call_target="tpu_custom_call" | custom-call | tf_op jit(solution)/shard_map/widen_gradients/pallas_call | solution.py:1119
  189.8 0.0 copy-start.4
  189.8 0.0 copy-done.5
  189.8 0.9 copy.26
  190.7 0.5 copy-done.4
  191.2 0.9 copy.27
Async XLA Ops:
  48.5 28.9 %collective-permute-start = (bf16[4,192,768]{2,1,0:T(8,128)(2,1)}, bf16[4,192,768]{2,1,0:T(8,128)(2,1)S(1)}, u32[]{:S(2)}, u32[]{:S(2)}) collective-permute-start(bf16[4,192,768]{2,1,0:T(8,128)(2,1)} %get-tuple-element.62), channel_id=1, source_target_pairs={{0,4},{4,0},{8,12},{12,8},{16,20},{20,16},{24,28},{28,24},{1,5},{5... | collective-permute-start | bytes 3538952 | tf_op jit(solution)/shard_map/ppermute | solution.py:1150
  49.8 27.6 %copy-start.3 = (bf16[4,192,768]{2,1,0:T(8,128)(2,1)S(1)}, bf16[4,192,768]{2,1,0:T(8,128)(2,1)}, u32[]{:S(2)}) copy-start(bf16[4,192,768]{2,1,0:T(8,128)(2,1)} %get-tuple-element.61) | copy-start | bytes 3538948
  77.6 22.2 %collective-permute-start.1 = (bf16[192,768]{1,0:T(8,128)(2,1)S(1)}, bf16[192,768]{1,0:T(8,128)(2,1)S(1)}, u32[]{:S(2)}, u32[]{:S(2)}) collective-permute-start(bf16[192,768]{1,0:T(8,128)(2,1)S(1)} %get-tuple-element.79), channel_id=1, source_target_pairs={{0,8},{4,12},{8,16},{12,20},{16,24},{20,28},{24,0},{28,4},{1,9},{5... | collective-permute-start | bytes 884744 | tf_op jit(solution)/shard_map/ppermute | solution.py:1154
  79.1 22.1 %collective-permute-start.2 = (bf16[192,768]{1,0:T(8,128)(2,1)S(1)}, bf16[192,768]{1,0:T(8,128)(2,1)S(1)}, u32[]{:S(2)}, u32[]{:S(2)}) collective-permute-start(bf16[192,768]{1,0:T(8,128)(2,1)S(1)} %get-tuple-element.81), channel_id=1, source_target_pairs={{0,16},{4,20},{8,24},{12,28},{16,0},{20,4},{24,8},{28,12},{1,17},{... | collective-permute-start | bytes 884744 | tf_op jit(solution)/shard_map/ppermute | solution.py:1154
  81.6 19.5 %collective-permute-start.3 = (bf16[192,768]{1,0:T(8,128)(2,1)S(1)}, bf16[192,768]{1,0:T(8,128)(2,1)S(1)}, u32[]{:S(2)}, u32[]{:S(2)}) collective-permute-start(bf16[192,768]{1,0:T(8,128)(2,1)S(1)} %get-tuple-element.80), channel_id=1, source_target_pairs={{0,24},{4,28},{8,0},{12,4},{16,8},{20,12},{24,16},{28,20},{1,25},{... | collective-permute-start | bytes 884744 | tf_op jit(solution)/shard_map/ppermute | solution.py:1154
  183.1 1.7 copy-start
  184.7 1.3 copy-start.1
  186.0 0.7 copy-start.2
  186.7 3.0 %copy-start.5 = (bf16[512,768]{1,0:T(8,128)(2,1)S(1)}, bf16[512,768]{1,0:T(8,128)(2,1)}, u32[]{:S(2)}) copy-start(bf16[512,768]{1,0:T(8,128)(2,1)} %get-tuple-element.93) | copy-start | bytes 2359300
  189.8 1.4 copy-start.4

commit v3 on v2

--- a/solution.py
+++ b/solution.py
@@ -134,13 +134,9 @@
 
 
 def attn_fwd_body(
-    heads, len_ref, group_ref, qa, ka, va, do, attn_out, mlp_part_hbm, call_hbm,
-    qb, dob, give, keep, attn_grad, seg, acc, ho, mlp_part, call, out_pad, grad_acc, sems,
+    heads, len_ref, group_ref, qa, ka, va, do, qb, dob, ho, seg, acc,
 ):
     strips, tok_dev = qa.shape[0], qa.shape[1]
-    loads = [pltpu.make_async_copy(mlp_part_hbm, mlp_part, sems.at[0]), pltpu.make_async_copy(call_hbm, call, sems.at[1])]
-    for load in loads:
-        load.start()
     zero = jnp.zeros((), BF16)
     big = middle_rows(tok_dev)
 
@@ -228,60 +224,25 @@
 
     for_segments(len_ref, group_ref, seg, strips, tok_dev, small, middle, large)
 
-    width = attn_out.shape[0]
-    out_pad[:width] = attn_out[...]
-    out_pad[width:] = jnp.zeros((out_pad.shape[0] - width, out_pad.shape[1]), BF16)
-    for load in loads:
-        load.wait()
-    me = lax.axis_index("tensor")
-    grad_acc[...] = jnp.zeros_like(grad_acc)
-
-    def project(strip, _):
-        heads_rows = ho[strip]
-        out = (nn(heads_rows, out_pad[...]) + mlp_part[strip].astype(F32)).astype(BF16)
-        own = jnp.where(strip // 2 == me // 2, 1, 0)
-
-        @pl.when(strip % 2 == me % 2)
-        def _():
-            keep[own] = out
-
-        @pl.when(strip % 2 != me % 2)
-        def _():
-            give[own] = out
-
-        grad_acc[...] += tn(heads_rows, call[strip])
-        return 0
-
-    lax.fori_loop(0, strips, project, 0)
-    attn_grad[...] = grad_acc[:width].astype(BF16)
-
-
-def attn_fwd(image_len, image_group, qa, ka, va, do, attn_out, mlp_part, call):
+
+def attn_fwd(image_len, image_group, qa, ka, va, do):
     strips, tok_dev, width = qa.shape
     heads = width // LANES
-    features = call.shape[2]
     packed = (heads + 1) // 2 * LANES
     like = jax.ShapeDtypeStruct(qa.shape, BF16)
-    half = jax.ShapeDtypeStruct((strips // 2, tok_dev, features), BF16)
     return pl.pallas_call(
         functools.partial(attn_fwd_body, heads),
-        out_shape=(like, like, half, half, jax.ShapeDtypeStruct(attn_out.shape, BF16)),
-        in_specs=[SMEM, SMEM] + [VMEM] * 5 + [ANY] * 2,
-        out_specs=(VMEM,) * 5,
+        out_shape=(like, like, jax.ShapeDtypeStruct((strips, tok_dev, packed), BF16)),
+        in_specs=[SMEM, SMEM] + [VMEM] * 4,
+        out_specs=(VMEM,) * 3,
         scratch_shapes=[
             pltpu.SMEM((2, image_len.shape[0] + 1), jnp.int32),
             pltpu.VMEM((heads, strips * middle_rows(tok_dev), LANES), F32),
-            pltpu.VMEM((strips, tok_dev, packed), BF16),
-            pltpu.VMEM(call.shape, BF16),
-            pltpu.VMEM(call.shape, BF16),
-            pltpu.VMEM((packed, features), BF16),
-            pltpu.VMEM((packed, features), F32),
-            pltpu.SemaphoreType.DMA((2,)),
         ],
         compiler_params=pltpu.CompilerParams(vmem_limit_bytes=60 << 20),
         cost_estimate=pl.CostEstimate(flops=8 * 10**9, bytes_accessed=30 * 10**6, transcendentals=8 * 10**6),
         name="attention_forward",
-    )(image_len, image_group, qa, ka, va, do, attn_out, mlp_part, call)
+    )(image_len, image_group, qa, ka, va, do)
 
 
 def attn_bwd_body(
@@ -489,14 +450,18 @@
     )
 
 
+def lo_rows(features):
+    return 2 * features * 2 // 3
+
+
 def front_body(
-    heads, tokens, cot, ln_gain, qkv_weight_t, q_gain, k_gain, attn_out, mlp_in, mlp_bias, mlp_out,
+    heads, n_hi, n_lo, tokens, cot, ln_gain, qkv_weight_t, q_gain, k_gain, attn_out, mlp_in, mlp_bias, mlp_out,
     qa_out, ka_out, va_out, do_out, u_out, r_out, mlp_part_out, dn_part_out, nall_out, call_out,
     *rest,
 ):
     (rows_out, both, wide, narrow, qkv_pad, mlp_out_t, mlp_in_t, attn_out_t, g_in, g_out,
      send_sem, recv_sem, save_sem) = rest[-13:]
-    grad_outs = rest[:-13]
+    lo_first, hi_first = rest[:n_lo], rest[n_lo : n_lo + n_hi]
     batch, me = lax.axis_index("batch"), lax.axis_index("tensor")
     sibling = me + 1 - 2 * (me % 2)
     across = (me + 2) % 4
@@ -655,21 +620,22 @@
 
     lax.fori_loop(0, 2 * CHUNKS, unit, 0)
 
-    n_lo = len(grad_outs)
-    n_hi, chunk_rows = grad_outs[0].shape[0], grad_outs[0].shape[1]
     hi, lo = batch // n_lo, batch % n_lo
-    per_grad = features // chunk_rows
     for o in range(n_hi * n_lo):
-        source = (g_in, g_out)[o // per_grad]
-        row = o % per_grad * chunk_rows
-        low = source[row : row + chunk_rows, :].astype(BF16)
         at_hi = (o // n_lo - hi + n_hi) % n_hi
         at_lo = (o % n_lo - lo + n_lo) % n_lo
-        for m in range(n_lo):
-
-            @pl.when(at_lo == m)
-            def _():
-                grad_outs[m][at_hi] = low
+        for first, part in ((0, lo_first), (lo_rows(features), hi_first)):
+            chunk_rows = part[0].shape[1]
+            row = first + o * chunk_rows
+            source = (g_in, g_out)[row // features]
+            row = row % features
+            low = source[row : row + chunk_rows, :].astype(BF16)
+            slot, place = (at_lo, at_hi) if first == 0 else (at_hi, at_lo)
+            for m in range(len(part)):
+
+                @pl.when(slot == m)
+                def _():
+                    part[m][place] = low
 
     grown = g_in[...] * mlp_in[...].astype(F32)
     grown_hi = grown.astype(BF16)
@@ -703,12 +669,14 @@
     like = jax.ShapeDtypeStruct((strips, tok_dev, width), BF16)
     rows = jax.ShapeDtypeStruct((strips, tok_dev, features), BF16)
     return pl.pallas_call(
-        functools.partial(front_body, heads),
+        functools.partial(front_body, heads, n_hi, n_lo),
         out_shape=(like,) * 6 + (rows,) * 4 + (
-            jax.ShapeDtypeStruct((n_hi, 2 * features // n_batch, features), BF16),
-        ) * n_lo + (jax.ShapeDtypeStruct((8, features), F32),),
+            jax.ShapeDtypeStruct((n_hi, lo_rows(features) // n_batch, features), BF16),
+        ) * n_lo + (
+            jax.ShapeDtypeStruct((n_lo, (2 * features - lo_rows(features)) // n_batch, features), BF16),
+        ) * n_hi + (jax.ShapeDtypeStruct((8, features), F32),),
         in_specs=[VMEM] * 10,
-        out_specs=(ANY,) * 10 + (VMEM,) * (n_lo + 1),
+        out_specs=(ANY,) * 10 + (VMEM,) * (n_lo + n_hi + 1),
         scratch_shapes=[
             pltpu.VMEM((2, strips, tok_dev, features), BF16),
             pltpu.VMEM((2, strips, tok_dev, features), BF16),
@@ -729,26 +697,29 @@
 
 
 def back_body(
-    heads, n_hi, n_lo, d_qkv_hbm, nall_hbm, dn_part_hbm, give, keep, qkv_weight_t, tokens, cot, ln_gain, out_bias, attn_grad,
-    mlp_own, front_rows, gain_rows, output, input_grad, mlp_all_out, joint_all_out, rows_out,
-    d_qkv, nall, dn_part, weight_t, acc, joint, joint_low, joint_got, joint_sum, joint_got_hi, joint_all, mlp_all,
-    near, core_give, core_got, x_give, x_got, out_got, out_give, out_far, vec, vec_lo, vec_hi, vec_pair,
-    load_sem, mlp_s, mlp_r, joint_s, joint_r, hi_s, hi_r, all_s, all_r, core_s, core_r, x_s, x_r, out_core_s, out_core_r, out_x_s, out_x_r, vec_s, vec_r, save_sem,
+    heads, n_hi, n_lo, d_qkv_hbm, nall_hbm, dn_part_hbm, ho_hbm, call_hbm, mlp_part_hbm, qkv_weight_t, attn_out, tokens, cot,
+    ln_gain, out_bias, own_lo, own_hi, front_rows, gain_rows, output, input_grad, mlp_all_out, joint_all_out, rows_out,
+    d_qkv, nall, dn_part, ho, call, mlp_part, weight_t, attn_pad, acc, attn_acc, joint, joint_low, joint_got, joint_sum,
+    joint_got_hi, joint_all, mlp_all, near, core_give, core_got, x_give, x_got, vec, vec_lo, vec_hi, vec_pair,
+    load_sem, mlp_z_s, mlp_z_r, mlp_y_s, mlp_y_r, joint_s, joint_r, hi_s, hi_r, all_z_s, all_z_r, all_y_s, all_y_r,
+    core_s, core_r, x_s, x_r, vec_s, vec_r, save_sem,
 ):
     batch, me = lax.axis_index("batch"), lax.axis_index("tensor")
     hi, lo = batch // n_lo, batch % n_lo
     sibling = me + 1 - 2 * (me % 2)
     across = (me + 2) % 4
-    chip, core = me // 2, me % 2
+    far_sibling = (sibling + 2) % 4
     tok_dev, features = tokens.shape
     step = tok_dev // CHUNKS
-    chunk_rows, chunk_cols = joint.shape[2], joint.shape[3]
-    half_cols = chunk_cols
-
-    loads = [
-        pltpu.make_async_copy(a, b, load_sem.at[i])
-        for i, (a, b) in enumerate(((d_qkv_hbm, d_qkv), (nall_hbm, nall), (dn_part_hbm, dn_part)))
-    ]
+    chunk_rows, half_cols = joint.shape[2], joint.shape[3]
+    every_k, every_m = range(1, n_hi), range(1, n_lo)
+    cut = chunk_rows // 2 // 16 * 16
+    parts = [pl.ds(0, cut), pl.ds(cut, chunk_rows - cut)]
+
+    sources = (
+        (d_qkv_hbm, d_qkv), (nall_hbm, nall), (ho_hbm, ho), (call_hbm, call), (dn_part_hbm, dn_part), (mlp_part_hbm, mlp_part)
+    )
+    loads = [pltpu.make_async_copy(a, b, load_sem.at[i]) for i, (a, b) in enumerate(sources)]
     for load in loads:
         load.start()
 
@@ -765,103 +736,120 @@
         return (hi * n_lo + lo_peer(m), me)
 
     barrier = pltpu.get_barrier_semaphore()
-    peers = [to_hi(k) for k in range(1, n_hi)] + [to_lo(m) for m in range(1, n_lo)] + [(batch, sibling), (batch, across)]
+    peers = [to_hi(k) for k in every_k] + [to_lo(m) for m in every_m] + [(batch, sibling), (batch, across)]
     for peer in peers:
         pl.semaphore_signal(barrier, inc=1, device_id=peer, device_id_type=pl.DeviceIdType.MESH)
-    mlp_all[hi, lo] = mlp_own[...]
+    mlp_all[hi, lo] = jnp.concatenate([own_lo[...], own_hi[...]], axis=0)
     pl.semaphore_wait(barrier, len(peers))
 
-    def gather_hi(buf, sends, recvs, k, back=0):
-        part = buf.at[hi_peer(back), lo]
-        return remote(part, part, sends.at[0, k], recvs.at[0, k], to_hi(k))
-
-    def gather_lo(buf, sends, recvs, m, k, back=0):
-        part = buf.at[hi_peer(-k), lo_peer(back)]
-        return remote(part, part, sends.at[m, k], recvs.at[m, k], to_lo(m))
-
-    def gather_start(buf, sends, recvs):
-        for k in range(1, n_hi):
-            gather_hi(buf, sends, recvs, k).start()
-        for m in range(1, n_lo):
-            gather_lo(buf, sends, recvs, m, 0).start()
-
-    def gather_pass(buf, sends, recvs, k):
-        gather_hi(buf, sends, recvs, k, -k).wait_recv()
-        for m in range(1, n_lo):
-            gather_lo(buf, sends, recvs, m, k).start()
-
-    def gather_end(buf, sends, recvs):
-        for m in range(1, n_lo):
-            for k in range(n_hi):
-                gather_lo(buf, sends, recvs, m, k, -m).wait_recv()
-        for k in range(1, n_hi):
-            gather_hi(buf, sends, recvs, k).wait_send()
-        for m in range(1, n_lo):
-            for k in range(n_hi):
-                gather_lo(buf, sends, recvs, m, k).wait_send()
-
-    def rows_of(c):
-        return pl.ds(pl.multiple_of(c * step, step), step)
-
-    def out_core(c):
-        where = rows_of(c)
-        return remote(give.at[:, where], out_got.at[:, where], out_core_s.at[c], out_core_r.at[c], (batch, sibling))
-
-    def out_across(c):
-        return remote(out_give.at[rows_of(c)], out_far.at[rows_of(c)], out_x_s.at[c], out_x_r.at[c], (batch, across))
-
-    def out_start(c, _):
-        out_core(c).start()
-        return 0
-
-    def out_send(c, _):
-        out_core(c).wait_recv()
-        where = rows_of(c)
-        out_give[where] = (keep[0, where].astype(F32) + out_got[0, where].astype(F32)).astype(BF16)
-        out_across(c).start()
-        return 0
-
-    def out_rows(c, _):
-        out_across(c).wait_recv()
-        where = rows_of(c)
-        total = keep[1, where].astype(F32) + out_got[1, where].astype(F32) + out_far[where].astype(F32)
-        output[where] = (tokens[where].astype(F32) + total + bias).astype(BF16)
-        return 0
-
-    bias = row_of(out_bias)
-    lax.fori_loop(0, CHUNKS, out_start, 0)
-    gather_start(mlp_all, mlp_s, mlp_r)
-    lax.fori_loop(0, CHUNKS, out_send, 0)
+    def mlp_hop(s, up, origin):
+        part = mlp_all.at[origin, lo]
+        to = ((hi + (1 if up else -1) + n_hi) % n_hi * n_lo + lo, me)
+        return remote(part, part, mlp_z_s.at[up, s], mlp_z_r.at[up, s], to)
+
+    def mlp_send_hop(s, wait=False):
+        for up in range(2):
+            origin = hi - (s - 1) if up else hi + (s - 1)
+            there = (origin >= 0) & (hi + 1 < n_hi) if up else (origin < n_hi) & (hi >= 1)
+
+            @pl.when(there)
+            def _():
+                hop = mlp_hop(s, up, (origin + n_hi) % n_hi)
+                hop.wait_send() if wait else hop.start()
+
+    def mlp_wait_hop(s):
+        for up in range(2):
+            origin = hi - s if up else hi + s
+
+            @pl.when((origin >= 0) if up else (origin < n_hi))
+            def _():
+                mlp_hop(s, up, (origin + n_hi) % n_hi).wait_recv()
+
+    def mlp_lo(m, k, back=0):
+        part = mlp_all.at[hi_peer(k), lo_peer(back)]
+        return remote(part, part, mlp_y_s.at[m, k], mlp_y_r.at[m, k], to_lo(m))
+
+    def mlp_send_lo(s):
+        for m in every_m:
+            for k, there in ((s, hi + s < n_hi), (n_hi - s, hi >= s)):
+
+                @pl.when(there)
+                def _():
+                    mlp_lo(m, k).start()
+
+    for m in every_m:
+        mlp_lo(m, 0).start()
+    mlp_send_hop(1)
 
     weight_t[...] = by_kind(qkv_weight_t, heads, weight_t.shape[0])
-
-    loads[0].wait()
-    loads[1].wait()
+    head_width = attn_out.shape[0]
+    attn_pad[:head_width] = attn_out[...]
+    attn_pad[head_width:] = jnp.zeros((attn_pad.shape[0] - head_width, features), BF16)
     acc[...] = jnp.zeros_like(acc)
+    attn_acc[...] = jnp.zeros_like(attn_acc)
+    for load in loads[:4]:
+        load.wait()
 
     def add_strip(i, _):
         acc[...] += tn(d_qkv[i], nall[i])
+        attn_acc[...] += tn(ho[i], call[i])
         return 0
 
     lax.fori_loop(0, nall.shape[0], add_strip, 0)
     width = qkv_weight_t.shape[0]
     joint_low[:width] = acc[:width].astype(BF16)
-    joint_low[width:] = attn_grad[...]
+    joint_low[width:] = attn_acc[:head_width].astype(BF16)
     per_half = features // chunk_rows
     for o in range(n_hi * n_lo):
         row = o % per_half * chunk_rows
         col = o // per_half * half_cols
-        joint[o // n_lo, o % n_lo] = joint_low[row : row + chunk_rows, col : col + half_cols]
-
-    def joint_move(m, k, back=0):
+        joint[o % n_lo, o // n_lo] = joint_low[row : row + chunk_rows, col : col + half_cols]
+
+    def joint_lo(p, m, back=0):
         return remote(
-            joint.at[hi_peer(k), lo_peer(m)], joint_got.at[lo_peer(back), hi_peer(k)],
-            joint_s.at[m, k], joint_r.at[m, k], to_lo(m),
+            joint.at[lo_peer(m), :, parts[p]], joint_got.at[lo_peer(back), :, parts[p]], joint_s.at[m, p], joint_r.at[m, p], to_lo(m)
         )
 
-    for k in list(range(1, n_hi)) + [0]:
-        for m in range(1, n_lo):
-            joint_move(m, k).start()
+    def joint_hi(p, k, back=0):
+        return remote(
+            joint_sum.at[hi_peer(k), parts[p]], joint_got_hi.at[hi_peer(back), parts[p]], hi_s.at[k, p], hi_r.at[k, p], to_hi(k)
+        )
+
+    def joint_sum_lo(p):
+        for m in every_m:
+            joint_lo(p, m, -m).wait_recv()
+        total = joint[lo, :, parts[p]].astype(F32)
+        for m in every_m:
+            total = total + joint_got[lo_peer(m), :, parts[p]].astype(F32)
+        joint_sum[:, parts[p]] = total.astype(BF16)
+        for k in every_k:
+            joint_hi(p, k).start()
+
+    def all_hi(p, k, back=0):
+        part = joint_all.at[lo, hi_peer(back), parts[p]]
+        return remote(part, part, all_z_s.at[k, p], all_z_r.at[k, p], to_hi(k))
+
+    def all_lo(p, m, back=0):
+        part = joint_all.at[lo_peer(back), :, parts[p]]
+        return remote(part, part, all_y_s.at[m, p], all_y_r.at[m, p], to_lo(m))
+
+    def joint_sum_hi(p):
+        total = joint_sum[hi, parts[p]].astype(F32)
+        for k in every_k:
+            joint_hi(p, k, -k).wait_recv()
+            total = total + joint_got_hi[hi_peer(-k), parts[p]].astype(F32)
+        joint_all[lo, hi, parts[p]] = total.astype(BF16)
+        for k in every_k:
+            all_hi(p, k).start()
+
+    def joint_pass(p):
+        for k in every_k:
+            all_hi(p, k, -k).wait_recv()
+        for m in every_m:
+            all_lo(p, m).start()
+
+    for m in every_m:
+        joint_lo(0, m).start()
 
     ln_row = jnp.sum(acc[...] * weight_t[...].astype(F32), axis=0, keepdims=True)
     gain = row_of(ln_gain)
@@ -880,72 +868,94 @@
     def vec_pair_move(i, to):
         return remote(vec.at[i], vec_pair.at[i], vec_s.at[n_lo + n_hi + i], vec_r.at[n_lo + n_hi + i], (batch, to))
 
-    for m in range(1, n_lo):
+    for m in every_m:
         vec_lo_move(m).start()
-
-    loads[2].wait()
-
-    def partial_rows(strip, c):
-        return nn(d_qkv[strip, rows_of(c)], weight_t[...]) + dn_part[strip, rows_of(c)].astype(F32)
-
-    def core_move(side, c):
+    mlp_wait_hop(1)
+    mlp_send_hop(2)
+
+    def rows_of(c):
+        return pl.ds(pl.multiple_of(c * step, step), step)
+
+    def partial_rows(which, strip, c):
+        if which == 0:
+            return nn(d_qkv[strip, rows_of(c)], weight_t[...]) + dn_part[strip, rows_of(c)].astype(F32)
+        return nn(ho[strip, rows_of(c)], attn_pad[...]) + mlp_part[strip, rows_of(c)].astype(F32)
+
+    def core_move(which, side, c):
+        where = rows_of(c)
         return remote(
-            core_give.at[side, rows_of(c)], core_got.at[side, rows_of(c)], core_s.at[side, c], core_r.at[side, c], (batch, sibling)
+            core_give.at[which, side, where], core_got.at[which, side, where],
+            core_s.at[which, side, c], core_r.at[which, side, c], (batch, sibling),
         )
 
-    def x_move(c):
-        return remote(x_give.at[rows_of(c)], x_got.at[rows_of(c)], x_s.at[c], x_r.at[c], (batch, across))
-
-    def give_far(c, _):
-        core_give[0, rows_of(c)] = partial_rows(across + sibling - me, c).astype(BF16)
-        core_move(0, c).start()
-        return 0
-
-    def send_far(c, _):
-        mine = partial_rows(across, c)
-        core_move(0, c).wait_recv()
-        x_give[rows_of(c)] = (mine + core_got[0, rows_of(c)].astype(F32)).astype(BF16)
-        x_move(c).start()
-        return 0
-
-    def give_near(c, _):
-        core_give[1, rows_of(c)] = partial_rows(sibling, c).astype(BF16)
-        core_move(1, c).start()
-        return 0
-
-    def keep_near(c, _):
-        mine = partial_rows(me, c)
-        core_move(1, c).wait_recv()
-        near[rows_of(c)] = mine + core_got[1, rows_of(c)].astype(F32)
-        return 0
-
-    for loop in (give_far, send_far, give_near, keep_near):
-        lax.fori_loop(0, CHUNKS, loop, 0)
-
-    for m in range(1, n_lo):
+    def x_move(which, c):
+        where = rows_of(c)
+        return remote(x_give.at[which, where], x_got.at[which, where], x_s.at[which, c], x_r.at[which, c], (batch, across))
+
+    def far(which):
+        def give(c, _):
+            core_give[which, 0, rows_of(c)] = partial_rows(which, far_sibling, c).astype(BF16)
+            core_move(which, 0, c).start()
+            return 0
+
+        def send(c, _):
+            mine = partial_rows(which, across, c)
+            core_move(which, 0, c).wait_recv()
+            x_give[which, rows_of(c)] = (mine + core_got[which, 0, rows_of(c)].astype(F32)).astype(BF16)
+            x_move(which, c).start()
+            return 0
+
+        lax.fori_loop(0, CHUNKS, give, 0)
+        lax.fori_loop(0, CHUNKS, send, 0)
+
+    def close(which):
+        def give(c, _):
+            core_give[which, 1, rows_of(c)] = partial_rows(which, sibling, c).astype(BF16)
+            core_move(which, 1, c).start()
+            return 0
+
+        def keep(c, _):
+            mine = partial_rows(which, me, c)
+            core_move(which, 1, c).wait_recv()
+            near[which, rows_of(c)] = mine + core_got[which, 1, rows_of(c)].astype(F32)
+            return 0
+
+        lax.fori_loop(0, CHUNKS, give, 0)
+        lax.fori_loop(0, CHUNKS, keep, 0)
+
+    for load in loads[4:]:
+        load.wait()
+    far(0)
+    for m in every_m:
+        joint_lo(1, m).start()
+    far(1)
+    joint_sum_lo(0)
+    for s in range(2, n_hi - 1):
+        mlp_wait_hop(s)
+        mlp_send_hop(s + 1)
+    close(0)
+    joint_sum_lo(1)
+    mlp_send_lo(1)
+    close(1)
+
+    for m in every_m:
         vec_lo_move(m, -m).wait_recv()
     total = vec_lo[0]
     for i in range(1, n_lo):
         total = total + vec_lo[i]
     vec_hi[hi] = total
-    for k in range(1, n_hi):
+    for k in every_k:
         vec_hi_move(k).start()
 
-    def hi_move(k, back=0):
-        return remote(joint_sum.at[hi_peer(k)], joint_got_hi.at[hi_peer(back)], hi_s.at[k], hi_r.at[k], to_hi(k))
-
-    for k in list(range(1, n_hi)) + [0]:
-        for m in range(1, n_lo):
-            joint_move(m, k, -m).wait_recv()
-        where = hi_peer(k)
-        total = joint[where, lo].astype(F32)
-        for m in range(1, n_lo):
-            total = total + joint_got[lo_peer(m), where].astype(F32)
-        joint_sum[where] = total.astype(BF16)
-        if k:
-            hi_move(k).start()
-
-    for k in range(1, n_hi):
+    joint_sum_hi(0)
+    for s in range(2, n_hi - 1):
+        mlp_send_lo(s)
+    joint_sum_hi(1)
+    if n_hi > 2:
+        mlp_wait_hop(n_hi - 1)
+        mlp_send_lo(n_hi - 1)
+
+    for k in every_k:
         vec_hi_move(k, -k).wait_recv()
     total = vec_hi[0]
     for i in range(1, n_hi):
@@ -953,64 +963,72 @@
     vec[0] = total
     vec_pair_move(0, sibling).start()
 
+    joint_pass(0)
+    vec_pair_move(0, sibling).wait_recv()
+    vec[1] = vec[0] + vec_pair[0]
+    vec_pair_move(1, across).start()
+
     def last_rows(c, _):
-        x_move(c).wait_recv()
-        d_normed = near[rows_of(c)] + x_got[rows_of(c)].astype(F32)
-        x = tokens[rows_of(c)].astype(F32)
+        x_move(0, c).wait_recv()
+        where = rows_of(c)
+        d_normed = near[0, where] + x_got[0, where].astype(F32)
+        x = tokens[where].astype(F32)
         centred = x - jnp.mean(x, axis=-1, keepdims=True)
         r = lax.rsqrt(jnp.mean(centred * centred, axis=-1, keepdims=True) + epsilon)
         xhat = centred * r
         e = d_normed * gain
         d_x = r * (e - jnp.mean(e, axis=-1, keepdims=True) - xhat * jnp.mean(e * xhat, axis=-1, keepdims=True))
-        input_grad[rows_of(c)] = (cot[rows_of(c)].astype(F32) + d_x).astype(BF16)
+        input_grad[where] = (cot[where].astype(F32) + d_x).astype(BF16)
         return 0
 
-    for k in range(1, n_hi):
-        gather_pass(mlp_all, mlp_s, mlp_r, k)
+    lax.fori_loop(0, CHUNKS, last_rows, 0)
+    joint_pass(1)
+    bias = row_of(out_bias)
+
+    def out_rows(c, _):
+        x_move(1, c).wait_recv()
+        where = rows_of(c)
+        output[where] = (tokens[where].astype(F32) + near[1, where] + x_got[1, where].astype(F32) + bias).astype(BF16)
+        return 0
+
     lax.fori_loop(0, CHUNKS, out_rows, 0)
-    lax.fori_loop(0, CHUNKS, last_rows, 0)
-
-    vec_pair_move(0, sibling).wait_recv()
-    vec[1] = vec[0] + vec_pair[0]
-    vec_pair_move(1, across).start()
-
-    total = joint_sum[hi].astype(F32)
-    for k in range(1, n_hi):
-        hi_move(k, -k).wait_recv()
-        total = total + joint_got_hi[hi_peer(-k)].astype(F32)
-    joint_all[hi, lo] = total.astype(BF16)
-    gather_start(joint_all, all_s, all_r)
-
     vec_pair_move(1, across).wait_recv()
     rows_out[...] = vec[0]
     rows_out[1:3, :] = vec[1, 1:3, :] + vec_pair[1, 1:3, :]
 
-    for k in range(1, n_hi):
-        gather_pass(joint_all, all_s, all_r, k)
-    gather_end(mlp_all, mlp_s, mlp_r)
+    for m in every_m:
+        for k in range(n_hi):
+            mlp_lo(m, k, -m).wait_recv()
     save_mlp = pltpu.make_async_copy(mlp_all, mlp_all_out, save_sem.at[0])
     save_mlp.start()
-
-    for m in range(1, n_lo):
+    for s in range(1, n_hi):
+        mlp_send_hop(s, wait=True)
+    for m in every_m:
         for k in range(n_hi):
-            joint_move(m, k).wait_send()
+            mlp_lo(m, k).wait_send()
+        for p in range(2):
+            joint_lo(p, m).wait_send()
         vec_lo_move(m).wait_send()
-    for k in range(1, n_hi):
-        hi_move(k).wait_send()
+    for k in every_k:
+        for p in range(2):
+            joint_hi(p, k).wait_send()
+            all_hi(p, k).wait_send()
         vec_hi_move(k).wait_send()
     vec_pair_move(0, sibling).wait_send()
     vec_pair_move(1, across).wait_send()
 
     def sent(c, _):
-        core_move(0, c).wait_send()
-        core_move(1, c).wait_send()
-        x_move(c).wait_send()
-        out_core(c).wait_send()
-        out_across(c).wait_send()
+        for which in range(2):
+            core_move(which, 0, c).wait_send()
+            core_move(which, 1, c).wait_send()
+            x_move(which, c).wait_send()
         return 0
 
     lax.fori_loop(0, CHUNKS, sent, 0)
-    gather_end(joint_all, all_s, all_r)
+    for m in every_m:
+        for p in range(2):
+            all_lo(p, m, -m).wait_recv()
+            all_lo(p, m).wait_send()
     save_joint = pltpu.make_async_copy(joint_all, joint_all_out, save_sem.at[1])
     save_joint.start()
     save_mlp.wait()
@@ -1022,111 +1040,148 @@
     return n_batch // lo, lo
 
 
-def back(n_batch, d_qkv, nall, dn_part, give, keep, qkv_weight_t, tokens, cot, ln_gain, out_bias, attn_grad,
-    mlp_own, front_rows, gain_rows):
+def back(
+    n_batch, d_qkv, nall, dn_part, ho, call, mlp_part, qkv_weight_t, attn_out, tokens, cot, ln_gain, out_bias,
+    own_lo, own_hi, front_rows, gain_rows,
+):
     n_hi, n_lo = levels(n_batch)
     strips, tok_dev, features = nall.shape
-    wide = d_qkv.shape[2]
-    heads = attn_grad.shape[0] // DH
+    own = (own_lo.shape[0] + own_hi.shape[0], features)
+    wide, packed = d_qkv.shape[2], ho.shape[2]
+    heads = attn_out.shape[0] // DH
     chunk = (2 * features // n_batch, features // 2)
     dma = pltpu.SemaphoreType.DMA
-    rows = pltpu.VMEM((8, features), F32)
+    vmem = pltpu.VMEM
     return pl.pallas_call(
         functools.partial(back_body, heads, n_hi, n_lo),
         out_shape=(
             jax.ShapeDtypeStruct(tokens.shape, BF16),
             jax.ShapeDtypeStruct(tokens.shape, BF16),
-            jax.ShapeDtypeStruct((n_hi, n_lo) + mlp_own.shape, BF16),
-            jax.ShapeDtypeStruct((n_hi, n_lo) + chunk, BF16),
+            jax.ShapeDtypeStruct((n_hi, n_lo) + own, BF16),
+            jax.ShapeDtypeStruct((n_lo, n_hi) + chunk, BF16),
             jax.ShapeDtypeStruct((8, features), F32),
         ),
-        in_specs=[ANY] * 3 + [VMEM] * 11,
+        in_specs=[ANY] * 6 + [VMEM] * 10,
         out_specs=(VMEM, VMEM, ANY, ANY, VMEM),
         scratch_shapes=[
-            pltpu.VMEM(d_qkv.shape, BF16),
-            pltpu.VMEM(nall.shape, BF16),
-            pltpu.VMEM(dn_part.shape, BF16),
-            pltpu.VMEM((wide, features), BF16),
-            pltpu.VMEM((wide, features), F32),
-            pltpu.VMEM((n_hi, n_lo) + chunk, BF16),
-            pltpu.VMEM((features, features), BF16),
-            pltpu.VMEM((n_lo, n_hi) + chunk, BF16),
-            pltpu.VMEM((n_hi,) + chunk, BF16),
-            pltpu.VMEM((n_hi,) + chunk, BF16),
-            pltpu.VMEM((n_hi, n_lo) + chunk, BF16),
-            pltpu.VMEM((n_hi, n_lo) + mlp_own.shape, BF16),
-            pltpu.VMEM(tokens.shape, F32),
-            pltpu.VMEM((2,) + tokens.shape, BF16),
-            pltpu.VMEM((2,) + tokens.shape, BF16),
-            pltpu.VMEM(tokens.shape, BF16),
-            pltpu.VMEM(tokens.shape, BF16),
-            pltpu.VMEM((2,) + tokens.shape, BF16),
-            pltpu.VMEM(tokens.shape, BF16),
-            pltpu.VMEM(tokens.shape, BF16),
-            pltpu.VMEM((2, 8, features), F32),
-            pltpu.VMEM((n_lo, 8, features), F32),
-            pltpu.VMEM((n_hi, 8, features), F32),
-            pltpu.VMEM((2, 8, features), F32),
-            dma((3,)),
+            vmem(d_qkv.shape, BF16), vmem(nall.shape, BF16), vmem(dn_part.shape, BF16),
+            vmem(ho.shape, BF16), vmem(call.shape, BF16), vmem(mlp_part.shape, BF16),
+            vmem((wide, features), BF16),
+            vmem((packed, features), BF16),
+            vmem((wide, features), F32),
+            vmem((packed, features), F32),
+            vmem((n_lo, n_hi) + chunk, BF16),
+            vmem((features, features), BF16),
+            vmem((n_lo, n_hi) + chunk, BF16),
+            vmem((n_hi,) + chunk, BF16),
+            vmem((n_hi,) + chunk, BF16),
+            vmem((n_lo, n_hi) + chunk, BF16),
+            vmem((n_hi, n_lo) + own, BF16),
+            vmem((2,) + tokens.shape, F32),
+            vmem((2, 2) + tokens.shape, BF16),
+            vmem((2, 2) + tokens.shape, BF16),
+            vmem((2,) + tokens.shape, BF16),
+            vmem((2,) + tokens.shape, BF16),
+            vmem((2, 8, features), F32),
+            vmem((n_lo, 8, features), F32),
+            vmem((n_hi, 8, features), F32),
+            vmem((2, 8, features), F32),
+            dma((6,)),
+            dma((2, n_hi)), dma((2, n_hi)),
             dma((n_lo, n_hi)), dma((n_lo, n_hi)),
-            dma((n_lo, n_hi)), dma((n_lo, n_hi)),
-            dma((n_hi,)), dma((n_hi,)),
-            dma((n_lo, n_hi)), dma((n_lo, n_hi)),
+            dma((n_lo, 2)), dma((n_lo, 2)),
+            dma((n_hi, 2)), dma((n_hi, 2)),
+            dma((n_hi, 2)), dma((n_hi, 2)),
+            dma((n_lo, 2)), dma((n_lo, 2)),
+            dma((2, 2, CHUNKS)), dma((2, 2, CHUNKS)),
             dma((2, CHUNKS)), dma((2, CHUNKS)),
-            dma((CHUNKS,)), dma((CHUNKS,)),
-            dma((CHUNKS,)), dma((CHUNKS,)),
-            dma((CHUNKS,)), dma((CHUNKS,)),
             dma((n_lo + n_hi + 2,)), dma((n_lo + n_hi + 2,)),
             dma((2,)),
         ],
         compiler_params=pltpu.CompilerParams(collective_id=1, has_side_effects=True, vmem_limit_bytes=60 << 20),
         name="reduce_gradients",
-    )(d_qkv, nall, dn_part, give, keep, qkv_weight_t, tokens, cot, ln_gain, out_bias, attn_grad,
-    mlp_own, front_rows, gain_rows)
-
-
-def widen_body(heads, mlp_all, joint_all, rows, qkv_t, attn, mlp_in, mlp_out, ln_gain, q_gain, k_gain, mlp_bias, out_bias):
+    )(
+        d_qkv, nall, dn_part, ho, call, mlp_part, qkv_weight_t, attn_out, tokens, cot, ln_gain, out_bias,
+        own_lo, own_hi, front_rows, gain_rows,
+    )
+
+
+def widen_body(
+    heads, mlp_hbm, joint_hbm, output_in, input_grad_in, rows,
+    output, input_grad, qkv_out, attn_out, mlp_in_out, mlp_out_out, ln_gain, q_gain, k_gain, mlp_bias, out_bias,
+    mlp_all, joint_all, joint, qkv_t, attn, mlp, sems,
+):
+    def copy(i, source, to):
+        made = pltpu.make_async_copy(source, to, sems.at[i])
+        made.start()
+        return made
+
+    load_joint = copy(0, joint_hbm, joint_all)
+    load_mlp = copy(1, mlp_hbm, mlp_all)
     features = rows.shape[1]
-    chunks = mlp_all.shape[0]
-    chunk_rows = mlp_all.shape[1]
-    per_grad = features // chunk_rows
-    width = qkv_t.shape[0]
-    cols = joint_all.shape[2]
-    for o in range(chunks):
-        low = o % per_grad * chunk_rows
-        (mlp_in, mlp_out)[o // per_grad][low : low + chunk_rows, :] = mlp_all[o].astype(F32)
-    for half in range(2):
-        at = slice(half * cols, (half + 1) * cols)
-        kinds = [(3 * h + i) * DH for h in range(heads) for i in range(2)] + [(3 * h + 2) * DH for h in range(heads)]
-        for i, to in enumerate(kinds):
-            qkv_t[to : to + DH, at] = joint_all[half, i * DH : (i + 1) * DH].astype(F32)
-        attn[:, at] = joint_all[half, width:].astype(F32)
     mlp_bias[...] = rows[0:1, :].reshape(features)
     out_bias[...] = rows[1:2, :].reshape(features)
     ln_gain[...] = rows[2:3, :].reshape(features)
     for offset, ref in ((0, q_gain), (DH, k_gain)):
         parts = [rows[3:4, h * LANES + offset : h * LANES + offset + DH] for h in range(heads)]
         ref[...] = jnp.concatenate(parts, axis=1).reshape(heads * DH)
-
-
-def widen(heads, width, mlp_all, joint_all, rows):
+    output[...] = output_in[...]
+    input_grad[...] = input_grad_in[...]
+    load_joint.wait()
+    n_lo, n_hi, chunk_rows, cols = joint_all.shape
+    width = qkv_t.shape[0]
+    per_half = features // chunk_rows
+    for o in range(n_lo * n_hi):
+        row = o % per_half * chunk_rows
+        joint[o // per_half, row : row + chunk_rows] = joint_all[o % n_lo, o // n_lo].astype(F32)
+    kinds = [(3 * h + i) * DH for h in range(heads) for i in range(2)] + [(3 * h + 2) * DH for h in range(heads)]
+    for half in range(2):
+        at = slice(half * cols, (half + 1) * cols)
+        for i, to in enumerate(kinds):
+            qkv_t[to : to + DH, at] = joint[half, i * DH : (i + 1) * DH]
+        attn[:, at] = joint[half, width:]
+    pending = [copy(4, qkv_t, qkv_out), copy(5, attn, attn_out)]
+    load_mlp.wait()
+    chunks = mlp_all.shape[0]
+    cut = lo_rows(features) // chunks
+    rest = mlp_all.shape[1] - cut
+    for o in range(chunks):
+        mlp[o * cut : (o + 1) * cut] = mlp_all[o, :cut].astype(F32)
+        row = lo_rows(features) + o * rest
+        mlp[row : row + rest] = mlp_all[o, cut:].astype(F32)
+    pending += [copy(6, mlp.at[:features], mlp_in_out), copy(7, mlp.at[features:], mlp_out_out)]
+    for made in pending:
+        made.wait()
+
+
+def widen(heads, width, mlp_all, joint_all, output, input_grad, rows):
     features = rows.shape[1]
     head_width = heads * DH
 
     def out(*shape):
         return jax.ShapeDtypeStruct(shape, F32)
 
+    like = jax.ShapeDtypeStruct(output.shape, BF16)
     return pl.pallas_call(
         functools.partial(widen_body, heads),
         out_shape=(
-            out(width, features), out(head_width, features), out(features, features), out(features, features),
+            like, like, out(width, features), out(head_width, features), out(features, features), out(features, features),
             out(features), out(head_width), out(head_width), out(features), out(features),
         ),
-        in_specs=[VMEM] * 3,
-        out_specs=(VMEM,) * 9,
-        compiler_params=pltpu.CompilerParams(vmem_limit_bytes=40 << 20),
+        in_specs=[ANY] * 2 + [VMEM] * 3,
+        out_specs=(VMEM,) * 2 + (ANY,) * 4 + (VMEM,) * 5,
+        scratch_shapes=[
+            pltpu.VMEM(mlp_all.shape, BF16),
+            pltpu.VMEM(joint_all.shape, BF16),
+            pltpu.VMEM((2, features, features // 2), F32),
+            pltpu.VMEM((width, features), F32),
+            pltpu.VMEM((head_width, features), F32),
+            pltpu.VMEM((2 * features, features), F32),
+            pltpu.SemaphoreType.DMA((8,)),
+        ],
+        compiler_params=pltpu.CompilerParams(vmem_limit_bytes=60 << 20),
         name="widen_gradients",
-    )(mlp_all, joint_all, rows)
+    )(mlp_all, joint_all, output, input_grad, rows)
 
 
 def on_device(
@@ -1159,18 +1214,24 @@
             total = total + other.astype(F32)
         return total.astype(BF16)
 
-    lo_got = [along_lo(mlp_grad[m], m) for m in range(1, n_lo)]
-    qb, dob, give, keep, attn_grad = attn_fwd(image_len, image_group, qa, ka, va, do, attn_out, mlp_part, call)
-    lo_sum = [add(mlp_grad[0][k], [got[k] for got in lo_got]) for k in range(n_hi)]
-    hi_got = [along_hi(lo_sum[k], k) for k in range(1, n_hi)]
+    lo_first, hi_first = mlp_grad[:n_lo], mlp_grad[n_lo:]
+    lo_got = [along_lo(lo_first[m], m) for m in range(1, n_lo)]
+    hi_got = [along_hi(hi_first[k], k) for k in range(1, n_hi)]
+    qb, dob, ho = attn_fwd(image_len, image_group, qa, ka, va, do)
+    lo_sum = [add(lo_first[0][k], [got[k] for got in lo_got]) for k in range(n_hi)]
+    hi_sum = [add(hi_first[0][m], [got[m] for got in hi_got]) for m in range(n_lo)]
+    qb, lo_sum, hi_sum = lax.optimization_barrier((qb, lo_sum, hi_sum))
+    lo_got = [along_hi(lo_sum[k], k) for k in range(1, n_hi)]
+    hi_got = [along_lo(hi_sum[m], m) for m in range(1, n_lo)]
     d_qkv, gain_rows = attn_bwd(image_len, image_group, qb, ka, va, dob, u, r, q_gain, k_gain)
-    mlp_own = add(lo_sum[0], hi_got)
+    own_lo, own_hi = add(lo_sum[0], lo_got), add(hi_sum[0], hi_got)
     output, input_grad, mlp_all, joint_all, rows = back(
-        n_batch, d_qkv, nall, dn_part, give, keep, weight_t, tokens, out_cotangent, ln_gain, out_bias, attn_grad,
-        mlp_own, front_rows, gain_rows,
+        n_batch, d_qkv, nall, dn_part, ho, call, mlp_part, weight_t, attn_out, tokens, out_cotangent, ln_gain, out_bias,
+        own_lo, own_hi, front_rows, gain_rows,
     )
-    qkv_t, attn, mlp_in_grad, mlp_out_grad, ln, q, k, bias, out_bias_grad = widen(
-        heads, qkv_cols, mlp_all.reshape((n_batch,) + mlp_all.shape[2:]), joint_all.reshape(2, features, -1), rows
+    output, input_grad, qkv_t, attn, mlp_in_grad, mlp_out_grad, ln, q, k, bias, out_bias_grad = widen(
+        heads, qkv_cols, mlp_all.reshape((n_batch,) + mlp_all.shape[2:]), joint_all,
+        output, input_grad, rows,
     )
     return output, input_grad, ln, qkv_t.T, q, k, attn, mlp_in_grad, bias, mlp_out_grad, out_bias_grad
 

time: 192 us -> 173 us (0.901)
  Pallas kernels: 172 us -> 158 us
  local copies, waits for them, and re-layouts: 5.96 us -> 0.01 us
  waiting for transfers between devices: 5.74 us -> 0.02 us
  starting transfers between devices: 6.6 us -> 12.3 us
    pallas_call x1, Pallas kernels: 81 us -> 67 us  [back(): pl.pallas_call(functools.partial(back_body, heads, n_hi, n_lo), out_shape...]
    unnamed x14 -> x4, local copies, waits for them, and re-layouts: 5.96 us -> 0.01 us
    ppermute x1 -> x2, waiting for transfers between devices: 4.48 us -> 0.01 us  [along_lo(): return lax.ppermute(x, 'batch', pairs)]
    pallas_call x1, Pallas kernels: 23.1 us -> 18.8 us  [attn_fwd(): pl.pallas_call(functools.partial(attn_fwd_body, heads), out_shape=(like,...]
    pallas_call x2, Pallas kernels: 50.9 us -> 55.2 us  [the longest x1 48.1 us: front(): pl.pallas_call(functools.partial(front_body, heads, n_hi, n_lo), out_shap...]
    ppermute x3 -> x6, starting transfers between devices: 5.36 us -> 9.06 us  [along_hi(): return lax.ppermute(x, 'batch', pairs)]
    ppermute x1 -> x2, starting transfers between devices: 1.24 us -> 3.24 us  [along_lo(): return lax.ppermute(x, 'batch', pairs)]
  transfers between devices with their start and end apart: 4 -> 8, of which waited for: 2 -> 0; matrix products, arithmetic and copies ran while one was open for 0% -> 0% of each run, Pallas kernels for 21% -> 21%
where the time goes in v3:
time: 173 us
  Pallas kernels  158 us (91%)
  starting transfers between devices  12.3 us (7%)
  other arithmetic  1.73 us (1%)
    pallas_call x1, Pallas kernels, back(): pl.pallas_call(functools.partial(back_body, heads, n_hi, n_lo), out_shape...  67 us
    pallas_call x1, Pallas kernels, front(): pl.pallas_call(functools.partial(front_body, heads, n_hi, n_lo), out_shap...  48.1 us
    pallas_call x1, Pallas kernels, attn_fwd(): pl.pallas_call(functools.partial(attn_fwd_body, heads), out_shape=(like,...  18.8 us
    pallas_call x1, Pallas kernels, attn_bwd(): pl.pallas_call(functools.partial(attn_bwd_body, heads), out_shape=(jax.Sh...  16.8 us
    ppermute x6, starting transfers between devices, along_hi(): return lax.ppermute(x, 'batch', pairs)  9.06 us
    pallas_call x1, Pallas kernels, widen(): pl.pallas_call(functools.partial(widen_body, heads), out_shape=(like, lik...  7.11 us
  transfers between devices with their start and end apart: 8, of which 0 were waited for; matrix products, arithmetic and copies ran while one was open for 0% of the time, Pallas kernels for 21%

profile of v3, /device:TPU:0, one launch (start us, length us, event | category | flops | bytes accessed | tf_op | source)
XLA Modules:
  0.0 172.8 jit_solution(3407282638759467945)
XLA Ops:
  0.6 48.1 %gather_and_project.1 = (bf16[4,512,384]{2,1,0:T(8,128)(2,1)}, bf16[4,512,384]{2,1,0:T(8,128)(2,1)}, bf16[4,512,384]{2,1,0:T(8,128)(2,1)}, bf16[4,512,384]{2,1,0...) custom-call(bf16[512,768]{1,0:T(8,128)(2,1)} %tokens.3, ...), custom_call_target="tpu_custom_call" | custom-call | tf_op jit(solution)/shard_map/gather_and_project/pallas_call | solution.py:671
  48.7 1.3 collective-permute-start.1
  50.0 2.6 %collective-permute-start.2 = (bf16[2,64,768]{2,1,0:T(8,128)(2,1)}, bf16[2,64,768]{2,1,0:T(8,128)(2,1)S(1)}, u32[]{:S(2)}, u32[]{:S(2)}) collective-permute-start(bf16[2,64,768]{2,1,0:T(8,128)(2,1)} %get-tuple-element.65), channel_id=1, source_target_pairs={{0,16},{4,20},{8,24},{12,28},{16,0},{20,4},{24,8},{28,12},{1,17},{... | collective-permute-start | bytes 589832 | tf_op jit(solution)/shard_map/ppermute | solution.py:1209
  52.6 1.4 collective-permute-start.3
  54.0 1.5 collective-permute-start
  55.5 0.0 copy-start.1
  55.5 0.0 copy-start
  55.5 18.8 %attention_forward.1 = (bf16[4,512,384]{2,1,0:T(8,128)(2,1)}, bf16[4,512,384]{2,1,0:T(8,128)(2,1)}, bf16[4,512,256]{2,1,0:T(8,128)(2,1)}) custom-call(s32[80]{0:T(128)} %len_ref.3, s32[80]{0:T(128)} %group_ref.3, bf16[4,512,384]{2,1,0:T(8,128)(2,1)} %get-tuple-element.56.qa, bf16[4,512,384]{2,1,0:T(8,128)(2,1)} %get-tuple-element.57.ka, ...), custom_call_target="tpu_custom_call" | custom-call | flops 8000000000 | bytes 30000000 | tf_op jit(solution)/shard_map/attention_forward/pallas_call | solution.py:233
  74.3 0.0 collective-permute-done.1
  74.3 0.0 collective-permute-done.2
  74.3 0.0 collective-permute-done.3
  74.4 0.0 copy-done.1
  74.4 0.1 fusion.5
  74.5 0.0 collective-permute-done
  74.5 0.0 copy-done
  74.5 0.2 fusion.3
  74.7 1.7 collective-permute-start.7
  76.4 0.2 collective-permute-start.4
  76.6 0.0 collective-permute-start.5
  76.7 3.6 %collective-permute-start.6 = (bf16[128,768]{1,0:T(8,128)(2,1)S(1)}, bf16[128,768]{1,0:T(8,128)(2,1)S(1)}, u32[]{:S(2)}, u32[]{:S(2)}) collective-permute-start(bf16[128,768]{1,0:T(8,128)(2,1)S(1)} %get-tuple-element.80), channel_id=1, source_target_pairs={{0,24},{4,28},{8,0},{12,4},{16,8},{20,12},{24,16},{28,20},{1,25},{... | collective-permute-start | bytes 589832 | tf_op jit(solution)/shard_map/ppermute | solution.py:1209
  80.2 16.8 %attention_backward.1 = (bf16[4,512,640]{2,1,0:T(8,128)(2,1)}, f32[8,384]{1,0:T(8,128)}) custom-call(s32[80]{0:T(128)} %len_ref.3, s32[80]{0:T(128)} %group_ref.3, bf16[4,512,384]{2,1,0:T(8,128)(2,1)} %get-tuple-element.67.qb, bf16[4,512,384]{2,1,0:T(8,128)(2,1)} %get-tuple-element.57.ka, bf16[4,512,384]{2,1,0:T(8,128)(2,1)} %get-tuple-element.58.va, ...), custom_call_target="tpu_custom_call" | custom-call | flops 16000000000 | bytes 30000000 | tf_op jit(solution)/shard_map/attention_backward/pallas_call | solution.py:410
  97.0 0.0 collective-permute-done.7
  97.0 0.7 add_convert_fusion.5.own_hi
  97.7 0.0 collective-permute-done.4
  97.7 0.0 collective-permute-done.5
  97.7 0.0 collective-permute-done.6
  97.7 0.8 add_convert_fusion.own_lo
  98.5 67.0 %reduce_gradients.1 = (bf16[512,768]{1,0:T(8,128)(2,1)}, bf16[512,768]{1,0:T(8,128)(2,1)}, bf16[4,2,192,768]{3,2,1,0:T(8,128)(2,1)}, bf16[2,4,192,384]{3,2,1,0:T(8,128)(2,1)}, f32[8,768]{1,0:T(8,128)}) custom-call(bf16[4,512,640]{2,1,0:T(8,128)(2,1)} %get-tuple-element.71.d_qkv_hbm, bf16[4,512,768]{2,1,0:T(8,128)(2,1)} %get-tuple-element.72.nall_hbm, ...), custom_call_target="tpu_custom_call" | custom-call | tf_op jit(solution)/shard_map/reduce_gradients/pallas_call | solution.py:1055
  165.5 7.1 %widen_gradients.1 = (bf16[512,768]{1,0:T(8,128)(2,1)}, bf16[512,768]{1,0:T(8,128)(2,1)}, f32[576,768]{1,0:T(8,128)}, f32[192,768]{1,0:T(8,128)}, f32[768,768]{1...) custom-call(bf16[8,192,768]{2,1,0:T(8,128)(2,1)} %bitcast.17, ...), custom_call_target="tpu_custom_call" | custom-call | tf_op jit(solution)/shard_map/widen_gradients/pallas_call | solution.py:1165
Async XLA Ops:
  48.7 25.6 %collective-permute-start.1 = (bf16[2,64,768]{2,1,0:T(8,128)(2,1)}, bf16[2,64,768]{2,1,0:T(8,128)(2,1)S(1)}, u32[]{:S(2)}, u32[]{:S(2)}) collective-permute-start(bf16[2,64,768]{2,1,0:T(8,128)(2,1)} %get-tuple-element.64), channel_id=1, source_target_pairs={{0,8},{4,12},{8,16},{12,20},{16,24},{20,28},{24,0},{28,4},{1,9},{5... | collective-permute-start | bytes 589832 | tf_op jit(solution)/shard_map/ppermute | solution.py:1209
  50.0 24.3 %collective-permute-start.2 = (bf16[2,64,768]{2,1,0:T(8,128)(2,1)}, bf16[2,64,768]{2,1,0:T(8,128)(2,1)S(1)}, u32[]{:S(2)}, u32[]{:S(2)}) collective-permute-start(bf16[2,64,768]{2,1,0:T(8,128)(2,1)} %get-tuple-element.65), channel_id=1, source_target_pairs={{0,16},{4,20},{8,24},{12,28},{16,0},{20,4},{24,8},{28,12},{1,17},{... | collective-permute-start | bytes 589832 | tf_op jit(solution)/shard_map/ppermute | solution.py:1209
  52.6 21.7 %collective-permute-start.3 = (bf16[2,64,768]{2,1,0:T(8,128)(2,1)}, bf16[2,64,768]{2,1,0:T(8,128)(2,1)S(1)}, u32[]{:S(2)}, u32[]{:S(2)}) collective-permute-start(bf16[2,64,768]{2,1,0:T(8,128)(2,1)} %get-tuple-element.66), channel_id=1, source_target_pairs={{0,24},{4,28},{8,0},{12,4},{16,8},{20,12},{24,16},{28,20},{1,25},{... | collective-permute-start | bytes 589832 | tf_op jit(solution)/shard_map/ppermute | solution.py:1209
  54.0 20.5 %collective-permute-start = (bf16[4,128,768]{2,1,0:T(8,128)(2,1)}, bf16[4,128,768]{2,1,0:T(8,128)(2,1)S(1)}, u32[]{:S(2)}, u32[]{:S(2)}) collective-permute-start(bf16[4,128,768]{2,1,0:T(8,128)(2,1)} %get-tuple-element.62), channel_id=1, source_target_pairs={{0,4},{4,0},{8,12},{12,8},{16,20},{20,16},{24,28},{28,24},{1,5},{5... | collective-permute-start | bytes 2359304 | tf_op jit(solution)/shard_map/ppermute | solution.py:1205
  55.5 18.9 %copy-start.1 = (bf16[2,64,768]{2,1,0:T(8,128)(2,1)S(1)}, bf16[2,64,768]{2,1,0:T(8,128)(2,1)}, u32[]{:S(2)}) copy-start(bf16[2,64,768]{2,1,0:T(8,128)(2,1)} %get-tuple-element.63) | copy-start | bytes 589828
  55.5 19.0 %copy-start = (bf16[4,128,768]{2,1,0:T(8,128)(2,1)S(1)}, bf16[4,128,768]{2,1,0:T(8,128)(2,1)}, u32[]{:S(2)}) copy-start(bf16[4,128,768]{2,1,0:T(8,128)(2,1)} %get-tuple-element.61) | copy-start | bytes 2359300
  74.7 22.4 %collective-permute-start.7 = (bf16[64,768]{1,0:T(8,128)(2,1)S(1)}, bf16[64,768]{1,0:T(8,128)(2,1)S(1)}, u32[]{:S(2)}, u32[]{:S(2)}) collective-permute-start(bf16[64,768]{1,0:T(8,128)(2,1)S(1)} %get-tuple-element.82), channel_id=1, source_target_pairs={{0,4},{4,0},{8,12},{12,8},{16,20},{20,16},{24,28},{28,24},{1,5},{5... | collective-permute-start | bytes 294920 | tf_op jit(solution)/shard_map/ppermute | solution.py:1205
  76.4 21.3 %collective-permute-start.4 = (bf16[128,768]{1,0:T(8,128)(2,1)S(1)}, bf16[128,768]{1,0:T(8,128)(2,1)S(1)}, u32[]{:S(2)}, u32[]{:S(2)}) collective-permute-start(bf16[128,768]{1,0:T(8,128)(2,1)S(1)} %get-tuple-element.78), channel_id=1, source_target_pairs={{0,8},{4,12},{8,16},{12,20},{16,24},{20,28},{24,0},{28,4},{1,9},{5... | collective-permute-start | bytes 589832 | tf_op jit(solution)/shard_map/ppermute | solution.py:1209
  76.6 21.1 %collective-permute-start.5 = (bf16[128,768]{1,0:T(8,128)(2,1)S(1)}, bf16[128,768]{1,0:T(8,128)(2,1)S(1)}, u32[]{:S(2)}, u32[]{:S(2)}) collective-permute-start(bf16[128,768]{1,0:T(8,128)(2,1)S(1)} %get-tuple-element.79), channel_id=1, source_target_pairs={{0,16},{4,20},{8,24},{12,28},{16,0},{20,4},{24,8},{28,12},{1,17},{... | collective-permute-start | bytes 589832 | tf_op jit(solution)/shard_map/ppermute | solution.py:1209
  76.7 21.1 %collective-permute-start.6 = (bf16[128,768]{1,0:T(8,128)(2,1)S(1)}, bf16[128,768]{1,0:T(8,128)(2,1)S(1)}, u32[]{:S(2)}, u32[]{:S(2)}) collective-permute-start(bf16[128,768]{1,0:T(8,128)(2,1)S(1)} %get-tuple-element.80), channel_id=1, source_target_pairs={{0,24},{4,28},{8,0},{12,4},{16,8},{20,12},{24,16},{28,20},{1,25},{... | collective-permute-start | bytes 589832 | tf_op jit(solution)/shard_map/ppermute | solution.py:1209

commit v4 on v3

--- a/solution.py
+++ b/solution.py
@@ -101,15 +101,43 @@
     ref[where] = jnp.where(mask, value.astype(ref.dtype), old).reshape(strips, win, width)
 
 
-def for_segments(len_ref, group_ref, seg, strips, tok_dev, small, middle, large):
+PIECES = 4
+
+
+def pieces_of(pairs, sem, tok_dev):
+    rows = tok_dev // PIECES
+    return [
+        [
+            pltpu.make_async_copy(a.at[:, pl.ds(p * rows, rows)], b.at[:, pl.ds(p * rows, rows)], sem.at[i, p])
+            for i, (a, b) in enumerate(pairs)
+        ]
+        for p in range(PIECES)
+    ]
+
+
+def for_segments(len_ref, group_ref, seg, strips, tok_dev, loads, later, stores, small, middle, large):
+    for piece in loads:
+        for copy in piece:
+            copy.start()
+    for copy in later:
+        copy.start()
     count = find_segments(len_ref, group_ref, seg, strips, tok_dev)
     big = middle_rows(tok_dev)
-
-    def segment(index, _):
+    rows = tok_dev // PIECES
+
+    def segment(index, ready):
         start, end = seg[0, index], seg[1, index]
         first = (start // ALIGN) * ALIGN
         windows = (end - first + WIN - 1) // WIN
         fits = end - first <= big
+        reach = jnp.where(windows == 1, first + WIN, jnp.where(fits, first + big, first + windows * WIN))
+        needed = jnp.minimum((reach + rows - 1) // rows, PIECES)
+        for p in range(PIECES):
+
+            @pl.when((p >= ready) & (p < needed))
+            def _():
+                for copy in loads[p]:
+                    copy.wait()
 
         @pl.when(windows == 1)
         def _():
@@ -124,9 +152,16 @@
         def _():
             large(start, end, first, windows)
 
-        return 0
-
-    lax.fori_loop(0, count, segment, 0)
+        for p, piece in enumerate(stores):
+
+            @pl.when((start < (p + 1) * rows) & ((p + 1) * rows <= end))
+            def _():
+                for copy in piece:
+                    copy.start()
+
+        return jnp.maximum(ready, needed)
+
+    lax.fori_loop(0, count, segment, jnp.int32(0))
 
 
 def middle_rows(tok_dev):
@@ -134,9 +169,12 @@
 
 
 def attn_fwd_body(
-    heads, len_ref, group_ref, qa, ka, va, do, qb, dob, ho, seg, acc,
+    heads, len_ref, group_ref, qa_hbm, ka_hbm, va_hbm, do_hbm, qb_hbm, dob_hbm, ho_hbm,
+    qa, ka, va, do, qb, dob, ho, seg, acc, in_sem, out_sem,
 ):
     strips, tok_dev = qa.shape[0], qa.shape[1]
+    loads = pieces_of([(qa_hbm, qa), (ka_hbm, ka), (va_hbm, va), (do_hbm, do)], in_sem, tok_dev)
+    stores = pieces_of([(qb, qb_hbm), (dob, dob_hbm), (ho, ho_hbm)], out_sem, tok_dev)
     zero = jnp.zeros((), BF16)
     big = middle_rows(tok_dev)
 
@@ -222,7 +260,10 @@
 
         lax.fori_loop(0, windows, q_window, 0)
 
-    for_segments(len_ref, group_ref, seg, strips, tok_dev, small, middle, large)
+    for_segments(len_ref, group_ref, seg, strips, tok_dev, loads, [], stores, small, middle, large)
+    for piece in stores:
+        for copy in piece:
+            copy.wait()
 
 
 def attn_fwd(image_len, image_group, qa, ka, va, do):
@@ -233,11 +274,14 @@
     return pl.pallas_call(
         functools.partial(attn_fwd_body, heads),
         out_shape=(like, like, jax.ShapeDtypeStruct((strips, tok_dev, packed), BF16)),
-        in_specs=[SMEM, SMEM] + [VMEM] * 4,
-        out_specs=(VMEM,) * 3,
-        scratch_shapes=[
+        in_specs=[SMEM, SMEM] + [ANY] * 4,
+        out_specs=(ANY,) * 3,
+        scratch_shapes=[pltpu.VMEM(qa.shape, BF16)] * 6 + [
+            pltpu.VMEM((strips, tok_dev, packed), BF16),
             pltpu.SMEM((2, image_len.shape[0] + 1), jnp.int32),
             pltpu.VMEM((heads, strips * middle_rows(tok_dev), LANES), F32),
+            pltpu.SemaphoreType.DMA((4, PIECES)),
+            pltpu.SemaphoreType.DMA((3, PIECES)),
         ],
         compiler_params=pltpu.CompilerParams(vmem_limit_bytes=60 << 20),
         cost_estimate=pl.CostEstimate(flops=8 * 10**9, bytes_accessed=30 * 10**6, transcendentals=8 * 10**6),
@@ -246,13 +290,13 @@
 
 
 def attn_bwd_body(
-    heads, len_ref, group_ref, qb, ka, va, dob, u_hbm, r_hbm, q_gain, k_gain,
-    d_qkv, gain_grad, seg, k_turned, dq_turned, dk_acc, dv_acc, dq, dk, dv, u_rows, r_rows, sems,
+    heads, len_ref, group_ref, qb_hbm, ka_hbm, va_hbm, dob_hbm, u_hbm, r_hbm, q_gain, k_gain,
+    d_qkv_hbm, gain_grad, seg, k_turned, dq_turned, dk_acc, dv_acc, dq, dk, dv, qb, ka, va, dob, u_rows, r_rows, d_qkv,
+    in_sem, out_sem, sems,
 ):
     strips, tok_dev = qb.shape[0], qb.shape[1]
+    pieces = pieces_of([(qb_hbm, qb), (ka_hbm, ka), (va_hbm, va), (dob_hbm, dob)], in_sem, tok_dev)
     loads = [pltpu.make_async_copy(u_hbm, u_rows, sems.at[0]), pltpu.make_async_copy(r_hbm, r_rows, sems.at[1])]
-    for load in loads:
-        load.start()
     zero = jnp.zeros((), BF16)
     big = middle_rows(tok_dev)
 
@@ -357,7 +401,7 @@
 
         lax.fori_loop(0, windows, q_out, 0)
 
-    for_segments(len_ref, group_ref, seg, strips, tok_dev, small, middle, large)
+    for_segments(len_ref, group_ref, seg, strips, tok_dev, pieces, loads, [], small, middle, large)
 
     rows = strips * WIN
     left = left_half(rows)
@@ -365,6 +409,10 @@
     gains = pair_row(q_gain, k_gain, heads)
     for load in loads:
         load.wait()
+
+    def save(i):
+        where = pl.ds(pl.multiple_of(i * WIN, WIN), WIN)
+        return pltpu.make_async_copy(d_qkv.at[:, where], d_qkv_hbm.at[:, where], out_sem.at[i])
 
     def chunk(i, totals):
         at = pl.multiple_of(i * WIN, WIN)
@@ -391,12 +439,19 @@
             parts.append(jnp.where(left, values[2 * b], pltpu.roll(values[2 * b + 1], DH, 1)))
         for b, part in enumerate(parts):
             d_qkv[:, pl.ds(at, WIN), b * LANES : (b + 1) * LANES] = part.astype(BF16).reshape(strips, WIN, LANES)
+        save(i).start()
         return tuple(new_totals)
 
     totals = lax.fori_loop(0, tok_dev // WIN, chunk, tuple(jnp.zeros((1, LANES), F32) for _ in range(heads)))
     gain_grad[...] = jnp.zeros_like(gain_grad)
     for h in range(heads):
         gain_grad[0:1, h * LANES : (h + 1) * LANES] = totals[h]
+
+    def saved(i, _):
+        save(i).wait()
+        return 0
+
+    lax.fori_loop(0, tok_dev // WIN, saved, 0)
 
 
 def attn_bwd(image_len, image_group, qb, ka, va, dob, u, r, q_gain, k_gain):
@@ -413,8 +468,8 @@
             jax.ShapeDtypeStruct((strips, tok_dev, blocks * LANES), BF16),
             jax.ShapeDtypeStruct((8, width), F32),
         ),
-        in_specs=[SMEM, SMEM] + [VMEM] * 4 + [ANY] * 2 + [VMEM] * 2,
-        out_specs=(VMEM, VMEM),
+        in_specs=[SMEM, SMEM] + [ANY] * 6 + [VMEM] * 2,
+        out_specs=(ANY, VMEM),
         scratch_shapes=[
             pltpu.SMEM((2, image_len.shape[0] + 1), jnp.int32),
             pltpu.VMEM((heads, DH, big), BF16),
@@ -422,8 +477,10 @@
             pltpu.VMEM((heads, big, LANES), F32),
             pltpu.VMEM((heads, big, LANES), F32),
             full, full, full,
-            pltpu.VMEM(u.shape, BF16),
-            pltpu.VMEM(r.shape, BF16),
+        ] + [pltpu.VMEM(qb.shape, BF16)] * 6 + [
+            pltpu.VMEM((strips, tok_dev, blocks * LANES), BF16),
+            pltpu.SemaphoreType.DMA((4, PIECES)),
+            pltpu.SemaphoreType.DMA((tok_dev // WIN,)),
             pltpu.SemaphoreType.DMA((2,)),
         ],
         compiler_params=pltpu.CompilerParams(vmem_limit_bytes=60 << 20),
@@ -432,16 +489,12 @@
     )(image_len, image_group, qb, ka, va, dob, u, r, q_gain, k_gain)
 
 
-CHUNKS = 4
-
-
-def by_kind(weight_t, heads, rows):
-    parts = [weight_t[3 * h * DH : (3 * h + 2) * DH, :] for h in range(heads)]
-    parts += [weight_t[(3 * h + 2) * DH : (3 * h + 3) * DH, :] for h in range(heads)]
-    spare = rows - weight_t.shape[0]
-    if spare:
-        parts.append(jnp.zeros((spare, weight_t.shape[1]), BF16))
-    return jnp.concatenate(parts, axis=0)
+CHUNKS = 8
+BACK_CHUNKS = 4
+
+
+def kind_order(heads):
+    return [3 * h + i for h in range(heads) for i in range(2)] + [3 * h + 2 for h in range(heads)]
 
 
 def remote(src, dst, send, recv, device):
@@ -455,12 +508,12 @@
 
 
 def front_body(
-    heads, n_hi, n_lo, tokens, cot, ln_gain, qkv_weight_t, q_gain, k_gain, attn_out, mlp_in, mlp_bias, mlp_out,
+    heads, n_hi, n_lo, tokens, cot, ln_gain, q_gain, k_gain, mlp_bias, qkv_hbm, attn_hbm, mlp_in_hbm, mlp_out_hbm,
     qa_out, ka_out, va_out, do_out, u_out, r_out, mlp_part_out, dn_part_out, nall_out, call_out,
     *rest,
 ):
-    (rows_out, both, wide, narrow, qkv_pad, mlp_out_t, mlp_in_t, attn_out_t, g_in, g_out,
-     send_sem, recv_sem, save_sem) = rest[-13:]
+    (rows_out, both, wide, narrow, qkv_rows, attn_pad, mlp_in, mlp_out, g_in, g_out,
+     send_sem, recv_sem, save_sem, load_sem) = rest[-14:]
     lo_first, hi_first = rest[:n_lo], rest[n_lo : n_lo + n_hi]
     batch, me = lax.axis_index("batch"), lax.axis_index("tensor")
     sibling = me + 1 - 2 * (me % 2)
@@ -468,7 +521,6 @@
     chip, far_chip = me // 2, 1 - me // 2
     tok_dev = tokens.shape[0]
     step = tok_dev // CHUNKS
-    rows = 2 * step
     features = tokens.shape[1]
     heads_wide = heads * LANES
 
@@ -482,11 +534,19 @@
     barrier = pltpu.get_barrier_semaphore()
     for other in (sibling, across):
         pl.semaphore_signal(barrier, inc=1, device_id=(batch, other), device_id_type=pl.DeviceIdType.MESH)
+    loads = [(mlp_in_hbm, mlp_in), (mlp_out_hbm, mlp_out)]
+    loads += [
+        (qkv_hbm.at[pl.ds(to * DH, DH)], qkv_rows.at[pl.ds(i * DH, DH)]) for i, to in enumerate(kind_order(heads))
+    ]
+    loads += [(attn_hbm.at[pl.ds(h * DH, DH)], attn_pad.at[pl.ds(h * LANES, DH)]) for h in range(heads)]
+    loads = [pltpu.make_async_copy(a, b, load_sem.at[i]) for i, (a, b) in enumerate(loads)]
+    for load in loads:
+        load.start()
+    both[0, me] = cot[...]
     gain = row_of(ln_gain)
     gains = pair_row(q_gain, k_gain, heads)
 
     def norm_chunk(c):
-        both[0, me, rows_of(c)] = cot[rows_of(c)]
         x = tokens[rows_of(c)].astype(F32)
         centred = x - jnp.mean(x, axis=-1, keepdims=True)
         variance = jnp.mean(centred * centred, axis=-1, keepdims=True)
@@ -495,9 +555,16 @@
     norm_chunk(0)
     pl.semaphore_wait(barrier, 2)
 
-    def first_sends(c, _):
+    def send_across(c):
         for kind in range(2):
             move(kind, 1, c, me, across).start()
+
+    def first_sends(c, _):
+        @pl.when(c < 3)
+        def _():
+            send_across(c)
+
+        for kind in range(2):
             move(kind, 0, c, me, sibling).start()
 
         @pl.when(c + 1 < CHUNKS)
@@ -511,73 +578,54 @@
     g_in[...] = jnp.zeros_like(g_in)
     g_out[...] = jnp.zeros_like(g_out)
     rows_out[...] = jnp.zeros_like(rows_out)
-    total = jnp.zeros((1, features), F32)
-    for c in range(CHUNKS):
-        total += jnp.sum(cot[c * step : (c + 1) * step].astype(F32), axis=0, keepdims=True)
-    rows_out[1:2, :] = total
-    qkv_pad[...] = by_kind(qkv_weight_t, heads, qkv_pad.shape[1]).T
-    mlp_out_t[...] = mlp_out[...].T
-    mlp_in_t[...] = mlp_in[...].T
+    rows_out[1:2, :] = jnp.sum(cot[...].astype(F32), axis=0, keepdims=True)
+    filled = 3 * heads * DH
+    if filled < qkv_rows.shape[0]:
+        qkv_rows[filled:] = jnp.zeros((qkv_rows.shape[0] - filled, features), BF16)
     for h in range(heads):
-        part = attn_out[h * DH : (h + 1) * DH, :]
-        attn_out_t[:, h * LANES : (h + 1) * LANES] = jnp.concatenate([part, jnp.zeros_like(part)], axis=0).T
-
-    left = left_half(rows)
+        attn_pad[h * LANES + DH : (h + 1) * LANES, :] = jnp.zeros((DH, features), BF16)
+    for load in loads:
+        load.wait()
+
     sums = half_sums()
     bias = row_of(mlp_bias)
 
-    def saves(c, at_chip):
-        strips = pl.ds(2 * at_chip, 2)
-        where = rows_of(c)
-        index = at_chip * CHUNKS + c
+    def chunks_of(c, n):
+        return pl.ds(pl.multiple_of(c * step, step), n * step)
+
+    def saves(at_chip, c, n):
+        strips, where = pl.ds(2 * at_chip, 2), chunks_of(c, n)
+        first = at_chip * CHUNKS + c
         pairs = [(narrow.at[a, strips, where], ref.at[strips, where]) for a, ref in enumerate(
             (qa_out, ka_out, va_out, do_out, u_out, r_out))]
-        pairs += [(wide.at[a, strips, where], ref.at[strips, where]) for a, ref in enumerate(
-            (mlp_part_out, dn_part_out))]
+        pairs += [(wide.at[a, strips, where], ref.at[strips, where]) for a, ref in enumerate((mlp_part_out, dn_part_out))]
         pairs += [(both.at[1, strips, where], nall_out.at[strips, where]), (both.at[0, strips, where], call_out.at[strips, where])]
-        return [pltpu.make_async_copy(a, b, save_sem.at[n, index]) for n, (a, b) in enumerate(pairs)]
-
-    def unit(i, _):
-        far = i >= CHUNKS
-        c = i % CHUNKS
-        at_chip = jnp.where(far, far_chip, chip)
-
-        @pl.when(jnp.logical_not(far))
-        def _():
-            for kind in range(2):
-                move(kind, 0, c, sibling, sibling).wait_recv()
-
-        def pass_on(k):
-            for kind in range(2):
-                move(kind, 1, k, across, across).wait_recv()
-                move(kind, 2, k, across, sibling).start()
-
-        @pl.when(i == CHUNKS - 1)
-        def _():
-            pass_on(0)
-
-        @pl.when(i == CHUNKS)
-        def _():
-            pass_on(1)
-
-        @pl.when(i > CHUNKS + 1)
-        def _():
-            pass_on(c)
-
-        @pl.when(far)
-        def _():
-            for kind in range(2):
-                move(kind, 2, c, across + 1 - 2 * (across % 2), sibling).wait_recv()
-
-        strips = pl.ds(2 * at_chip, 2)
-        where = rows_of(c)
-        n = both[1, strips, where].reshape(rows, features)
+        return [pltpu.make_async_copy(a, b, save_sem.at[i, first]) for i, (a, b) in enumerate(pairs)]
+
+    def wait_sibling(c):
+        for kind in range(2):
+            move(kind, 0, c, sibling, sibling).wait_recv()
+
+    def pass_on(c):
+        for kind in range(2):
+            move(kind, 1, c, across, across).wait_recv()
+            move(kind, 2, c, across, sibling).start()
+
+    def wait_passed(c):
+        for kind in range(2):
+            move(kind, 2, c, across + 1 - 2 * (across % 2), sibling).wait_recv()
+
+    def unit(at_chip, c, n, between=None):
+        rows = 2 * n * step
+        left = left_half(rows)
+        strips, where = pl.ds(2 * at_chip, 2), chunks_of(c, n)
+        normed = both[1, strips, where].reshape(rows, features)
         d = both[0, strips, where].reshape(rows, features)
 
         def save(ref, a, h, value):
-            ref[a, strips, where, h * LANES : (h + 1) * LANES] = value.astype(BF16).reshape(2, step, LANES)
-
-        qkv = nn(n, qkv_pad[...])
+            ref[a, strips, where, h * LANES : (h + 1) * LANES] = value.astype(BF16).reshape(2, n * step, LANES)
+
+        qkv = nt(normed, qkv_rows[...])
 
         def block(b):
             return qkv[:, b * LANES : (b + 1) * LANES]
@@ -591,6 +639,10 @@
         means = stacked_means(pairs)
         centred = [pairs[h] - means[h] for h in range(heads)]
         variances = stacked_means([x * x for x in centred])
+        hidden = nn(normed, mlp_in[...]) + bias
+        d_act = nt(d, mlp_out[...])
+        if between:
+            between()
         for h in range(heads):
             rstd = lax.rsqrt(variances[h] + epsilon)
             u = centred[h] * rstd
@@ -601,24 +653,67 @@
             save(narrow, 2, h, jnp.where(left, pltpu.roll(value, DH, 1) if h % 2 else value, 1.0))
             save(narrow, 4, h, u)
             save(narrow, 5, h, rstd)
-        narrow[3, strips, where] = nn(d, attn_out_t[...]).astype(BF16).reshape(2, step, heads_wide)
-
-        hidden = nn(n, mlp_in[...]) + bias
+        narrow[3, strips, where] = nt(d, attn_pad[...]).astype(BF16).reshape(2, n * step, heads_wide)
         cdf = 0.5 + 0.5 * lax.erf(hidden * 0.7071067811865476)
         act = (hidden * cdf).astype(BF16)
         slope = cdf + hidden * (0.3989422804014327 * jnp.exp(hidden * hidden * -0.5))
-        wide[0, strips, where] = nn(act, mlp_out[...]).astype(BF16).reshape(2, step, features)
-        d_hidden = nn(d, mlp_out_t[...]) * slope
-        d_low = d_hidden.astype(BF16)
+        d_low = (d_act * slope).astype(BF16)
+        wide[0, strips, where] = nn(act, mlp_out[...]).astype(BF16).reshape(2, n * step, features)
+        d_normed = nt(d_low, mlp_in[...])
+        rows_out[2:3, :] += jnp.sum(d_normed * normed.astype(F32), axis=0, keepdims=True)
+        wide[1, strips, where] = d_normed.astype(BF16).reshape(2, n * step, features)
         rows_out[0:1, :] += jnp.sum(d_low.astype(F32), axis=0, keepdims=True)
-        wide[1, strips, where] = nn(d_low, mlp_in_t[...]).astype(BF16).reshape(2, step, features)
         g_out[...] += tn(act, d)
-        g_in[...] += tn(n, d_low)
-        for copy in saves(c, at_chip):
+        g_in[...] += tn(normed, d_low)
+        for copy in saves(at_chip, c, n):
             copy.start()
+
+    half, quarter = CHUNKS // 2, CHUNKS // 4
+    for c in range(half):
+        wait_sibling(c)
+    unit(chip, 0, half)
+
+    def middle(i, _):
+        send_across(3 + i)
+
+        @pl.when(i < 2)
+        def _():
+            for c in range(quarter):
+                wait_sibling(half + i * quarter + c)
+
+        @pl.when(i == 4)
+        def _():
+            pass_on(5)
+
+        @pl.when(i >= 2)
+        def _():
+            for c in range(quarter):
+                wait_passed((i - 2) * quarter + c)
+
+        def between():
+            @pl.when((i == 1) | (i == 2))
+            def _():
+                pass_on(2 * i - 2)
+                pass_on(2 * i - 1)
+
+            @pl.when(i == 3)
+            def _():
+                pass_on(4)
+
+        unit(
+            jnp.where(i < 2, chip, far_chip), jnp.where(i < 2, half + i * quarter, (i - 2) * quarter), quarter, between
+        )
         return 0
 
-    lax.fori_loop(0, 2 * CHUNKS, unit, 0)
+    lax.fori_loop(0, 5, middle, 0)
+
+    def last(i, _):
+        pass_on(6 + i)
+        wait_passed(6 + i)
+        unit(far_chip, 6 + i, 1)
+        return 0
+
+    lax.fori_loop(0, 2, last, 0)
 
     hi, lo = batch // n_lo, batch % n_lo
     for o in range(n_hi * n_lo):
@@ -637,17 +732,12 @@
                 def _():
                     part[m][place] = low
 
-    grown = g_in[...] * mlp_in[...].astype(F32)
-    grown_hi = grown.astype(BF16)
-    ones = jnp.ones((8, grown.shape[1]), BF16)
-    rows_out[2:3, :] = (nt(ones, grown_hi) + nt(ones, (grown - grown_hi.astype(F32)).astype(BF16)))[0:1]
-
-    def finish(i, _):
-        for copy in saves(i % CHUNKS, i // CHUNKS):
+    for at_chip, c, n in (
+        [(chip, 0, half), (chip, half, quarter), (chip, half + quarter, quarter)]
+        + [(far_chip, i * quarter, quarter) for i in range(3)] + [(far_chip, 6, 1), (far_chip, 7, 1)]
+    ):
+        for copy in saves(at_chip, c, n):
             copy.wait()
-        return 0
-
-    lax.fori_loop(0, 2 * CHUNKS, finish, 0)
 
     def sent(c, _):
         for kind in range(2):
@@ -659,7 +749,7 @@
     lax.fori_loop(0, CHUNKS, sent, 0)
 
 
-def front(strips, n_batch, tokens, cot, ln_gain, qkv_weight_t, q_gain, k_gain, attn_out, mlp_in, mlp_bias, mlp_out):
+def front(strips, n_batch, tokens, cot, ln_gain, q_gain, k_gain, mlp_bias, qkv_weight_t, attn_out, mlp_in, mlp_out):
     tok_dev, features = tokens.shape
     heads = q_gain.shape[0] // DH
     width = heads * LANES
@@ -675,25 +765,26 @@
         ) * n_lo + (
             jax.ShapeDtypeStruct((n_lo, (2 * features - lo_rows(features)) // n_batch, features), BF16),
         ) * n_hi + (jax.ShapeDtypeStruct((8, features), F32),),
-        in_specs=[VMEM] * 10,
+        in_specs=[VMEM] * 6 + [ANY] * 4,
         out_specs=(ANY,) * 10 + (VMEM,) * (n_lo + n_hi + 1),
         scratch_shapes=[
             pltpu.VMEM((2, strips, tok_dev, features), BF16),
             pltpu.VMEM((2, strips, tok_dev, features), BF16),
             pltpu.VMEM((6, strips, tok_dev, width), BF16),
-            pltpu.VMEM((features, blocks * LANES), BF16),
-            pltpu.VMEM((features, hidden), BF16),
-            pltpu.VMEM((hidden, features), BF16),
-            pltpu.VMEM((features, width), BF16),
+            pltpu.VMEM((blocks * LANES, features), BF16),
+            pltpu.VMEM((width, features), BF16),
+            pltpu.VMEM(mlp_in.shape, BF16),
+            pltpu.VMEM(mlp_out.shape, BF16),
             pltpu.VMEM((features, hidden), F32),
             pltpu.VMEM((hidden, features), F32),
             pltpu.SemaphoreType.DMA((2, 3, CHUNKS)),
             pltpu.SemaphoreType.DMA((2, 3, CHUNKS)),
             pltpu.SemaphoreType.DMA((10, 2 * CHUNKS)),
+            pltpu.SemaphoreType.DMA((2 + 4 * heads,)),
         ],
         compiler_params=pltpu.CompilerParams(collective_id=0, has_side_effects=True, vmem_limit_bytes=60 << 20),
         name="gather_and_project",
-    )(tokens, cot, ln_gain, qkv_weight_t, q_gain, k_gain, attn_out, mlp_in, mlp_bias, mlp_out)
+    )(tokens, cot, ln_gain, q_gain, k_gain, mlp_bias, qkv_weight_t, attn_out, mlp_in, mlp_out)
 
 
 def back_body(
@@ -710,7 +801,7 @@
     across = (me + 2) % 4
     far_sibling = (sibling + 2) % 4
     tok_dev, features = tokens.shape
-    step = tok_dev // CHUNKS
+    step = tok_dev // BACK_CHUNKS
     chunk_rows, half_cols = joint.shape[2], joint.shape[3]
     every_k, every_m = range(1, n_hi), range(1, n_lo)
     cut = chunk_rows // 2 // 16 * 16
@@ -781,7 +872,11 @@
         mlp_lo(m, 0).start()
     mlp_send_hop(1)
 
-    weight_t[...] = by_kind(qkv_weight_t, heads, weight_t.shape[0])
+    for i, place in enumerate(kind_order(heads)):
+        weight_t[i * DH : (i + 1) * DH] = qkv_weight_t[place * DH : (place + 1) * DH]
+    filled = qkv_weight_t.shape[0]
+    if filled < weight_t.shape[0]:
+        weight_t[filled:] = jnp.zeros((weight_t.shape[0] - filled, features), BF16)
     head_width = attn_out.shape[0]
     attn_pad[:head_width] = attn_out[...]
     attn_pad[head_width:] = jnp.zeros((attn_pad.shape[0] - head_width, features), BF16)
@@ -905,8 +1000,8 @@
             x_move(which, c).start()
             return 0
 
-        lax.fori_loop(0, CHUNKS, give, 0)
-        lax.fori_loop(0, CHUNKS, send, 0)
+        lax.fori_loop(0, BACK_CHUNKS, give, 0)
+        lax.fori_loop(0, BACK_CHUNKS, send, 0)
 
     def close(which):
         def give(c, _):
@@ -920,8 +1015,8 @@
             near[which, rows_of(c)] = mine + core_got[which, 1, rows_of(c)].astype(F32)
             return 0
 
-        lax.fori_loop(0, CHUNKS, give, 0)
-        lax.fori_loop(0, CHUNKS, keep, 0)
+        lax.fori_loop(0, BACK_CHUNKS, give, 0)
+        lax.fori_loop(0, BACK_CHUNKS, keep, 0)
 
     for load in loads[4:]:
         load.wait()
@@ -981,7 +1076,7 @@
         input_grad[where] = (cot[where].astype(F32) + d_x).astype(BF16)
         return 0
 
-    lax.fori_loop(0, CHUNKS, last_rows, 0)
+    lax.fori_loop(0, BACK_CHUNKS, last_rows, 0)
     joint_pass(1)
     bias = row_of(out_bias)
 
@@ -991,7 +1086,7 @@
         output[where] = (tokens[where].astype(F32) + near[1, where] + x_got[1, where].astype(F32) + bias).astype(BF16)
         return 0
 
-    lax.fori_loop(0, CHUNKS, out_rows, 0)
+    lax.fori_loop(0, BACK_CHUNKS, out_rows, 0)
     vec_pair_move(1, across).wait_recv()
     rows_out[...] = vec[0]
     rows_out[1:3, :] = vec[1, 1:3, :] + vec_pair[1, 1:3, :]
@@ -1024,7 +1119,7 @@
             x_move(which, c).wait_send()
         return 0
 
-    lax.fori_loop(0, CHUNKS, sent, 0)
+    lax.fori_loop(0, BACK_CHUNKS, sent, 0)
     for m in every_m:
         for p in range(2):
             all_lo(p, m, -m).wait_recv()
@@ -1093,8 +1188,8 @@
             dma((n_hi, 2)), dma((n_hi, 2)),
             dma((n_hi, 2)), dma((n_hi, 2)),
             dma((n_lo, 2)), dma((n_lo, 2)),
-            dma((2, 2, CHUNKS)), dma((2, 2, CHUNKS)),
-            dma((2, CHUNKS)), dma((2, CHUNKS)),
+            dma((2, 2, BACK_CHUNKS)), dma((2, 2, BACK_CHUNKS)),
+            dma((2, BACK_CHUNKS)), dma((2, BACK_CHUNKS)),
             dma((n_lo + n_hi + 2,)), dma((n_lo + n_hi + 2,)),
             dma((2,)),
         ],
@@ -1109,7 +1204,7 @@
 def widen_body(
     heads, mlp_hbm, joint_hbm, output_in, input_grad_in, rows,
     output, input_grad, qkv_out, attn_out, mlp_in_out, mlp_out_out, ln_gain, q_gain, k_gain, mlp_bias, out_bias,
-    mlp_all, joint_all, joint, qkv_t, attn, mlp, sems,
+    kept, mlp_all, joint_all, joint, qkv_t, attn, mlp, sems,
 ):
     def copy(i, source, to):
         made = pltpu.make_async_copy(source, to, sems.at[i])
@@ -1118,6 +1213,7 @@
 
     load_joint = copy(0, joint_hbm, joint_all)
     load_mlp = copy(1, mlp_hbm, mlp_all)
+    load_rows = [copy(2, output_in, kept.at[0]), copy(3, input_grad_in, kept.at[1])]
     features = rows.shape[1]
     mlp_bias[...] = rows[0:1, :].reshape(features)
     out_bias[...] = rows[1:2, :].reshape(features)
@@ -1125,31 +1221,36 @@
     for offset, ref in ((0, q_gain), (DH, k_gain)):
         parts = [rows[3:4, h * LANES + offset : h * LANES + offset + DH] for h in range(heads)]
         ref[...] = jnp.concatenate(parts, axis=1).reshape(heads * DH)
-    output[...] = output_in[...]
-    input_grad[...] = input_grad_in[...]
     load_joint.wait()
     n_lo, n_hi, chunk_rows, cols = joint_all.shape
     width = qkv_t.shape[0]
     per_half = features // chunk_rows
     for o in range(n_lo * n_hi):
         row = o % per_half * chunk_rows
-        joint[o // per_half, row : row + chunk_rows] = joint_all[o % n_lo, o // n_lo].astype(F32)
-    kinds = [(3 * h + i) * DH for h in range(heads) for i in range(2)] + [(3 * h + 2) * DH for h in range(heads)]
+        joint[o // per_half, row : row + chunk_rows] = joint_all[o % n_lo, o // n_lo]
+    pending = []
     for half in range(2):
         at = slice(half * cols, (half + 1) * cols)
-        for i, to in enumerate(kinds):
-            qkv_t[to : to + DH, at] = joint[half, i * DH : (i + 1) * DH]
-        attn[:, at] = joint[half, width:]
-    pending = [copy(4, qkv_t, qkv_out), copy(5, attn, attn_out)]
+        attn[:, at] = joint[half, width:].astype(F32)
+        for i, place in enumerate(kind_order(heads)):
+            qkv_t[place * DH : (place + 1) * DH, at] = joint[half, i * DH : (i + 1) * DH].astype(F32)
+    pending += [copy(4, qkv_t, qkv_out), copy(5, attn, attn_out)]
     load_mlp.wait()
     chunks = mlp_all.shape[0]
     cut = lo_rows(features) // chunks
     rest = mlp_all.shape[1] - cut
+    for o in range(features // cut):
+        mlp[o * cut : (o + 1) * cut] = mlp_all[o, :cut].astype(F32)
+    pending.append(copy(6, mlp.at[pl.ds(0, features)], mlp_in_out))
+    for o in range(features // cut, chunks):
+        mlp[o * cut : (o + 1) * cut] = mlp_all[o, :cut].astype(F32)
     for o in range(chunks):
-        mlp[o * cut : (o + 1) * cut] = mlp_all[o, :cut].astype(F32)
         row = lo_rows(features) + o * rest
         mlp[row : row + rest] = mlp_all[o, cut:].astype(F32)
-    pending += [copy(6, mlp.at[:features], mlp_in_out), copy(7, mlp.at[features:], mlp_out_out)]
+    pending.append(copy(7, mlp.at[pl.ds(features, features)], mlp_out_out))
+    for i, (load, to) in enumerate(zip(load_rows, (output, input_grad))):
+        load.wait()
+        pending.append(copy(8 + i, kept.at[i], to))
     for made in pending:
         made.wait()
 
@@ -1168,16 +1269,17 @@
             like, like, out(width, features), out(head_width, features), out(features, features), out(features, features),
             out(features), out(head_width), out(head_width), out(features), out(features),
         ),
-        in_specs=[ANY] * 2 + [VMEM] * 3,
-        out_specs=(VMEM,) * 2 + (ANY,) * 4 + (VMEM,) * 5,
+        in_specs=[ANY] * 4 + [VMEM],
+        out_specs=(ANY,) * 6 + (VMEM,) * 5,
         scratch_shapes=[
+            pltpu.VMEM((2,) + output.shape, BF16),
             pltpu.VMEM(mlp_all.shape, BF16),
             pltpu.VMEM(joint_all.shape, BF16),
-            pltpu.VMEM((2, features, features // 2), F32),
+            pltpu.VMEM((2, features, features // 2), BF16),
             pltpu.VMEM((width, features), F32),
             pltpu.VMEM((head_width, features), F32),
             pltpu.VMEM((2 * features, features), F32),
-            pltpu.SemaphoreType.DMA((8,)),
+            pltpu.SemaphoreType.DMA((10,)),
         ],
         compiler_params=pltpu.CompilerParams(vmem_limit_bytes=60 << 20),
         name="widen_gradients",
@@ -1197,7 +1299,7 @@
 
     weight_t = qkv_weight.T
     (qa, ka, va, do, u, r, mlp_part, dn_part, nall, call, *mlp_grad, front_rows) = front(
-        strips, n_batch, tokens, out_cotangent, ln_gain, weight_t, q_gain, k_gain, attn_out, mlp_in, mlp_bias, mlp_out
+        strips, n_batch, tokens, out_cotangent, ln_gain, q_gain, k_gain, mlp_bias, weight_t, attn_out, mlp_in, mlp_out
     )
 
     def along_lo(x, m):

time: 173 us -> 170 us (0.983)
  Pallas kernels: 158 us -> 153 us
    pallas_call x1, Pallas kernels: 18.8 us -> 16.4 us  [attn_fwd(): pl.pallas_call(functools.partial(attn_fwd_body, heads), out_shape=(like,...]
  transfers between devices with their start and end apart: 8 -> 8, of which waited for: 0 -> 1; matrix products, arithmetic and copies ran while one was open for 0% -> 0% of each run, Pallas kernels for 21% -> 19%
where the time goes in v4:
time: 170 us
  Pallas kernels  153 us (90%)
  starting transfers between devices  12.8 us (8%)
  other arithmetic  1.73 us (1%)
    pallas_call x1, Pallas kernels, back(): pl.pallas_call(functools.partial(back_body, heads, n_hi, n_lo), out_shape...  68 us
    pallas_call x1, Pallas kernels, front(): pl.pallas_call(functools.partial(front_body, heads, n_hi, n_lo), out_shap...  47.4 us
    pallas_call x1, Pallas kernels, attn_fwd(): pl.pallas_call(functools.partial(attn_fwd_body, heads), out_shape=(like,...  16.4 us
    pallas_call x1, Pallas kernels, attn_bwd(): pl.pallas_call(functools.partial(attn_bwd_body, heads), out_shape=(jax.Sh...  15.2 us
    ppermute x6, starting transfers between devices, along_hi(): return lax.ppermute(x, 'batch', pairs)  9.77 us
    pallas_call x1, Pallas kernels, widen(): pl.pallas_call(functools.partial(widen_body, heads), out_shape=(like, lik...  6.32 us
  transfers between devices with their start and end apart: 8, of which 1 were waited for; matrix products, arithmetic and copies ran while one was open for 0% of the time, Pallas kernels for 19%

profile of v4, /device:TPU:0, one launch (start us, length us, event | category | flops | bytes accessed | tf_op | source)
XLA Modules:
  0.0 170.0 jit_solution(13092709807995290098)
XLA Ops:
  0.6 47.4 %gather_and_project.1 = (bf16[4,512,384]{2,1,0:T(8,128)(2,1)}, bf16[4,512,384]{2,1,0:T(8,128)(2,1)}, bf16[4,512,384]{2,1,0:T(8,128)(2,1)}, bf16[4,512,384]{2,1,0...) custom-call(bf16[512,768]{1,0:T(8,128)(2,1)} %tokens.3, ...), custom_call_target="tpu_custom_call" | custom-call | tf_op jit(solution)/shard_map/gather_and_project/pallas_call | solution.py:761
  48.1 2.0 %collective-permute-start.1 = (bf16[2,64,768]{2,1,0:T(8,128)(2,1)}, bf16[2,64,768]{2,1,0:T(8,128)(2,1)S(1)}, u32[]{:S(2)}, u32[]{:S(2)}) collective-permute-start(bf16[2,64,768]{2,1,0:T(8,128)(2,1)} %get-tuple-element.64), channel_id=1, source_target_pairs={{0,8},{4,12},{8,16},{12,20},{16,24},{20,28},{24,0},{28,4},{1,9},{5... | collective-permute-start | bytes 589832 | tf_op jit(solution)/shard_map/ppermute | solution.py:1311
  50.1 2.6 %collective-permute-start.2 = (bf16[2,64,768]{2,1,0:T(8,128)(2,1)}, bf16[2,64,768]{2,1,0:T(8,128)(2,1)S(1)}, u32[]{:S(2)}, u32[]{:S(2)}) collective-permute-start(bf16[2,64,768]{2,1,0:T(8,128)(2,1)} %get-tuple-element.65), channel_id=1, source_target_pairs={{0,16},{4,20},{8,24},{12,28},{16,0},{20,4},{24,8},{28,12},{1,17},{... | collective-permute-start | bytes 589832 | tf_op jit(solution)/shard_map/ppermute | solution.py:1311
  52.7 1.4 collective-permute-start.3
  54.0 1.5 collective-permute-start
  55.6 0.0 copy-start.1
  55.6 0.0 copy-start
  55.6 16.4 %attention_forward.1 = (bf16[4,512,384]{2,1,0:T(8,128)(2,1)}, bf16[4,512,384]{2,1,0:T(8,128)(2,1)}, bf16[4,512,256]{2,1,0:T(8,128)(2,1)}) custom-call(s32[80]{0:T(128)} %len_ref.3, s32[80]{0:T(128)} %group_ref.3, bf16[4,512,384]{2,1,0:T(8,128)(2,1)} %get-tuple-element.56.qa_hbm, bf16[4,512,384]{2,1,0:T(8,128)(2,1)} %get-tuple-element.57.ka_hbm, ...), custom_call_target="tpu_custom_call" | custom-call | flops 8000000000 | bytes 30000000 | tf_op jit(solution)/shard_map/attention_forward/pallas_call | solution.py:274
  72.0 0.0 collective-permute-done.1
  72.0 0.0 collective-permute-done.2
  72.0 0.0 collective-permute-done.3
  72.1 0.0 copy-done.1
  72.1 0.1 fusion.5
  72.2 1.1 collective-permute-done
  73.3 0.0 copy-done
  73.3 0.2 fusion.3
  73.5 1.5 collective-permute-start.7
  75.0 0.7 collective-permute-start.4
  75.7 0.3 collective-permute-start.5
  76.0 2.8 %collective-permute-start.6 = (bf16[128,768]{1,0:T(8,128)(2,1)S(1)}, bf16[128,768]{1,0:T(8,128)(2,1)S(1)}, u32[]{:S(2)}, u32[]{:S(2)}) collective-permute-start(bf16[128,768]{1,0:T(8,128)(2,1)S(1)} %get-tuple-element.80), channel_id=1, source_target_pairs={{0,24},{4,28},{8,0},{12,4},{16,8},{20,12},{24,16},{28,20},{1,25},{... | collective-permute-start | bytes 589832 | tf_op jit(solution)/shard_map/ppermute | solution.py:1311
  78.8 15.2 %attention_backward.1 = (bf16[4,512,640]{2,1,0:T(8,128)(2,1)}, f32[8,384]{1,0:T(8,128)}) custom-call(s32[80]{0:T(128)} %len_ref.3, s32[80]{0:T(128)} %group_ref.3, bf16[4,512,384]{2,1,0:T(8,128)(2,1)} %get-tuple-element.67.qb_hbm, bf16[4,512,384]{2,1,0:T(8,128)(2,1)} %get-tuple-element.57.ka_hbm, bf16[4,512,384]{2,1,0:T(8,128)(2,1)} %get-tuple-element.58.va_hbm, ...), custom_call_target="tpu_custom_call" | custom-call | flops 16000000000 | bytes 30000000 | tf_op jit(solution)/shard_map/attention_backward/pallas_call | solution.py:465
  94.1 0.0 collective-permute-done.7
  94.1 0.7 add_convert_fusion.5.own_hi
  94.8 0.0 collective-permute-done.4
  94.8 0.0 collective-permute-done.5
  94.8 0.0 collective-permute-done.6
  94.8 0.8 add_convert_fusion.own_lo
  95.5 68.0 %reduce_gradients.1 = (bf16[512,768]{1,0:T(8,128)(2,1)}, bf16[512,768]{1,0:T(8,128)(2,1)}, bf16[4,2,192,768]{3,2,1,0:T(8,128)(2,1)}, bf16[2,4,192,384]{3,2,1,0:T(8,128)(2,1)}, f32[8,768]{1,0:T(8,128)}) custom-call(bf16[4,512,640]{2,1,0:T(8,128)(2,1)} %get-tuple-element.71.d_qkv_hbm, bf16[4,512,768]{2,1,0:T(8,128)(2,1)} %get-tuple-element.72.nall_hbm, ...), custom_call_target="tpu_custom_call" | custom-call | tf_op jit(solution)/shard_map/reduce_gradients/pallas_call | solution.py:1150
  163.5 6.3 %widen_gradients.1 = (bf16[512,768]{1,0:T(8,128)(2,1)}, bf16[512,768]{1,0:T(8,128)(2,1)}, f32[576,768]{1,0:T(8,128)}, f32[192,768]{1,0:T(8,128)}, f32[768,768]{1...) custom-call(bf16[8,192,768]{2,1,0:T(8,128)(2,1)} %bitcast.17, ...), custom_call_target="tpu_custom_call" | custom-call | tf_op jit(solution)/shard_map/widen_gradients/pallas_call | solution.py:1266
Async XLA Ops:
  48.1 23.9 %collective-permute-start.1 = (bf16[2,64,768]{2,1,0:T(8,128)(2,1)}, bf16[2,64,768]{2,1,0:T(8,128)(2,1)S(1)}, u32[]{:S(2)}, u32[]{:S(2)}) collective-permute-start(bf16[2,64,768]{2,1,0:T(8,128)(2,1)} %get-tuple-element.64), channel_id=1, source_target_pairs={{0,8},{4,12},{8,16},{12,20},{16,24},{20,28},{24,0},{28,4},{1,9},{5... | collective-permute-start | bytes 589832 | tf_op jit(solution)/shard_map/ppermute | solution.py:1311
  50.1 21.9 %collective-permute-start.2 = (bf16[2,64,768]{2,1,0:T(8,128)(2,1)}, bf16[2,64,768]{2,1,0:T(8,128)(2,1)S(1)}, u32[]{:S(2)}, u32[]{:S(2)}) collective-permute-start(bf16[2,64,768]{2,1,0:T(8,128)(2,1)} %get-tuple-element.65), channel_id=1, source_target_pairs={{0,16},{4,20},{8,24},{12,28},{16,0},{20,4},{24,8},{28,12},{1,17},{... | collective-permute-start | bytes 589832 | tf_op jit(solution)/shard_map/ppermute | solution.py:1311
  52.7 19.4 %collective-permute-start.3 = (bf16[2,64,768]{2,1,0:T(8,128)(2,1)}, bf16[2,64,768]{2,1,0:T(8,128)(2,1)S(1)}, u32[]{:S(2)}, u32[]{:S(2)}) collective-permute-start(bf16[2,64,768]{2,1,0:T(8,128)(2,1)} %get-tuple-element.66), channel_id=1, source_target_pairs={{0,24},{4,28},{8,0},{12,4},{16,8},{20,12},{24,16},{28,20},{1,25},{... | collective-permute-start | bytes 589832 | tf_op jit(solution)/shard_map/ppermute | solution.py:1311
  54.0 19.2 %collective-permute-start = (bf16[4,128,768]{2,1,0:T(8,128)(2,1)}, bf16[4,128,768]{2,1,0:T(8,128)(2,1)S(1)}, u32[]{:S(2)}, u32[]{:S(2)}) collective-permute-start(bf16[4,128,768]{2,1,0:T(8,128)(2,1)} %get-tuple-element.62), channel_id=1, source_target_pairs={{0,4},{4,0},{8,12},{12,8},{16,20},{20,16},{24,28},{28,24},{1,5},{5... | collective-permute-start | bytes 2359304 | tf_op jit(solution)/shard_map/ppermute | solution.py:1307
  55.6 16.5 %copy-start.1 = (bf16[2,64,768]{2,1,0:T(8,128)(2,1)S(1)}, bf16[2,64,768]{2,1,0:T(8,128)(2,1)}, u32[]{:S(2)}) copy-start(bf16[2,64,768]{2,1,0:T(8,128)(2,1)} %get-tuple-element.63) | copy-start | bytes 589828
  55.6 17.7 %copy-start = (bf16[4,128,768]{2,1,0:T(8,128)(2,1)S(1)}, bf16[4,128,768]{2,1,0:T(8,128)(2,1)}, u32[]{:S(2)}) copy-start(bf16[4,128,768]{2,1,0:T(8,128)(2,1)} %get-tuple-element.61) | copy-start | bytes 2359300
  73.5 20.6 %collective-permute-start.7 = (bf16[64,768]{1,0:T(8,128)(2,1)S(1)}, bf16[64,768]{1,0:T(8,128)(2,1)S(1)}, u32[]{:S(2)}, u32[]{:S(2)}) collective-permute-start(bf16[64,768]{1,0:T(8,128)(2,1)S(1)} %get-tuple-element.82), channel_id=1, source_target_pairs={{0,4},{4,0},{8,12},{12,8},{16,20},{20,16},{24,28},{28,24},{1,5},{5... | collective-permute-start | bytes 294920 | tf_op jit(solution)/shard_map/ppermute | solution.py:1307
  75.0 19.8 %collective-permute-start.4 = (bf16[128,768]{1,0:T(8,128)(2,1)S(1)}, bf16[128,768]{1,0:T(8,128)(2,1)S(1)}, u32[]{:S(2)}, u32[]{:S(2)}) collective-permute-start(bf16[128,768]{1,0:T(8,128)(2,1)S(1)} %get-tuple-element.78), channel_id=1, source_target_pairs={{0,8},{4,12},{8,16},{12,20},{16,24},{20,28},{24,0},{28,4},{1,9},{5... | collective-permute-start | bytes 589832 | tf_op jit(solution)/shard_map/ppermute | solution.py:1311
  75.7 19.0 %collective-permute-start.5 = (bf16[128,768]{1,0:T(8,128)(2,1)S(1)}, bf16[128,768]{1,0:T(8,128)(2,1)S(1)}, u32[]{:S(2)}, u32[]{:S(2)}) collective-permute-start(bf16[128,768]{1,0:T(8,128)(2,1)S(1)} %get-tuple-element.79), channel_id=1, source_target_pairs={{0,16},{4,20},{8,24},{12,28},{16,0},{20,4},{24,8},{28,12},{1,17},{... | collective-permute-start | bytes 589832 | tf_op jit(solution)/shard_map/ppermute | solution.py:1311
  76.0 18.7 %collective-permute-start.6 = (bf16[128,768]{1,0:T(8,128)(2,1)S(1)}, bf16[128,768]{1,0:T(8,128)(2,1)S(1)}, u32[]{:S(2)}, u32[]{:S(2)}) collective-permute-start(bf16[128,768]{1,0:T(8,128)(2,1)S(1)} %get-tuple-element.80), channel_id=1, source_target_pairs={{0,24},{4,28},{8,0},{12,4},{16,8},{20,12},{24,16},{28,20},{1,25},{... | collective-permute-start | bytes 589832 | tf_op jit(solution)/shard_map/ppermute | solution.py:1311

commit v5 on v4

--- a/solution.py
+++ b/solution.py
@@ -44,9 +44,9 @@
     return jnp.concatenate(parts, axis=1)
 
 
-def half_sums():
-    row = lax.broadcasted_iota(jnp.int32, (LANES, LANES), 0) // DH
-    col = lax.broadcasted_iota(jnp.int32, (LANES, LANES), 1) // DH
+def half_sums(lanes=LANES):
+    row = lax.broadcasted_iota(jnp.int32, (lanes, lanes), 0) // DH
+    col = lax.broadcasted_iota(jnp.int32, (lanes, lanes), 1) // DH
     return jnp.where(row == col, 1.0, 0.0).astype(BF16)
 
 
@@ -87,6 +87,10 @@
 def row_mask(low, high, strips, win=WIN, width=LANES):
     j = lax.broadcasted_iota(jnp.int32, (strips, win, width), 1).reshape(strips * win, width)
     return (j >= low) & (j < high)
+
+
+def low_mask(mask):
+    return jnp.where(mask, 1.0, 0.0).astype(BF16) > jnp.asarray(0.5, BF16)
 
 
 def tile(ref, at, h, win=WIN):
@@ -129,7 +133,7 @@
         start, end = seg[0, index], seg[1, index]
         first = (start // ALIGN) * ALIGN
         windows = (end - first + WIN - 1) // WIN
-        fits = end - first <= big
+        fits = (end - first <= big) & (end - start <= big - ALIGN)
         reach = jnp.where(windows == 1, first + WIN, jnp.where(fits, first + big, first + windows * WIN))
         needed = jnp.minimum((reach + rows - 1) // rows, PIECES)
         for p in range(PIECES):
@@ -162,6 +166,25 @@
         return jnp.maximum(ready, needed)
 
     lax.fori_loop(0, count, segment, jnp.int32(0))
+
+
+def edge_tile(ref, at, h, low):
+    strips = ref.shape[0]
+    cols = slice(h * LANES, (h + 1) * LANES)
+    last = middle_rows(ref.shape[1]) - ALIGN
+    body = ref[:, pl.ds(at + last - WIN + ALIGN, WIN - ALIGN), cols]
+    late = low_mask(row_mask(low, ALIGN, strips, ALIGN))
+    edge = jnp.where(late, tile(ref, at, h, ALIGN), tile(ref, at + last, h, ALIGN))
+    return jnp.concatenate([body, edge.reshape(strips, ALIGN, LANES)], axis=1).reshape(strips * WIN, LANES)
+
+
+def edge_mask(low, high, strips, tok_dev):
+    last = middle_rows(tok_dev) - ALIGN
+    j = lax.broadcasted_iota(jnp.int32, (strips, WIN, LANES), 1).reshape(strips * WIN, LANES)
+    edge = j - (WIN - ALIGN)
+    body = j + (last - WIN + ALIGN)
+    inner = (edge < 0) & (body >= low) & (body < high)
+    return inner | ((edge >= 0) & ((edge >= low) | (edge < high - last)))
 
 
 def middle_rows(tok_dev):
@@ -180,22 +203,23 @@
 
     def finish(at, low, high, totals, win=WIN):
         rows = strips * win
-        mask = row_mask(low, high, strips, win)
+        mask = low_mask(row_mask(low, high, strips, win))
         lane = lax.broadcasted_iota(jnp.int32, (rows, LANES), 1)
         left = lane < DH
+        first, second = low_mask(lane == DH), low_mask(lane == DH + 1)
         outs = []
         for h in range(heads):
             total = totals[h]
-            rows_sum = jnp.where(left, pltpu.roll(total, DH, 1), total)
-            out = jnp.where(left, total / rows_sum, 0.0)
-            log_sum = jnp.log2(rows_sum)
-            d_out = tile(do, at, h, win).astype(F32)
-            delta = jnp.sum(out * d_out, axis=-1, keepdims=True)
-            log_hi = log_sum.astype(BF16).astype(F32)
-            delta_hi = delta.astype(BF16).astype(F32)
-            q = tile(qa, at, h, win).astype(F32)
-            q = jnp.where(lane == DH, -log_hi, jnp.where(lane == DH + 1, log_hi - log_sum, q))
-            d_out = jnp.where(lane == DH, -delta_hi, jnp.where(lane == DH + 1, delta_hi - delta, d_out))
+            log_sum = jnp.log2(jnp.where(left, pltpu.roll(total, DH, 1), total))
+            out = jnp.where(left, total * jnp.exp2(-log_sum), 0.0)
+            d_out = tile(do, at, h, win)
+            delta = jnp.sum(out * d_out.astype(F32), axis=-1, keepdims=True)
+            delta = jnp.broadcast_to(delta, (rows, LANES))
+            log_hi, delta_hi = log_sum.astype(BF16), delta.astype(BF16)
+            log_low = (log_hi.astype(F32) - log_sum).astype(BF16)
+            delta_low = (delta_hi.astype(F32) - delta).astype(BF16)
+            q = jnp.where(first, -log_hi, jnp.where(second, log_low, tile(qa, at, h, win)))
+            d_out = jnp.where(first, -delta_hi, jnp.where(second, delta_low, d_out))
             put_tile(qb, at, h, mask, q, win)
             put_tile(dob, at, h, mask, d_out, win)
             outs.append(out)
@@ -204,31 +228,36 @@
         for b in range(len(outs) // 2):
             put_tile(ho, at, b, mask, jnp.where(left, outs[2 * b], pltpu.roll(outs[2 * b + 1], DH, 1)), win)
 
-    def products(at_q, at_k, k_mask, win_q=WIN, win_k=WIN):
-        scores = [nt(tile(qa, at_q, h, win_q), tile(ka, at_k, h, win_k)) for h in range(heads)]
+    def products(at_q, keys, values, k_mask, win_q=WIN):
+        scores = [nt(tile(qa, at_q, h, win_q), keys(h)) for h in range(heads)]
         weights = [jnp.exp2(s).astype(BF16) for s in scores]
-        return [nn(weights[h], jnp.where(k_mask, tile(va, at_k, h, win_k), zero)) for h in range(heads)]
+        k_mask = low_mask(k_mask)
+        return [nn(weights[h], jnp.where(k_mask, values(h), zero)) for h in range(heads)]
+
+    def plain(at_q, at_k, k_mask, win_q=WIN):
+        return products(at_q, lambda h: tile(ka, at_k, h), lambda h: tile(va, at_k, h), k_mask, win_q)
 
     def small(at, low, high):
-        finish(at, low, high, products(at, at, row_mask(low, high, strips)))
+        finish(at, low, high, plain(at, at, row_mask(low, high, strips)))
 
     def middle(at, low, high):
-        def add(at_k, k_mask, win, first=False):
-            for h, new in enumerate(products(at, at_k, k_mask, big, win)):
-                acc[h] = new if first else acc[h] + new
-
+        edges = products(
+            at, lambda h: edge_tile(ka, at, h, low), lambda h: edge_tile(va, at, h, low),
+            edge_mask(low, high, strips, tok_dev), big,
+        )
+        for h in range(heads):
+            acc[h] = edges[h]
+
+        def k_window(k, _):
+            offset = ALIGN + k * WIN
+            new = plain(pl.multiple_of(at, ALIGN), pl.multiple_of(at + offset, ALIGN), row_mask(low - offset, high - offset, strips), big)
+            for h in range(heads):
+                acc[h] = acc[h] + new[h]
+            return 0
+
+        lax.fori_loop(0, big // WIN - 1, k_window, 0)
         rest = big % WIN
         base = at + big - rest
-        if rest:
-            add(base, row_mask(low - (big - rest), high - (big - rest), strips, rest), rest, True)
-        else:
-            acc[...] = jnp.zeros_like(acc)
-
-        def k_window(k, _):
-            add(pl.multiple_of(at + k * WIN, ALIGN), row_mask(low - k * WIN, high - k * WIN, strips), WIN)
-            return 0
-
-        lax.fori_loop(0, big // WIN, k_window, 0)
 
         def total(h, offset, win):
             return acc[h].reshape(strips, big, LANES)[:, offset : offset + win].reshape(strips * win, LANES)
@@ -250,7 +279,7 @@
 
             def k_window(k, _):
                 at_k, low_k, high_k = window(start, end, first, k, tok_dev)
-                for h, new in enumerate(products(at_q, at_k, row_mask(low_k, high_k, strips))):
+                for h, new in enumerate(plain(at_q, at_k, row_mask(low_k, high_k, strips))):
                     acc[h, :rows] += new
                 return 0
 
@@ -300,10 +329,11 @@
     zero = jnp.zeros((), BF16)
     big = middle_rows(tok_dev)
 
-    def products(at_q, at_k, q_mask, k_turned_of, win_q=WIN, win_k=WIN):
+    def products(queries, d_rows, at_k, q_mask, k_turned_of, win_k=WIN):
         every = range(heads)
-        qs = [tile(qb, at_q, h, win_q) for h in every]
-        d_outs = [jnp.where(q_mask, tile(dob, at_q, h, win_q), zero) for h in every]
+        qs = [queries(h) for h in every]
+        q_mask = low_mask(q_mask)
+        d_outs = [jnp.where(q_mask, d_rows(h), zero) for h in every]
         scores = [nt(tile(ka, at_k, h, win_k), qs[h]) for h in every]
         d_weights = [nt(tile(va, at_k, h, win_k), d_outs[h]) for h in every]
         weights = [jnp.exp2(s) for s in scores]
@@ -313,13 +343,16 @@
         dq_new = [nn(k_turned_of(h), d_scores[h]) for h in every]
         return dq_new, dk_new, dv_new
 
+    def plain(at_q, at_k, q_mask, k_turned_of, win_k=WIN):
+        return products(lambda h: tile(qb, at_q, h), lambda h: tile(dob, at_q, h), at_k, q_mask, k_turned_of, win_k)
+
     def turned(h, at_k, mask, win=WIN):
-        return jnp.where(mask, tile(ka, at_k, h, win), zero).T[:DH]
+        return jnp.where(low_mask(mask), tile(ka, at_k, h, win), zero).T[:DH]
 
     def small(at, low, high):
         mask = row_mask(low, high, strips)
         half = row_mask(low, high, strips, width=DH)
-        dq_t, dk_new, dv_new = products(at, at, mask, lambda h: turned(h, at, mask))
+        dq_t, dk_new, dv_new = plain(at, at, mask, lambda h: turned(h, at, mask))
         for h in range(heads):
             put_tile(dq, at, h, half, dq_t[h].T, width=DH)
             put_tile(dk, at, h, mask, dk_new[h])
@@ -330,28 +363,37 @@
         for h in range(heads):
             k_turned[h] = turned(h, at, mask, big)
 
-        def q_window(at_q, low_q, high_q, win, first=False):
-            mask_q = row_mask(low_q, high_q, strips, win)
-            half = row_mask(low_q, high_q, strips, win, DH)
-            dq_t, dk_new, dv_new = products(at_q, at, mask_q, lambda h: k_turned[h], win, big)
+        dq_t, dk_new, dv_new = products(
+            lambda h: edge_tile(qb, at, h, low), lambda h: edge_tile(dob, at, h, low), at,
+            edge_mask(low, high, strips, tok_dev), lambda h: k_turned[h], big,
+        )
+        last = big - ALIGN
+        body = last - WIN + ALIGN
+        body_mask = row_mask(low - body, high - body, strips, WIN - ALIGN, DH)
+        first_mask = row_mask(low, ALIGN, strips, ALIGN, DH)
+        last_mask = row_mask(0, high - last, strips, ALIGN, DH)
+        for h in range(heads):
+            dk_acc[h], dv_acc[h] = dk_new[h], dv_new[h]
+            rows_new = dq_t[h].T.reshape(strips, WIN, DH)
+            edge = rows_new[:, WIN - ALIGN :].reshape(strips * ALIGN, DH)
+            inner = rows_new[:, : WIN - ALIGN].reshape(strips * (WIN - ALIGN), DH)
+            put_tile(dq, at + body, h, body_mask, inner, WIN - ALIGN, DH)
+            put_tile(dq, at, h, first_mask, edge, ALIGN, DH)
+            put_tile(dq, at + last, h, last_mask, edge, ALIGN, DH)
+
+        def each(i, _):
+            offset = ALIGN + i * WIN
+            at_q = pl.multiple_of(at + offset, ALIGN)
+            mask_q = row_mask(low - offset, high - offset, strips)
+            half = row_mask(low - offset, high - offset, strips, width=DH)
+            dq_t, dk_new, dv_new = plain(at_q, pl.multiple_of(at, ALIGN), mask_q, lambda h: k_turned[h], big)
             for h in range(heads):
-                put_tile(dq, at_q, h, half, dq_t[h].T, win, DH)
-                dk_acc[h] = dk_new[h] if first else dk_acc[h] + dk_new[h]
-                dv_acc[h] = dv_new[h] if first else dv_acc[h] + dv_new[h]
-
-        rest = big % WIN
-        offset = big - rest
-        if rest:
-            q_window(at + offset, low - offset, high - offset, rest, True)
-        else:
-            dk_acc[...] = jnp.zeros_like(dk_acc)
-            dv_acc[...] = jnp.zeros_like(dv_acc)
-
-        def each(i, _):
-            q_window(pl.multiple_of(at + i * WIN, ALIGN), low - i * WIN, high - i * WIN, WIN)
+                put_tile(dq, at_q, h, half, dq_t[h].T, width=DH)
+                dk_acc[h] = dk_acc[h] + dk_new[h]
+                dv_acc[h] = dv_acc[h] + dv_new[h]
             return 0
 
-        lax.fori_loop(0, big // WIN, each, 0)
+        lax.fori_loop(0, big // WIN - 1, each, 0)
         for h in range(heads):
             put_tile(dk, at, h, mask, dk_acc[h], big)
             put_tile(dv, at, h, mask, dv_acc[h], big)
@@ -377,7 +419,7 @@
             def q_window(i, _):
                 at_q, low_q, high_q = window(start, end, first, i, tok_dev)
                 mask_q = row_mask(low_q, high_q, strips)
-                dq_t, dk_new, dv_new = products(at_q, at_k, mask_q, lambda h: k_turned[h, :, :rows])
+                dq_t, dk_new, dv_new = plain(at_q, at_k, mask_q, lambda h: k_turned[h, :, :rows])
                 for h in range(heads):
                     dq_turned[h, i] += dq_t[h]
                     dk_acc[h, :rows] += dk_new[h]
@@ -405,7 +447,7 @@
 
     rows = strips * WIN
     left = left_half(rows)
-    sums = half_sums()
+    sums = half_sums(2 * LANES)
     gains = pair_row(q_gain, k_gain, heads)
     for load in loads:
         load.wait()
@@ -425,12 +467,12 @@
             new_totals.append(totals[h] + jnp.sum(both * u, axis=0, keepdims=True))
             scaled.append(both * gains[:, cols])
             us.append(u)
-        stacked = [s.astype(BF16) for s in scaled] + [(scaled[h] * us[h]).astype(BF16) for h in range(heads)]
-        means = nn(jnp.concatenate(stacked, axis=0), sums) * (1.0 / DH)
+        pairs = [jnp.concatenate([scaled[h].astype(BF16), (scaled[h] * us[h]).astype(BF16)], axis=1) for h in range(heads)]
+        means = nn(jnp.concatenate(pairs, axis=0), sums) * (1.0 / DH)
         parts = []
         for h in range(heads):
-            mean = means[h * rows : (h + 1) * rows]
-            mean_u = means[(heads + h) * rows : (heads + h + 1) * rows]
+            mean = means[h * rows : (h + 1) * rows, :LANES]
+            mean_u = means[h * rows : (h + 1) * rows, LANES:]
             parts.append((scaled[h] - mean - us[h] * mean_u) * tile(r_rows, at, h).astype(F32))
         values = [tile(dv, at, h) for h in range(heads)]
         if heads % 2:
@@ -508,20 +550,20 @@
 
 
 def front_body(
-    heads, n_hi, n_lo, tokens, cot, ln_gain, q_gain, k_gain, mlp_bias, qkv_hbm, attn_hbm, mlp_in_hbm, mlp_out_hbm,
+    heads, n_hi, n_lo, tokens_hbm, cot_hbm, ln_gain, q_gain, k_gain, mlp_bias, qkv_hbm, attn_hbm, mlp_in_hbm, mlp_out_hbm,
     qa_out, ka_out, va_out, do_out, u_out, r_out, mlp_part_out, dn_part_out, nall_out, call_out,
     *rest,
 ):
     (rows_out, both, wide, narrow, qkv_rows, attn_pad, mlp_in, mlp_out, g_in, g_out,
-     send_sem, recv_sem, save_sem, load_sem) = rest[-14:]
+     tokens, low, send_sem, recv_sem, save_sem, load_sem, row_sem) = rest[-17:]
     lo_first, hi_first = rest[:n_lo], rest[n_lo : n_lo + n_hi]
     batch, me = lax.axis_index("batch"), lax.axis_index("tensor")
     sibling = me + 1 - 2 * (me % 2)
     across = (me + 2) % 4
     chip, far_chip = me // 2, 1 - me // 2
-    tok_dev = tokens.shape[0]
+    tok_dev = tokens_hbm.shape[0]
     step = tok_dev // CHUNKS
-    features = tokens.shape[1]
+    features = tokens_hbm.shape[1]
     heads_wide = heads * LANES
 
     def rows_of(c):
@@ -531,6 +573,10 @@
         part = both.at[kind, strip, rows_of(c)]
         return remote(part, part, send_sem.at[kind, route, c], recv_sem.at[kind, route, c], (batch, to))
 
+    load_cot = pltpu.make_async_copy(cot_hbm, both.at[0, me], row_sem.at[0])
+    load_tokens = pltpu.make_async_copy(tokens_hbm, tokens, row_sem.at[1])
+    load_cot.start()
+    load_tokens.start()
     barrier = pltpu.get_barrier_semaphore()
     for other in (sibling, across):
         pl.semaphore_signal(barrier, inc=1, device_id=(batch, other), device_id_type=pl.DeviceIdType.MESH)
@@ -542,7 +588,6 @@
     loads = [pltpu.make_async_copy(a, b, load_sem.at[i]) for i, (a, b) in enumerate(loads)]
     for load in loads:
         load.start()
-    both[0, me] = cot[...]
     gain = row_of(ln_gain)
     gains = pair_row(q_gain, k_gain, heads)
 
@@ -552,24 +597,26 @@
         variance = jnp.mean(centred * centred, axis=-1, keepdims=True)
         both[1, me, rows_of(c)] = (centred * lax.rsqrt(variance + epsilon) * gain).astype(BF16)
 
-    norm_chunk(0)
-    pl.semaphore_wait(barrier, 2)
-
     def send_across(c):
         for kind in range(2):
             move(kind, 1, c, me, across).start()
 
+    load_cot.wait()
+    pl.semaphore_wait(barrier, 2)
+    early = 3
+    for c in range(early):
+        move(0, 1, c, me, across).start()
+    load_tokens.wait()
+
     def first_sends(c, _):
-        @pl.when(c < 3)
+        norm_chunk(c)
+
+        @pl.when(c < early)
         def _():
-            send_across(c)
+            move(1, 1, c, me, across).start()
 
         for kind in range(2):
             move(kind, 0, c, me, sibling).start()
-
-        @pl.when(c + 1 < CHUNKS)
-        def _():
-            norm_chunk(c + 1)
 
         return 0
 
@@ -578,7 +625,7 @@
     g_in[...] = jnp.zeros_like(g_in)
     g_out[...] = jnp.zeros_like(g_out)
     rows_out[...] = jnp.zeros_like(rows_out)
-    rows_out[1:2, :] = jnp.sum(cot[...].astype(F32), axis=0, keepdims=True)
+    rows_out[1:2, :] = jnp.sum(both[0, me].astype(F32), axis=0, keepdims=True)
     filled = 3 * heads * DH
     if filled < qkv_rows.shape[0]:
         qkv_rows[filled:] = jnp.zeros((qkv_rows.shape[0] - filled, features), BF16)
@@ -716,21 +763,32 @@
     lax.fori_loop(0, 2, last, 0)
 
     hi, lo = batch // n_lo, batch % n_lo
-    for o in range(n_hi * n_lo):
-        at_hi = (o // n_lo - hi + n_hi) % n_hi
-        at_lo = (o % n_lo - lo + n_lo) % n_lo
-        for first, part in ((0, lo_first), (lo_rows(features), hi_first)):
-            chunk_rows = part[0].shape[1]
-            row = first + o * chunk_rows
-            source = (g_in, g_out)[row // features]
-            row = row % features
-            low = source[row : row + chunk_rows, :].astype(BF16)
-            slot, place = (at_lo, at_hi) if first == 0 else (at_hi, at_lo)
-            for m in range(len(part)):
-
-                @pl.when(slot == m)
-                def _():
-                    part[m][place] = low
+    def grad_saves():
+        made = []
+        for o in range(n_hi * n_lo):
+            at_hi = (o // n_lo - hi + n_hi) % n_hi
+            at_lo = (o % n_lo - lo + n_lo) % n_lo
+            for first, part in ((0, lo_first), (lo_rows(features), hi_first)):
+                count = part[0].shape[1]
+                rows = low.at[pl.ds(first + o * count, count)]
+                slot, place = (at_lo, at_hi) if first == 0 else (at_hi, at_lo)
+                for m in range(len(part)):
+                    made.append((slot == m, pltpu.make_async_copy(rows, part[m].at[place], save_sem.at[10, (first > 0) * n_hi * n_lo + o])))
+        return made
+
+    low[:features] = g_in[...].astype(BF16)
+    low[features:] = g_out[...].astype(BF16)
+    for chosen, copy in grad_saves():
+
+        @pl.when(chosen)
+        def _():
+            copy.start()
+
+    for chosen, copy in grad_saves():
+
+        @pl.when(chosen)
+        def _():
+            copy.wait()
 
     for at_chip, c, n in (
         [(chip, 0, half), (chip, half, quarter), (chip, half + quarter, quarter)]
@@ -765,8 +823,8 @@
         ) * n_lo + (
             jax.ShapeDtypeStruct((n_lo, (2 * features - lo_rows(features)) // n_batch, features), BF16),
         ) * n_hi + (jax.ShapeDtypeStruct((8, features), F32),),
-        in_specs=[VMEM] * 6 + [ANY] * 4,
-        out_specs=(ANY,) * 10 + (VMEM,) * (n_lo + n_hi + 1),
+        in_specs=[ANY] * 2 + [VMEM] * 4 + [ANY] * 4,
+        out_specs=(ANY,) * (10 + n_lo + n_hi) + (VMEM,),
         scratch_shapes=[
             pltpu.VMEM((2, strips, tok_dev, features), BF16),
             pltpu.VMEM((2, strips, tok_dev, features), BF16),
@@ -777,10 +835,13 @@
             pltpu.VMEM(mlp_out.shape, BF16),
             pltpu.VMEM((features, hidden), F32),
             pltpu.VMEM((hidden, features), F32),
+            pltpu.VMEM(tokens.shape, BF16),
+            pltpu.VMEM((features + hidden, features), BF16),
             pltpu.SemaphoreType.DMA((2, 3, CHUNKS)),
             pltpu.SemaphoreType.DMA((2, 3, CHUNKS)),
-            pltpu.SemaphoreType.DMA((10, 2 * CHUNKS)),
+            pltpu.SemaphoreType.DMA((11, max(2 * CHUNKS, 2 * n_batch))),
             pltpu.SemaphoreType.DMA((2 + 4 * heads,)),
+            pltpu.SemaphoreType.DMA((2,)),
         ],
         compiler_params=pltpu.CompilerParams(collective_id=0, has_side_effects=True, vmem_limit_bytes=60 << 20),
         name="gather_and_project",
@@ -807,11 +868,20 @@
     cut = chunk_rows // 2 // 16 * 16
     parts = [pl.ds(0, cut), pl.ds(cut, chunk_rows - cut)]
 
-    sources = (
-        (d_qkv_hbm, d_qkv), (nall_hbm, nall), (ho_hbm, ho), (call_hbm, call), (dn_part_hbm, dn_part), (mlp_part_hbm, mlp_part)
-    )
-    loads = [pltpu.make_async_copy(a, b, load_sem.at[i]) for i, (a, b) in enumerate(sources)]
-    for load in loads:
+    strips = call.shape[0]
+    by_strip = ((ho_hbm, ho), (call_hbm, call), (d_qkv_hbm, d_qkv), (nall_hbm, nall))
+
+    def strip_loads(i):
+        return [pltpu.make_async_copy(a.at[i], b.at[i], load_sem.at[n, i]) for n, (a, b) in enumerate(by_strip)]
+
+    def rest_loads():
+        pairs = ((dn_part_hbm, dn_part), (mlp_part_hbm, mlp_part))
+        return [pltpu.make_async_copy(a, b, load_sem.at[len(by_strip) + n, 0]) for n, (a, b) in enumerate(pairs)]
+
+    for i in range(strips):
+        for load in strip_loads(i):
+            load.start()
+    for load in rest_loads():
         load.start()
 
     def hi_peer(k):
@@ -882,10 +952,10 @@
     attn_pad[head_width:] = jnp.zeros((attn_pad.shape[0] - head_width, features), BF16)
     acc[...] = jnp.zeros_like(acc)
     attn_acc[...] = jnp.zeros_like(attn_acc)
-    for load in loads[:4]:
-        load.wait()
 
     def add_strip(i, _):
+        for load in strip_loads(i):
+            load.wait()
         acc[...] += tn(d_qkv[i], nall[i])
         attn_acc[...] += tn(ho[i], call[i])
         return 0
@@ -1018,7 +1088,7 @@
         lax.fori_loop(0, BACK_CHUNKS, give, 0)
         lax.fori_loop(0, BACK_CHUNKS, keep, 0)
 
-    for load in loads[4:]:
+    for load in rest_loads():
         load.wait()
     far(0)
     for m in every_m:
@@ -1181,7 +1251,7 @@
             vmem((n_lo, 8, features), F32),
             vmem((n_hi, 8, features), F32),
             vmem((2, 8, features), F32),
-            dma((6,)),
+            dma((6, strips)),
             dma((2, n_hi)), dma((2, n_hi)),
             dma((n_lo, n_hi)), dma((n_lo, n_hi)),
             dma((n_lo, 2)), dma((n_lo, 2)),

time: 170 us -> 170 us (level)
    pallas_call x1, Pallas kernels: 68 us -> 59.9 us  [back(): pl.pallas_call(functools.partial(back_body, heads, n_hi, n_lo), out_shape...]
    pallas_call x1, Pallas kernels: 15.2 us -> 21.7 us  [attn_bwd(): pl.pallas_call(functools.partial(attn_bwd_body, heads), out_shape=(jax.Sh...]
  transfers between devices with their start and end apart: 8 -> 8, of which waited for: 1 -> 1; matrix products, arithmetic and copies ran while one was open for 0% -> 0% of each run, Pallas kernels for 19% -> 23%
where the time goes in v5:
time: 170 us; the launch traced here: 169 us
  Pallas kernels  153 us (90%)
  starting transfers between devices  12.5 us (7%)
  other arithmetic  1.73 us (1%)
    pallas_call x1, Pallas kernels, back(): pl.pallas_call(functools.partial(back_body, heads, n_hi, n_lo), out_shape...  59.9 us
    pallas_call x1, Pallas kernels, front(): pl.pallas_call(functools.partial(front_body, heads, n_hi, n_lo), out_shap...  48.1 us
    pallas_call x1, Pallas kernels, attn_bwd(): pl.pallas_call(functools.partial(attn_bwd_body, heads), out_shape=(jax.Sh...  21.7 us
    pallas_call x1, Pallas kernels, attn_fwd(): pl.pallas_call(functools.partial(attn_fwd_body, heads), out_shape=(like,...  17.1 us
    ppermute x6, starting transfers between devices, along_hi(): return lax.ppermute(x, 'batch', pairs)  9.44 us
    pallas_call x1, Pallas kernels, widen(): pl.pallas_call(functools.partial(widen_body, heads), out_shape=(like, lik...  6.32 us
  transfers between devices with their start and end apart: 8, of which 1 were waited for; matrix products, arithmetic and copies ran while one was open for 0% of the time, Pallas kernels for 23%

profile of v5, /device:TPU:0, one launch (start us, length us, event | category | flops | bytes accessed | tf_op | source)
XLA Modules:
  0.0 168.7 jit_solution(913524623209881449)
XLA Ops:
  0.6 48.1 %gather_and_project.1 = (bf16[4,512,384]{2,1,0:T(8,128)(2,1)}, bf16[4,512,384]{2,1,0:T(8,128)(2,1)}, bf16[4,512,384]{2,1,0:T(8,128)(2,1)}, bf16[4,512,384]{2,1,0...) custom-call(bf16[512,768]{1,0:T(8,128)(2,1)} %tokens.1, ...), custom_call_target="tpu_custom_call" | custom-call | tf_op jit(solution)/shard_map/gather_and_project/pallas_call | solution.py:819
  48.8 1.7 collective-permute-start.1
  50.4 2.7 %collective-permute-start.2 = (bf16[2,64,768]{2,1,0:T(8,128)(2,1)}, bf16[2,64,768]{2,1,0:T(8,128)(2,1)S(1)}, u32[]{:S(2)}, u32[]{:S(2)}) collective-permute-start(bf16[2,64,768]{2,1,0:T(8,128)(2,1)} %get-tuple-element.65), channel_id=1, source_target_pairs={{0,16},{4,20},{8,24},{12,28},{16,0},{20,4},{24,8},{28,12},{1,17},{... | collective-permute-start | bytes 589832 | tf_op jit(solution)/shard_map/ppermute | solution.py:1381
  53.1 1.3 collective-permute-start.3
  54.4 1.5 collective-permute-start
  55.9 0.0 copy-start.1
  55.9 0.0 copy-start
  55.9 17.1 %attention_forward.1 = (bf16[4,512,384]{2,1,0:T(8,128)(2,1)}, bf16[4,512,384]{2,1,0:T(8,128)(2,1)}, bf16[4,512,256]{2,1,0:T(8,128)(2,1)}) custom-call(s32[80]{0:T(128)} %len_ref.3, s32[80]{0:T(128)} %group_ref.3, bf16[4,512,384]{2,1,0:T(8,128)(2,1)} %get-tuple-element.56.qa_hbm, bf16[4,512,384]{2,1,0:T(8,128)(2,1)} %get-tuple-element.57.ka_hbm, ...), custom_call_target="tpu_custom_call" | custom-call | flops 8000000000 | bytes 30000000 | tf_op jit(solution)/shard_map/attention_forward/pallas_call | solution.py:303
  73.1 0.0 collective-permute-done.1
  73.1 0.0 collective-permute-done.2
  73.1 0.0 collective-permute-done.3
  73.1 0.0 copy-done.1
  73.1 0.1 fusion.5
  73.2 0.4 collective-permute-done
  73.6 0.0 copy-done
  73.6 0.2 fusion.3
  73.8 1.6 collective-permute-start.7
  75.3 0.7 collective-permute-start.4
  76.1 0.3 collective-permute-start.5
  76.4 2.8 %collective-permute-start.6 = (bf16[128,768]{1,0:T(8,128)(2,1)S(1)}, bf16[128,768]{1,0:T(8,128)(2,1)S(1)}, u32[]{:S(2)}, u32[]{:S(2)}) collective-permute-start(bf16[128,768]{1,0:T(8,128)(2,1)S(1)} %get-tuple-element.80), channel_id=1, source_target_pairs={{0,24},{4,28},{8,0},{12,4},{16,8},{20,12},{24,16},{28,20},{1,25},{... | collective-permute-start | bytes 589832 | tf_op jit(solution)/shard_map/ppermute | solution.py:1381
  79.2 21.7 %attention_backward.1 = (bf16[4,512,640]{2,1,0:T(8,128)(2,1)}, f32[8,384]{1,0:T(8,128)}) custom-call(s32[80]{0:T(128)} %len_ref.3, s32[80]{0:T(128)} %group_ref.3, bf16[4,512,384]{2,1,0:T(8,128)(2,1)} %get-tuple-element.67.qb_hbm, bf16[4,512,384]{2,1,0:T(8,128)(2,1)} %get-tuple-element.57.ka_hbm, bf16[4,512,384]{2,1,0:T(8,128)(2,1)} %get-tuple-element.58.va_hbm, ...), custom_call_target="tpu_custom_call" | custom-call | flops 16000000000 | bytes 30000000 | tf_op jit(solution)/shard_map/attention_backward/pallas_call | solution.py:507
  100.9 0.0 collective-permute-done.7
  100.9 0.7 add_convert_fusion.5.own_hi
  101.6 0.0 collective-permute-done.4
  101.6 0.0 collective-permute-done.5
  101.6 0.0 collective-permute-done.6
  101.6 0.8 add_convert_fusion.own_lo
  102.3 59.9 %reduce_gradients.1 = (bf16[512,768]{1,0:T(8,128)(2,1)}, bf16[512,768]{1,0:T(8,128)(2,1)}, bf16[4,2,192,768]{3,2,1,0:T(8,128)(2,1)}, bf16[2,4,192,384]{3,2,1,0:T(8,128)(2,1)}, f32[8,768]{1,0:T(8,128)}) custom-call(bf16[4,512,640]{2,1,0:T(8,128)(2,1)} %get-tuple-element.71.d_qkv_hbm, bf16[4,512,768]{2,1,0:T(8,128)(2,1)} %get-tuple-element.72.nall_hbm, ...), custom_call_target="tpu_custom_call" | custom-call | tf_op jit(solution)/shard_map/reduce_gradients/pallas_call | solution.py:1220
  162.3 6.3 %widen_gradients.1 = (bf16[512,768]{1,0:T(8,128)(2,1)}, bf16[512,768]{1,0:T(8,128)(2,1)}, f32[576,768]{1,0:T(8,128)}, f32[192,768]{1,0:T(8,128)}, f32[768,768]{1...) custom-call(bf16[8,192,768]{2,1,0:T(8,128)(2,1)} %bitcast.17, ...), custom_call_target="tpu_custom_call" | custom-call | tf_op jit(solution)/shard_map/widen_gradients/pallas_call | solution.py:1336
Async XLA Ops:
  48.8 24.3 %collective-permute-start.1 = (bf16[2,64,768]{2,1,0:T(8,128)(2,1)}, bf16[2,64,768]{2,1,0:T(8,128)(2,1)S(1)}, u32[]{:S(2)}, u32[]{:S(2)}) collective-permute-start(bf16[2,64,768]{2,1,0:T(8,128)(2,1)} %get-tuple-element.64), channel_id=1, source_target_pairs={{0,8},{4,12},{8,16},{12,20},{16,24},{20,28},{24,0},{28,4},{1,9},{5... | collective-permute-start | bytes 589832 | tf_op jit(solution)/shard_map/ppermute | solution.py:1381
  50.4 22.6 %collective-permute-start.2 = (bf16[2,64,768]{2,1,0:T(8,128)(2,1)}, bf16[2,64,768]{2,1,0:T(8,128)(2,1)S(1)}, u32[]{:S(2)}, u32[]{:S(2)}) collective-permute-start(bf16[2,64,768]{2,1,0:T(8,128)(2,1)} %get-tuple-element.65), channel_id=1, source_target_pairs={{0,16},{4,20},{8,24},{12,28},{16,0},{20,4},{24,8},{28,12},{1,17},{... | collective-permute-start | bytes 589832 | tf_op jit(solution)/shard_map/ppermute | solution.py:1381
  53.1 20.0 %collective-permute-start.3 = (bf16[2,64,768]{2,1,0:T(8,128)(2,1)}, bf16[2,64,768]{2,1,0:T(8,128)(2,1)S(1)}, u32[]{:S(2)}, u32[]{:S(2)}) collective-permute-start(bf16[2,64,768]{2,1,0:T(8,128)(2,1)} %get-tuple-element.66), channel_id=1, source_target_pairs={{0,24},{4,28},{8,0},{12,4},{16,8},{20,12},{24,16},{28,20},{1,25},{... | collective-permute-start | bytes 589832 | tf_op jit(solution)/shard_map/ppermute | solution.py:1381
  54.4 19.2 %collective-permute-start = (bf16[4,128,768]{2,1,0:T(8,128)(2,1)}, bf16[4,128,768]{2,1,0:T(8,128)(2,1)S(1)}, u32[]{:S(2)}, u32[]{:S(2)}) collective-permute-start(bf16[4,128,768]{2,1,0:T(8,128)(2,1)} %get-tuple-element.62), channel_id=1, source_target_pairs={{0,4},{4,0},{8,12},{12,8},{16,20},{20,16},{24,28},{28,24},{1,5},{5... | collective-permute-start | bytes 2359304 | tf_op jit(solution)/shard_map/ppermute | solution.py:1377
  55.9 17.2 %copy-start.1 = (bf16[2,64,768]{2,1,0:T(8,128)(2,1)S(1)}, bf16[2,64,768]{2,1,0:T(8,128)(2,1)}, u32[]{:S(2)}) copy-start(bf16[2,64,768]{2,1,0:T(8,128)(2,1)} %get-tuple-element.63) | copy-start | bytes 589828
  55.9 17.7 %copy-start = (bf16[4,128,768]{2,1,0:T(8,128)(2,1)S(1)}, bf16[4,128,768]{2,1,0:T(8,128)(2,1)}, u32[]{:S(2)}) copy-start(bf16[4,128,768]{2,1,0:T(8,128)(2,1)} %get-tuple-element.61) | copy-start | bytes 2359300
  73.8 27.1 %collective-permute-start.7 = (bf16[64,768]{1,0:T(8,128)(2,1)S(1)}, bf16[64,768]{1,0:T(8,128)(2,1)S(1)}, u32[]{:S(2)}, u32[]{:S(2)}) collective-permute-start(bf16[64,768]{1,0:T(8,128)(2,1)S(1)} %get-tuple-element.82), channel_id=1, source_target_pairs={{0,4},{4,0},{8,12},{12,8},{16,20},{20,16},{24,28},{28,24},{1,5},{5... | collective-permute-start | bytes 294920 | tf_op jit(solution)/shard_map/ppermute | solution.py:1377
  75.3 26.2 %collective-permute-start.4 = (bf16[128,768]{1,0:T(8,128)(2,1)S(1)}, bf16[128,768]{1,0:T(8,128)(2,1)S(1)}, u32[]{:S(2)}, u32[]{:S(2)}) collective-permute-start(bf16[128,768]{1,0:T(8,128)(2,1)S(1)} %get-tuple-element.78), channel_id=1, source_target_pairs={{0,8},{4,12},{8,16},{12,20},{16,24},{20,28},{24,0},{28,4},{1,9},{5... | collective-permute-start | bytes 589832 | tf_op jit(solution)/shard_map/ppermute | solution.py:1381
  76.1 25.5 %collective-permute-start.5 = (bf16[128,768]{1,0:T(8,128)(2,1)S(1)}, bf16[128,768]{1,0:T(8,128)(2,1)S(1)}, u32[]{:S(2)}, u32[]{:S(2)}) collective-permute-start(bf16[128,768]{1,0:T(8,128)(2,1)S(1)} %get-tuple-element.79), channel_id=1, source_target_pairs={{0,16},{4,20},{8,24},{12,28},{16,0},{20,4},{24,8},{28,12},{1,17},{... | collective-permute-start | bytes 589832 | tf_op jit(solution)/shard_map/ppermute | solution.py:1381
  76.4 25.2 %collective-permute-start.6 = (bf16[128,768]{1,0:T(8,128)(2,1)S(1)}, bf16[128,768]{1,0:T(8,128)(2,1)S(1)}, u32[]{:S(2)}, u32[]{:S(2)}) collective-permute-start(bf16[128,768]{1,0:T(8,128)(2,1)S(1)} %get-tuple-element.80), channel_id=1, source_target_pairs={{0,24},{4,28},{8,0},{12,4},{16,8},{20,12},{24,16},{28,20},{1,25},{... | collective-permute-start | bytes 589832 | tf_op jit(solution)/shard_map/ppermute | solution.py:1381

commit v6 on v5

--- a/solution.py
+++ b/solution.py
@@ -950,17 +950,17 @@
     head_width = attn_out.shape[0]
     attn_pad[:head_width] = attn_out[...]
     attn_pad[head_width:] = jnp.zeros((attn_pad.shape[0] - head_width, features), BF16)
-    acc[...] = jnp.zeros_like(acc)
-    attn_acc[...] = jnp.zeros_like(attn_acc)
-
-    def add_strip(i, _):
-        for load in strip_loads(i):
+    def rows_of_pair(ref, i):
+        return ref[2 * i : 2 * i + 2].reshape(2 * ref.shape[1], ref.shape[2])
+
+    for i in range(strips // 2):
+        for load in strip_loads(2 * i) + strip_loads(2 * i + 1):
             load.wait()
-        acc[...] += tn(d_qkv[i], nall[i])
-        attn_acc[...] += tn(ho[i], call[i])
-        return 0
-
-    lax.fori_loop(0, nall.shape[0], add_strip, 0)
+        new = tn(rows_of_pair(d_qkv, i), rows_of_pair(nall, i))
+        acc[...] = acc[...] + new if i else new
+        new = tn(rows_of_pair(ho, i), rows_of_pair(call, i))
+        attn_acc[...] = attn_acc[...] + new if i else new
+
     width = qkv_weight_t.shape[0]
     joint_low[:width] = acc[:width].astype(BF16)
     joint_low[width:] = attn_acc[:head_width].astype(BF16)
@@ -1094,13 +1094,13 @@
     for m in every_m:
         joint_lo(1, m).start()
     far(1)
+    mlp_send_lo(1)
     joint_sum_lo(0)
     for s in range(2, n_hi - 1):
         mlp_wait_hop(s)
         mlp_send_hop(s + 1)
     close(0)
     joint_sum_lo(1)
-    mlp_send_lo(1)
     close(1)
 
     for m in every_m:
@@ -1112,13 +1112,13 @@
     for k in every_k:
         vec_hi_move(k).start()
 
-    joint_sum_hi(0)
     for s in range(2, n_hi - 1):
         mlp_send_lo(s)
-    joint_sum_hi(1)
+    joint_sum_hi(0)
     if n_hi > 2:
         mlp_wait_hop(n_hi - 1)
         mlp_send_lo(n_hi - 1)
+    joint_sum_hi(1)
 
     for k in every_k:
         vec_hi_move(k, -k).wait_recv()

time: 170 us -> 167 us (0.982)
  Pallas kernels: 153 us -> 149 us
  waiting for transfers between devices: 0.39 us -> 2.17 us
    pallas_call x1, Pallas kernels: 21.7 us -> 15.4 us  [attn_bwd(): pl.pallas_call(functools.partial(attn_bwd_body, heads), out_shape=(jax.Sh...]
    pallas_call x1, Pallas kernels: 59.9 us -> 64.1 us  [back(): pl.pallas_call(functools.partial(back_body, heads, n_hi, n_lo), out_shape...]
    ppermute x2, waiting for transfers between devices: 0.37 us -> 2.16 us  [along_lo(): return lax.ppermute(x, 'batch', pairs)]
    pallas_call x1, Pallas kernels: 17.1 us -> 15.4 us  [attn_fwd(): pl.pallas_call(functools.partial(attn_fwd_body, heads), out_shape=(like,...]
  transfers between devices with their start and end apart: 8 -> 8, of which waited for: 1 -> 1; matrix products, arithmetic and copies ran while one was open for 0% -> 0% of each run, Pallas kernels for 23% -> 18%
where the time goes in v6:
time: 167 us
  Pallas kernels  149 us (89%)
  starting transfers between devices  12.5 us (7%)
  waiting for transfers between devices  2.17 us (1%)
  other arithmetic  1.73 us (1%)
    pallas_call x1, Pallas kernels, back(): pl.pallas_call(functools.partial(back_body, heads, n_hi, n_lo), out_shape...  64.1 us
    pallas_call x1, Pallas kernels, front(): pl.pallas_call(functools.partial(front_body, heads, n_hi, n_lo), out_shap...  48.1 us
    pallas_call x1, Pallas kernels, attn_bwd(): pl.pallas_call(functools.partial(attn_bwd_body, heads), out_shape=(jax.Sh...  15.4 us
    pallas_call x1, Pallas kernels, attn_fwd(): pl.pallas_call(functools.partial(attn_fwd_body, heads), out_shape=(like,...  15.4 us
    ppermute x6, starting transfers between devices, along_hi(): return lax.ppermute(x, 'batch', pairs)  9.44 us
    pallas_call x1, Pallas kernels, widen(): pl.pallas_call(functools.partial(widen_body, heads), out_shape=(like, lik...  6.32 us
  transfers between devices with their start and end apart: 8, of which 1 were waited for; matrix products, arithmetic and copies ran while one was open for 0% of the time, Pallas kernels for 18%

profile of v6, /device:TPU:0, one launch (start us, length us, event | category | flops | bytes accessed | tf_op | source)
XLA Modules:
  0.0 166.7 jit_solution(15774586567010675123)
XLA Ops:
  0.6 48.1 %gather_and_project.1 = (bf16[4,512,384]{2,1,0:T(8,128)(2,1)}, bf16[4,512,384]{2,1,0:T(8,128)(2,1)}, bf16[4,512,384]{2,1,0:T(8,128)(2,1)}, bf16[4,512,384]{2,1,0...) custom-call(bf16[512,768]{1,0:T(8,128)(2,1)} %tokens.1, ...), custom_call_target="tpu_custom_call" | custom-call | tf_op jit(solution)/shard_map/gather_and_project/pallas_call | solution.py:819
  48.8 1.7 %collective-permute-start.1 = (bf16[2,64,768]{2,1,0:T(8,128)(2,1)}, bf16[2,64,768]{2,1,0:T(8,128)(2,1)S(1)}, u32[]{:S(2)}, u32[]{:S(2)}) collective-permute-start(bf16[2,64,768]{2,1,0:T(8,128)(2,1)} %get-tuple-element.64), channel_id=1, source_target_pairs={{0,8},{4,12},{8,16},{12,20},{16,24},{20,28},{24,0},{28,4},{1,9},{5... | collective-permute-start | bytes 589832 | tf_op jit(solution)/shard_map/ppermute | solution.py:1381
  50.4 2.7 %collective-permute-start.2 = (bf16[2,64,768]{2,1,0:T(8,128)(2,1)}, bf16[2,64,768]{2,1,0:T(8,128)(2,1)S(1)}, u32[]{:S(2)}, u32[]{:S(2)}) collective-permute-start(bf16[2,64,768]{2,1,0:T(8,128)(2,1)} %get-tuple-element.65), channel_id=1, source_target_pairs={{0,16},{4,20},{8,24},{12,28},{16,0},{20,4},{24,8},{28,12},{1,17},{... | collective-permute-start | bytes 589832 | tf_op jit(solution)/shard_map/ppermute | solution.py:1381
  53.1 1.3 collective-permute-start.3
  54.4 1.5 collective-permute-start
  55.9 0.0 copy-start.1
  55.9 0.0 copy-start
  55.9 15.4 %attention_forward.1 = (bf16[4,512,384]{2,1,0:T(8,128)(2,1)}, bf16[4,512,384]{2,1,0:T(8,128)(2,1)}, bf16[4,512,256]{2,1,0:T(8,128)(2,1)}) custom-call(s32[80]{0:T(128)} %len_ref.3, s32[80]{0:T(128)} %group_ref.3, bf16[4,512,384]{2,1,0:T(8,128)(2,1)} %get-tuple-element.56.qa_hbm, bf16[4,512,384]{2,1,0:T(8,128)(2,1)} %get-tuple-element.57.ka_hbm, ...), custom_call_target="tpu_custom_call" | custom-call | flops 8000000000 | bytes 30000000 | tf_op jit(solution)/shard_map/attention_forward/pallas_call | solution.py:303
  71.3 0.0 collective-permute-done.1
  71.3 0.0 collective-permute-done.2
  71.3 0.0 collective-permute-done.3
  71.3 0.0 copy-done.1
  71.3 0.1 fusion.5
  71.4 2.2 %collective-permute-done = bf16[4,128,768]{2,1,0:T(8,128)(2,1)S(1)} collective-permute-done((bf16[4,128,768]{2,1,0:T(8,128)(2,1)}, bf16[4,128,768]{2,1,0:T(8,128)(2,1)S(1)}, u32[]{:S(2)}, u32[]{:S(2)}) %collective-permute-start) | collective-permute-done | bytes 786464 | tf_op jit(solution)/shard_map/ppermute | solution.py:1377
  73.6 0.0 copy-done
  73.6 0.2 fusion.3
  73.8 1.6 collective-permute-start.7
  75.3 0.7 collective-permute-start.4
  76.1 0.3 collective-permute-start.5
  76.4 2.8 %collective-permute-start.6 = (bf16[128,768]{1,0:T(8,128)(2,1)S(1)}, bf16[128,768]{1,0:T(8,128)(2,1)S(1)}, u32[]{:S(2)}, u32[]{:S(2)}) collective-permute-start(bf16[128,768]{1,0:T(8,128)(2,1)S(1)} %get-tuple-element.80), channel_id=1, source_target_pairs={{0,24},{4,28},{8,0},{12,4},{16,8},{20,12},{24,16},{28,20},{1,25},{... | collective-permute-start | bytes 589832 | tf_op jit(solution)/shard_map/ppermute | solution.py:1381
  79.2 15.4 %attention_backward.1 = (bf16[4,512,640]{2,1,0:T(8,128)(2,1)}, f32[8,384]{1,0:T(8,128)}) custom-call(s32[80]{0:T(128)} %len_ref.3, s32[80]{0:T(128)} %group_ref.3, bf16[4,512,384]{2,1,0:T(8,128)(2,1)} %get-tuple-element.67.qb_hbm, bf16[4,512,384]{2,1,0:T(8,128)(2,1)} %get-tuple-element.57.ka_hbm, bf16[4,512,384]{2,1,0:T(8,128)(2,1)} %get-tuple-element.58.va_hbm, ...), custom_call_target="tpu_custom_call" | custom-call | flops 16000000000 | bytes 30000000 | tf_op jit(solution)/shard_map/attention_backward/pallas_call | solution.py:507
  94.5 0.0 collective-permute-done.7
  94.6 0.7 add_convert_fusion.5.own_hi
  95.2 0.0 collective-permute-done.4
  95.2 0.0 collective-permute-done.5
  95.2 0.0 collective-permute-done.6
  95.2 0.8 add_convert_fusion.own_lo
  96.0 64.1 %reduce_gradients.1 = (bf16[512,768]{1,0:T(8,128)(2,1)}, bf16[512,768]{1,0:T(8,128)(2,1)}, bf16[4,2,192,768]{3,2,1,0:T(8,128)(2,1)}, bf16[2,4,192,384]{3,2,1,0:T(8,128)(2,1)}, f32[8,768]{1,0:T(8,128)}) custom-call(bf16[4,512,640]{2,1,0:T(8,128)(2,1)} %get-tuple-element.71.d_qkv_hbm, bf16[4,512,768]{2,1,0:T(8,128)(2,1)} %get-tuple-element.72.nall_hbm, ...), custom_call_target="tpu_custom_call" | custom-call | tf_op jit(solution)/shard_map/reduce_gradients/pallas_call | solution.py:1220
  160.2 6.3 %widen_gradients.1 = (bf16[512,768]{1,0:T(8,128)(2,1)}, bf16[512,768]{1,0:T(8,128)(2,1)}, f32[576,768]{1,0:T(8,128)}, f32[192,768]{1,0:T(8,128)}, f32[768,768]{1...) custom-call(bf16[8,192,768]{2,1,0:T(8,128)(2,1)} %bitcast.17, ...), custom_call_target="tpu_custom_call" | custom-call | tf_op jit(solution)/shard_map/widen_gradients/pallas_call | solution.py:1336
Async XLA Ops:
  48.8 22.5 %collective-permute-start.1 = (bf16[2,64,768]{2,1,0:T(8,128)(2,1)}, bf16[2,64,768]{2,1,0:T(8,128)(2,1)S(1)}, u32[]{:S(2)}, u32[]{:S(2)}) collective-permute-start(bf16[2,64,768]{2,1,0:T(8,128)(2,1)} %get-tuple-element.64), channel_id=1, source_target_pairs={{0,8},{4,12},{8,16},{12,20},{16,24},{20,28},{24,0},{28,4},{1,9},{5... | collective-permute-start | bytes 589832 | tf_op jit(solution)/shard_map/ppermute | solution.py:1381
  50.4 20.8 %collective-permute-start.2 = (bf16[2,64,768]{2,1,0:T(8,128)(2,1)}, bf16[2,64,768]{2,1,0:T(8,128)(2,1)S(1)}, u32[]{:S(2)}, u32[]{:S(2)}) collective-permute-start(bf16[2,64,768]{2,1,0:T(8,128)(2,1)} %get-tuple-element.65), channel_id=1, source_target_pairs={{0,16},{4,20},{8,24},{12,28},{16,0},{20,4},{24,8},{28,12},{1,17},{... | collective-permute-start | bytes 589832 | tf_op jit(solution)/shard_map/ppermute | solution.py:1381
  53.1 18.2 %collective-permute-start.3 = (bf16[2,64,768]{2,1,0:T(8,128)(2,1)}, bf16[2,64,768]{2,1,0:T(8,128)(2,1)S(1)}, u32[]{:S(2)}, u32[]{:S(2)}) collective-permute-start(bf16[2,64,768]{2,1,0:T(8,128)(2,1)} %get-tuple-element.66), channel_id=1, source_target_pairs={{0,24},{4,28},{8,0},{12,4},{16,8},{20,12},{24,16},{28,20},{1,25},{... | collective-permute-start | bytes 589832 | tf_op jit(solution)/shard_map/ppermute | solution.py:1381
  54.4 19.2 %collective-permute-start = (bf16[4,128,768]{2,1,0:T(8,128)(2,1)}, bf16[4,128,768]{2,1,0:T(8,128)(2,1)S(1)}, u32[]{:S(2)}, u32[]{:S(2)}) collective-permute-start(bf16[4,128,768]{2,1,0:T(8,128)(2,1)} %get-tuple-element.62), channel_id=1, source_target_pairs={{0,4},{4,0},{8,12},{12,8},{16,20},{20,16},{24,28},{28,24},{1,5},{5... | collective-permute-start | bytes 2359304 | tf_op jit(solution)/shard_map/ppermute | solution.py:1377
  55.9 15.4 %copy-start.1 = (bf16[2,64,768]{2,1,0:T(8,128)(2,1)S(1)}, bf16[2,64,768]{2,1,0:T(8,128)(2,1)}, u32[]{:S(2)}) copy-start(bf16[2,64,768]{2,1,0:T(8,128)(2,1)} %get-tuple-element.63) | copy-start | bytes 589828
  55.9 17.7 %copy-start = (bf16[4,128,768]{2,1,0:T(8,128)(2,1)S(1)}, bf16[4,128,768]{2,1,0:T(8,128)(2,1)}, u32[]{:S(2)}) copy-start(bf16[4,128,768]{2,1,0:T(8,128)(2,1)} %get-tuple-element.61) | copy-start | bytes 2359300
  73.8 20.8 %collective-permute-start.7 = (bf16[64,768]{1,0:T(8,128)(2,1)S(1)}, bf16[64,768]{1,0:T(8,128)(2,1)S(1)}, u32[]{:S(2)}, u32[]{:S(2)}) collective-permute-start(bf16[64,768]{1,0:T(8,128)(2,1)S(1)} %get-tuple-element.82), channel_id=1, source_target_pairs={{0,4},{4,0},{8,12},{12,8},{16,20},{20,16},{24,28},{28,24},{1,5},{5... | collective-permute-start | bytes 294920 | tf_op jit(solution)/shard_map/ppermute | solution.py:1377
  75.3 19.9 %collective-permute-start.4 = (bf16[128,768]{1,0:T(8,128)(2,1)S(1)}, bf16[128,768]{1,0:T(8,128)(2,1)S(1)}, u32[]{:S(2)}, u32[]{:S(2)}) collective-permute-start(bf16[128,768]{1,0:T(8,128)(2,1)S(1)} %get-tuple-element.78), channel_id=1, source_target_pairs={{0,8},{4,12},{8,16},{12,20},{16,24},{20,28},{24,0},{28,4},{1,9},{5... | collective-permute-start | bytes 589832 | tf_op jit(solution)/shard_map/ppermute | solution.py:1381
  76.1 19.2 %collective-permute-start.5 = (bf16[128,768]{1,0:T(8,128)(2,1)S(1)}, bf16[128,768]{1,0:T(8,128)(2,1)S(1)}, u32[]{:S(2)}, u32[]{:S(2)}) collective-permute-start(bf16[128,768]{1,0:T(8,128)(2,1)S(1)} %get-tuple-element.79), channel_id=1, source_target_pairs={{0,16},{4,20},{8,24},{12,28},{16,0},{20,4},{24,8},{28,12},{1,17},{... | collective-permute-start | bytes 589832 | tf_op jit(solution)/shard_map/ppermute | solution.py:1381
  76.4 18.9 %collective-permute-start.6 = (bf16[128,768]{1,0:T(8,128)(2,1)S(1)}, bf16[128,768]{1,0:T(8,128)(2,1)S(1)}, u32[]{:S(2)}, u32[]{:S(2)}) collective-permute-start(bf16[128,768]{1,0:T(8,128)(2,1)S(1)} %get-tuple-element.80), channel_id=1, source_target_pairs={{0,24},{4,28},{8,0},{12,4},{16,8},{20,12},{24,16},{28,20},{1,25},{... | collective-permute-start | bytes 589832 | tf_op jit(solution)/shard_map/ppermute | solution.py:1381

commit v7 on v6

--- a/solution.py
+++ b/solution.py
@@ -1133,6 +1133,8 @@
     vec[1] = vec[0] + vec_pair[0]
     vec_pair_move(1, across).start()
 
+    joint_pass(1)
+
     def last_rows(c, _):
         x_move(0, c).wait_recv()
         where = rows_of(c)
@@ -1147,7 +1149,6 @@
         return 0
 
     lax.fori_loop(0, BACK_CHUNKS, last_rows, 0)
-    joint_pass(1)
     bias = row_of(out_bias)
 
     def out_rows(c, _):
@@ -1281,8 +1282,9 @@
         made.start()
         return made
 
+    chunks = mlp_all.shape[0]
+    load_mlp = [copy(10 + o, mlp_hbm.at[o], mlp_all.at[o]) for o in range(chunks)]
     load_joint = copy(0, joint_hbm, joint_all)
-    load_mlp = copy(1, mlp_hbm, mlp_all)
     load_rows = [copy(2, output_in, kept.at[0]), copy(3, input_grad_in, kept.at[1])]
     features = rows.shape[1]
     mlp_bias[...] = rows[0:1, :].reshape(features)
@@ -1291,6 +1293,21 @@
     for offset, ref in ((0, q_gain), (DH, k_gain)):
         parts = [rows[3:4, h * LANES + offset : h * LANES + offset + DH] for h in range(heads)]
         ref[...] = jnp.concatenate(parts, axis=1).reshape(heads * DH)
+    cut = lo_rows(features) // chunks
+    rest = mlp_all.shape[1] - cut
+    pending = []
+
+    def store(sem, row, count):
+        to = mlp_in_out if row < features else mlp_out_out
+        pending.append(copy(sem, mlp.at[pl.ds(row, count)], to.at[pl.ds(row % features, count)]))
+
+    for o in range(chunks):
+        load_mlp[o].wait()
+        row = lo_rows(features) + o * rest
+        mlp[o * cut : (o + 1) * cut] = mlp_all[o, :cut].astype(F32)
+        mlp[row : row + rest] = mlp_all[o, cut:].astype(F32)
+        store(10 + chunks + o, o * cut, cut)
+        store(10 + 2 * chunks + o, row, rest)
     load_joint.wait()
     n_lo, n_hi, chunk_rows, cols = joint_all.shape
     width = qkv_t.shape[0]
@@ -1298,26 +1315,12 @@
     for o in range(n_lo * n_hi):
         row = o % per_half * chunk_rows
         joint[o // per_half, row : row + chunk_rows] = joint_all[o % n_lo, o // n_lo]
-    pending = []
     for half in range(2):
         at = slice(half * cols, (half + 1) * cols)
         attn[:, at] = joint[half, width:].astype(F32)
         for i, place in enumerate(kind_order(heads)):
             qkv_t[place * DH : (place + 1) * DH, at] = joint[half, i * DH : (i + 1) * DH].astype(F32)
     pending += [copy(4, qkv_t, qkv_out), copy(5, attn, attn_out)]
-    load_mlp.wait()
-    chunks = mlp_all.shape[0]
-    cut = lo_rows(features) // chunks
-    rest = mlp_all.shape[1] - cut
-    for o in range(features // cut):
-        mlp[o * cut : (o + 1) * cut] = mlp_all[o, :cut].astype(F32)
-    pending.append(copy(6, mlp.at[pl.ds(0, features)], mlp_in_out))
-    for o in range(features // cut, chunks):
-        mlp[o * cut : (o + 1) * cut] = mlp_all[o, :cut].astype(F32)
-    for o in range(chunks):
-        row = lo_rows(features) + o * rest
-        mlp[row : row + rest] = mlp_all[o, cut:].astype(F32)
-    pending.append(copy(7, mlp.at[pl.ds(features, features)], mlp_out_out))
     for i, (load, to) in enumerate(zip(load_rows, (output, input_grad))):
         load.wait()
         pending.append(copy(8 + i, kept.at[i], to))
@@ -1349,7 +1352,7 @@
             pltpu.VMEM((width, features), F32),
             pltpu.VMEM((head_width, features), F32),
             pltpu.VMEM((2 * features, features), F32),
-            pltpu.SemaphoreType.DMA((10,)),
+            pltpu.SemaphoreType.DMA((10 + 3 * mlp_all.shape[0],)),
         ],
         compiler_params=pltpu.CompilerParams(vmem_limit_bytes=60 << 20),
         name="widen_gradients",

time: 167 us -> 169 us (1.012)
  Pallas kernels: 149 us -> 152 us
    pallas_call x1, Pallas kernels: 64.1 us -> 66.8 us  [back(): pl.pallas_call(functools.partial(back_body, heads, n_hi, n_lo), out_shape...]
where the time goes in v7:
time: 169 us
  Pallas kernels  152 us (90%)
  starting transfers between devices  12.5 us (7%)
  waiting for transfers between devices  2.17 us (1%)
  other arithmetic  1.73 us (1%)
    pallas_call x1, Pallas kernels, back(): pl.pallas_call(functools.partial(back_body, heads, n_hi, n_lo), out_shape...  66.8 us
    pallas_call x1, Pallas kernels, front(): pl.pallas_call(functools.partial(front_body, heads, n_hi, n_lo), out_shap...  48.1 us
    pallas_call x1, Pallas kernels, attn_bwd(): pl.pallas_call(functools.partial(attn_bwd_body, heads), out_shape=(jax.Sh...  15.4 us
    pallas_call x1, Pallas kernels, attn_fwd(): pl.pallas_call(functools.partial(attn_fwd_body, heads), out_shape=(like,...  15.4 us
    ppermute x6, starting transfers between devices, along_hi(): return lax.ppermute(x, 'batch', pairs)  9.44 us
    pallas_call x1, Pallas kernels, widen(): pl.pallas_call(functools.partial(widen_body, heads), out_shape=(like, lik...  6.24 us
  transfers between devices with their start and end apart: 8, of which 1 were waited for; matrix products, arithmetic and copies ran while one was open for 0% of the time, Pallas kernels for 18%

profile of v7, /device:TPU:0, one launch (start us, length us, event | category | flops | bytes accessed | tf_op | source)
XLA Modules:
  0.0 169.3 jit_solution(16635281411682638439)
XLA Ops:
  0.6 48.1 %gather_and_project.1 = (bf16[4,512,384]{2,1,0:T(8,128)(2,1)}, bf16[4,512,384]{2,1,0:T(8,128)(2,1)}, bf16[4,512,384]{2,1,0:T(8,128)(2,1)}, bf16[4,512,384]{2,1,0...) custom-call(bf16[512,768]{1,0:T(8,128)(2,1)} %tokens.1, ...), custom_call_target="tpu_custom_call" | custom-call | tf_op jit(solution)/shard_map/gather_and_project/pallas_call | solution.py:819
  48.8 1.7 collective-permute-start.1
  50.4 2.7 %collective-permute-start.2 = (bf16[2,64,768]{2,1,0:T(8,128)(2,1)}, bf16[2,64,768]{2,1,0:T(8,128)(2,1)S(1)}, u32[]{:S(2)}, u32[]{:S(2)}) collective-permute-start(bf16[2,64,768]{2,1,0:T(8,128)(2,1)} %get-tuple-element.65), channel_id=1, source_target_pairs={{0,16},{4,20},{8,24},{12,28},{16,0},{20,4},{24,8},{28,12},{1,17},{... | collective-permute-start | bytes 589832 | tf_op jit(solution)/shard_map/ppermute | solution.py:1384
  53.1 1.3 collective-permute-start.3
  54.4 1.5 collective-permute-start
  55.9 0.0 copy-start.1
  55.9 0.0 copy-start
  55.9 15.4 %attention_forward.1 = (bf16[4,512,384]{2,1,0:T(8,128)(2,1)}, bf16[4,512,384]{2,1,0:T(8,128)(2,1)}, bf16[4,512,256]{2,1,0:T(8,128)(2,1)}) custom-call(s32[80]{0:T(128)} %len_ref.3, s32[80]{0:T(128)} %group_ref.3, bf16[4,512,384]{2,1,0:T(8,128)(2,1)} %get-tuple-element.56.qa_hbm, bf16[4,512,384]{2,1,0:T(8,128)(2,1)} %get-tuple-element.57.ka_hbm, ...), custom_call_target="tpu_custom_call" | custom-call | flops 8000000000 | bytes 30000000 | tf_op jit(solution)/shard_map/attention_forward/pallas_call | solution.py:303
  71.3 0.0 collective-permute-done.1
  71.3 0.0 collective-permute-done.2
  71.3 0.0 collective-permute-done.3
  71.3 0.0 copy-done.1
  71.3 0.1 fusion.5
  71.4 2.2 %collective-permute-done = bf16[4,128,768]{2,1,0:T(8,128)(2,1)S(1)} collective-permute-done((bf16[4,128,768]{2,1,0:T(8,128)(2,1)}, bf16[4,128,768]{2,1,0:T(8,128)(2,1)S(1)}, u32[]{:S(2)}, u32[]{:S(2)}) %collective-permute-start) | collective-permute-done | bytes 786464 | tf_op jit(solution)/shard_map/ppermute | solution.py:1380
  73.6 0.0 copy-done
  73.6 0.2 fusion.3
  73.8 1.6 collective-permute-start.7
  75.3 0.7 collective-permute-start.4
  76.1 0.3 collective-permute-start.5
  76.4 2.8 %collective-permute-start.6 = (bf16[128,768]{1,0:T(8,128)(2,1)S(1)}, bf16[128,768]{1,0:T(8,128)(2,1)S(1)}, u32[]{:S(2)}, u32[]{:S(2)}) collective-permute-start(bf16[128,768]{1,0:T(8,128)(2,1)S(1)} %get-tuple-element.80), channel_id=1, source_target_pairs={{0,24},{4,28},{8,0},{12,4},{16,8},{20,12},{24,16},{28,20},{1,25},{... | collective-permute-start | bytes 589832 | tf_op jit(solution)/shard_map/ppermute | solution.py:1384
  79.2 15.4 %attention_backward.1 = (bf16[4,512,640]{2,1,0:T(8,128)(2,1)}, f32[8,384]{1,0:T(8,128)}) custom-call(s32[80]{0:T(128)} %len_ref.3, s32[80]{0:T(128)} %group_ref.3, bf16[4,512,384]{2,1,0:T(8,128)(2,1)} %get-tuple-element.67.qb_hbm, bf16[4,512,384]{2,1,0:T(8,128)(2,1)} %get-tuple-element.57.ka_hbm, bf16[4,512,384]{2,1,0:T(8,128)(2,1)} %get-tuple-element.58.va_hbm, ...), custom_call_target="tpu_custom_call" | custom-call | flops 16000000000 | bytes 30000000 | tf_op jit(solution)/shard_map/attention_backward/pallas_call | solution.py:507
  94.5 0.0 collective-permute-done.7
  94.6 0.7 add_convert_fusion.5.own_hi
  95.2 0.0 collective-permute-done.4
  95.2 0.0 collective-permute-done.5
  95.2 0.0 collective-permute-done.6
  95.2 0.8 add_convert_fusion.own_lo
  96.0 66.8 %reduce_gradients.1 = (bf16[512,768]{1,0:T(8,128)(2,1)}, bf16[512,768]{1,0:T(8,128)(2,1)}, bf16[4,2,192,768]{3,2,1,0:T(8,128)(2,1)}, bf16[2,4,192,384]{3,2,1,0:T(8,128)(2,1)}, f32[8,768]{1,0:T(8,128)}) custom-call(bf16[4,512,640]{2,1,0:T(8,128)(2,1)} %get-tuple-element.71.d_qkv_hbm, bf16[4,512,768]{2,1,0:T(8,128)(2,1)} %get-tuple-element.72.nall_hbm, ...), custom_call_target="tpu_custom_call" | custom-call | tf_op jit(solution)/shard_map/reduce_gradients/pallas_call | solution.py:1221
  162.8 6.2 %widen_gradients.1 = (bf16[512,768]{1,0:T(8,128)(2,1)}, bf16[512,768]{1,0:T(8,128)(2,1)}, f32[576,768]{1,0:T(8,128)}, f32[192,768]{1,0:T(8,128)}, f32[768,768]{1...) custom-call(bf16[8,192,768]{2,1,0:T(8,128)(2,1)} %bitcast.17, ...), custom_call_target="tpu_custom_call" | custom-call | tf_op jit(solution)/shard_map/widen_gradients/pallas_call | solution.py:1339
Async XLA Ops:
  48.8 22.5 %collective-permute-start.1 = (bf16[2,64,768]{2,1,0:T(8,128)(2,1)}, bf16[2,64,768]{2,1,0:T(8,128)(2,1)S(1)}, u32[]{:S(2)}, u32[]{:S(2)}) collective-permute-start(bf16[2,64,768]{2,1,0:T(8,128)(2,1)} %get-tuple-element.64), channel_id=1, source_target_pairs={{0,8},{4,12},{8,16},{12,20},{16,24},{20,28},{24,0},{28,4},{1,9},{5... | collective-permute-start | bytes 589832 | tf_op jit(solution)/shard_map/ppermute | solution.py:1384
  50.4 20.8 %collective-permute-start.2 = (bf16[2,64,768]{2,1,0:T(8,128)(2,1)}, bf16[2,64,768]{2,1,0:T(8,128)(2,1)S(1)}, u32[]{:S(2)}, u32[]{:S(2)}) collective-permute-start(bf16[2,64,768]{2,1,0:T(8,128)(2,1)} %get-tuple-element.65), channel_id=1, source_target_pairs={{0,16},{4,20},{8,24},{12,28},{16,0},{20,4},{24,8},{28,12},{1,17},{... | collective-permute-start | bytes 589832 | tf_op jit(solution)/shard_map/ppermute | solution.py:1384
  53.1 18.2 %collective-permute-start.3 = (bf16[2,64,768]{2,1,0:T(8,128)(2,1)}, bf16[2,64,768]{2,1,0:T(8,128)(2,1)S(1)}, u32[]{:S(2)}, u32[]{:S(2)}) collective-permute-start(bf16[2,64,768]{2,1,0:T(8,128)(2,1)} %get-tuple-element.66), channel_id=1, source_target_pairs={{0,24},{4,28},{8,0},{12,4},{16,8},{20,12},{24,16},{28,20},{1,25},{... | collective-permute-start | bytes 589832 | tf_op jit(solution)/shard_map/ppermute | solution.py:1384
  54.4 19.2 %collective-permute-start = (bf16[4,128,768]{2,1,0:T(8,128)(2,1)}, bf16[4,128,768]{2,1,0:T(8,128)(2,1)S(1)}, u32[]{:S(2)}, u32[]{:S(2)}) collective-permute-start(bf16[4,128,768]{2,1,0:T(8,128)(2,1)} %get-tuple-element.62), channel_id=1, source_target_pairs={{0,4},{4,0},{8,12},{12,8},{16,20},{20,16},{24,28},{28,24},{1,5},{5... | collective-permute-start | bytes 2359304 | tf_op jit(solution)/shard_map/ppermute | solution.py:1380
  55.9 15.4 %copy-start.1 = (bf16[2,64,768]{2,1,0:T(8,128)(2,1)S(1)}, bf16[2,64,768]{2,1,0:T(8,128)(2,1)}, u32[]{:S(2)}) copy-start(bf16[2,64,768]{2,1,0:T(8,128)(2,1)} %get-tuple-element.63) | copy-start | bytes 589828
  55.9 17.7 %copy-start = (bf16[4,128,768]{2,1,0:T(8,128)(2,1)S(1)}, bf16[4,128,768]{2,1,0:T(8,128)(2,1)}, u32[]{:S(2)}) copy-start(bf16[4,128,768]{2,1,0:T(8,128)(2,1)} %get-tuple-element.61) | copy-start | bytes 2359300
  73.8 20.8 %collective-permute-start.7 = (bf16[64,768]{1,0:T(8,128)(2,1)S(1)}, bf16[64,768]{1,0:T(8,128)(2,1)S(1)}, u32[]{:S(2)}, u32[]{:S(2)}) collective-permute-start(bf16[64,768]{1,0:T(8,128)(2,1)S(1)} %get-tuple-element.82), channel_id=1, source_target_pairs={{0,4},{4,0},{8,12},{12,8},{16,20},{20,16},{24,28},{28,24},{1,5},{5... | collective-permute-start | bytes 294920 | tf_op jit(solution)/shard_map/ppermute | solution.py:1380
  75.3 19.9 %collective-permute-start.4 = (bf16[128,768]{1,0:T(8,128)(2,1)S(1)}, bf16[128,768]{1,0:T(8,128)(2,1)S(1)}, u32[]{:S(2)}, u32[]{:S(2)}) collective-permute-start(bf16[128,768]{1,0:T(8,128)(2,1)S(1)} %get-tuple-element.78), channel_id=1, source_target_pairs={{0,8},{4,12},{8,16},{12,20},{16,24},{20,28},{24,0},{28,4},{1,9},{5... | collective-permute-start | bytes 589832 | tf_op jit(solution)/shard_map/ppermute | solution.py:1384
  76.1 19.2 %collective-permute-start.5 = (bf16[128,768]{1,0:T(8,128)(2,1)S(1)}, bf16[128,768]{1,0:T(8,128)(2,1)S(1)}, u32[]{:S(2)}, u32[]{:S(2)}) collective-permute-start(bf16[128,768]{1,0:T(8,128)(2,1)S(1)} %get-tuple-element.79), channel_id=1, source_target_pairs={{0,16},{4,20},{8,24},{12,28},{16,0},{20,4},{24,8},{28,12},{1,17},{... | collective-permute-start | bytes 589832 | tf_op jit(solution)/shard_map/ppermute | solution.py:1384
  76.4 18.9 %collective-permute-start.6 = (bf16[128,768]{1,0:T(8,128)(2,1)S(1)}, bf16[128,768]{1,0:T(8,128)(2,1)S(1)}, u32[]{:S(2)}, u32[]{:S(2)}) collective-permute-start(bf16[128,768]{1,0:T(8,128)(2,1)S(1)} %get-tuple-element.80), channel_id=1, source_target_pairs={{0,24},{4,28},{8,0},{12,4},{16,8},{20,12},{24,16},{28,20},{1,25},{... | collective-permute-start | bytes 589832 | tf_op jit(solution)/shard_map/ppermute | solution.py:1384

commit v8 on v7

--- a/solution.py
+++ b/solution.py
@@ -1315,12 +1315,15 @@
     for o in range(n_lo * n_hi):
         row = o % per_half * chunk_rows
         joint[o // per_half, row : row + chunk_rows] = joint_all[o % n_lo, o // n_lo]
+    for i, place in enumerate(kind_order(heads)):
+        for half in range(2):
+            at = slice(half * cols, (half + 1) * cols)
+            qkv_t[place * DH : (place + 1) * DH, at] = joint[half, i * DH : (i + 1) * DH].astype(F32)
+        rows_at = pl.ds(place * DH, DH)
+        pending.append(copy(10 + 3 * chunks + i, qkv_t.at[rows_at], qkv_out.at[rows_at]))
     for half in range(2):
-        at = slice(half * cols, (half + 1) * cols)
-        attn[:, at] = joint[half, width:].astype(F32)
-        for i, place in enumerate(kind_order(heads)):
-            qkv_t[place * DH : (place + 1) * DH, at] = joint[half, i * DH : (i + 1) * DH].astype(F32)
-    pending += [copy(4, qkv_t, qkv_out), copy(5, attn, attn_out)]
+        attn[:, half * cols : (half + 1) * cols] = joint[half, width:].astype(F32)
+    pending.append(copy(5, attn, attn_out))
     for i, (load, to) in enumerate(zip(load_rows, (output, input_grad))):
         load.wait()
         pending.append(copy(8 + i, kept.at[i], to))
@@ -1352,7 +1355,7 @@
             pltpu.VMEM((width, features), F32),
             pltpu.VMEM((head_width, features), F32),
             pltpu.VMEM((2 * features, features), F32),
-            pltpu.SemaphoreType.DMA((10 + 3 * mlp_all.shape[0],)),
+            pltpu.SemaphoreType.DMA((10 + 3 * mlp_all.shape[0] + 3 * heads,)),
         ],
         compiler_params=pltpu.CompilerParams(vmem_limit_bytes=60 << 20),
         name="widen_gradients",

time: 169 us -> 166 us (0.982)
  Pallas kernels: 152 us -> 150 us
    pallas_call x1, Pallas kernels: 66.8 us -> 58.3 us  [back(): pl.pallas_call(functools.partial(back_body, heads, n_hi, n_lo), out_shape...]
    pallas_call x1, Pallas kernels: 15.4 us -> 21.1 us  [attn_bwd(): pl.pallas_call(functools.partial(attn_bwd_body, heads), out_shape=(jax.Sh...]
  transfers between devices with their start and end apart: 8 -> 8, of which waited for: 1 -> 1; matrix products, arithmetic and copies ran while one was open for 0% -> 0% of each run, Pallas kernels for 18% -> 22%
where the time goes in v8:
time: 166 us; the launch traced here: 167 us
  Pallas kernels  150 us (90%)
  starting transfers between devices  12.5 us (8%)
  other arithmetic  1.73 us (1%)
    pallas_call x1, Pallas kernels, back(): pl.pallas_call(functools.partial(back_body, heads, n_hi, n_lo), out_shape...  58.3 us
    pallas_call x1, Pallas kernels, front(): pl.pallas_call(functools.partial(front_body, heads, n_hi, n_lo), out_shap...  48.1 us
    pallas_call x1, Pallas kernels, attn_bwd(): pl.pallas_call(functools.partial(attn_bwd_body, heads), out_shape=(jax.Sh...  21.1 us
    pallas_call x1, Pallas kernels, attn_fwd(): pl.pallas_call(functools.partial(attn_fwd_body, heads), out_shape=(like,...  16.3 us
    ppermute x6, starting transfers between devices, along_hi(): return lax.ppermute(x, 'batch', pairs)  9.44 us
    pallas_call x1, Pallas kernels, widen(): pl.pallas_call(functools.partial(widen_body, heads), out_shape=(like, lik...  6.32 us
  transfers between devices with their start and end apart: 8, of which 1 were waited for; matrix products, arithmetic and copies ran while one was open for 0% of the time, Pallas kernels for 22%

profile of v8, /device:TPU:0, one launch (start us, length us, event | category | flops | bytes accessed | tf_op | source)
XLA Modules:
  0.0 166.5 jit_solution(16627976814149991611)
XLA Ops:
  0.6 48.1 %gather_and_project.1 = (bf16[4,512,384]{2,1,0:T(8,128)(2,1)}, bf16[4,512,384]{2,1,0:T(8,128)(2,1)}, bf16[4,512,384]{2,1,0:T(8,128)(2,1)}, bf16[4,512,384]{2,1,0...) custom-call(bf16[512,768]{1,0:T(8,128)(2,1)} %tokens.1, ...), custom_call_target="tpu_custom_call" | custom-call | tf_op jit(solution)/shard_map/gather_and_project/pallas_call | solution.py:819
  48.8 1.7 %collective-permute-start.1 = (bf16[2,64,768]{2,1,0:T(8,128)(2,1)}, bf16[2,64,768]{2,1,0:T(8,128)(2,1)S(1)}, u32[]{:S(2)}, u32[]{:S(2)}) collective-permute-start(bf16[2,64,768]{2,1,0:T(8,128)(2,1)} %get-tuple-element.64), channel_id=1, source_target_pairs={{0,8},{4,12},{8,16},{12,20},{16,24},{20,28},{24,0},{28,4},{1,9},{5... | collective-permute-start | bytes 589832 | tf_op jit(solution)/shard_map/ppermute | solution.py:1387
  50.4 2.7 %collective-permute-start.2 = (bf16[2,64,768]{2,1,0:T(8,128)(2,1)}, bf16[2,64,768]{2,1,0:T(8,128)(2,1)S(1)}, u32[]{:S(2)}, u32[]{:S(2)}) collective-permute-start(bf16[2,64,768]{2,1,0:T(8,128)(2,1)} %get-tuple-element.65), channel_id=1, source_target_pairs={{0,16},{4,20},{8,24},{12,28},{16,0},{20,4},{24,8},{28,12},{1,17},{... | collective-permute-start | bytes 589832 | tf_op jit(solution)/shard_map/ppermute | solution.py:1387
  53.1 1.3 collective-permute-start.3
  54.4 1.5 collective-permute-start
  55.9 0.0 copy-start.1
  55.9 0.0 copy-start
  55.9 16.3 %attention_forward.1 = (bf16[4,512,384]{2,1,0:T(8,128)(2,1)}, bf16[4,512,384]{2,1,0:T(8,128)(2,1)}, bf16[4,512,256]{2,1,0:T(8,128)(2,1)}) custom-call(s32[80]{0:T(128)} %len_ref.3, s32[80]{0:T(128)} %group_ref.3, bf16[4,512,384]{2,1,0:T(8,128)(2,1)} %get-tuple-element.56.qa_hbm, bf16[4,512,384]{2,1,0:T(8,128)(2,1)} %get-tuple-element.57.ka_hbm, ...), custom_call_target="tpu_custom_call" | custom-call | flops 8000000000 | bytes 30000000 | tf_op jit(solution)/shard_map/attention_forward/pallas_call | solution.py:303
  72.2 0.0 collective-permute-done.1
  72.2 0.0 collective-permute-done.2
  72.2 0.0 collective-permute-done.3
  72.2 0.0 copy-done.1
  72.3 0.1 fusion.5
  72.4 1.2 collective-permute-done
  73.6 0.0 copy-done
  73.6 0.2 fusion.3
  73.8 1.6 collective-permute-start.7
  75.3 0.7 collective-permute-start.4
  76.1 0.3 collective-permute-start.5
  76.4 2.8 %collective-permute-start.6 = (bf16[128,768]{1,0:T(8,128)(2,1)S(1)}, bf16[128,768]{1,0:T(8,128)(2,1)S(1)}, u32[]{:S(2)}, u32[]{:S(2)}) collective-permute-start(bf16[128,768]{1,0:T(8,128)(2,1)S(1)} %get-tuple-element.80), channel_id=1, source_target_pairs={{0,24},{4,28},{8,0},{12,4},{16,8},{20,12},{24,16},{28,20},{1,25},{... | collective-permute-start | bytes 589832 | tf_op jit(solution)/shard_map/ppermute | solution.py:1387
  79.2 21.1 %attention_backward.1 = (bf16[4,512,640]{2,1,0:T(8,128)(2,1)}, f32[8,384]{1,0:T(8,128)}) custom-call(s32[80]{0:T(128)} %len_ref.3, s32[80]{0:T(128)} %group_ref.3, bf16[4,512,384]{2,1,0:T(8,128)(2,1)} %get-tuple-element.67.qb_hbm, bf16[4,512,384]{2,1,0:T(8,128)(2,1)} %get-tuple-element.57.ka_hbm, bf16[4,512,384]{2,1,0:T(8,128)(2,1)} %get-tuple-element.58.va_hbm, ...), custom_call_target="tpu_custom_call" | custom-call | flops 16000000000 | bytes 30000000 | tf_op jit(solution)/shard_map/attention_backward/pallas_call | solution.py:507
  100.2 0.0 collective-permute-done.7
  100.2 0.7 add_convert_fusion.5.own_hi
  100.9 0.0 collective-permute-done.4
  100.9 0.0 collective-permute-done.5
  100.9 0.0 collective-permute-done.6
  100.9 0.8 add_convert_fusion.own_lo
  101.7 58.3 %reduce_gradients.1 = (bf16[512,768]{1,0:T(8,128)(2,1)}, bf16[512,768]{1,0:T(8,128)(2,1)}, bf16[4,2,192,768]{3,2,1,0:T(8,128)(2,1)}, bf16[2,4,192,384]{3,2,1,0:T(8,128)(2,1)}, f32[8,768]{1,0:T(8,128)}) custom-call(bf16[4,512,640]{2,1,0:T(8,128)(2,1)} %get-tuple-element.71.d_qkv_hbm, bf16[4,512,768]{2,1,0:T(8,128)(2,1)} %get-tuple-element.72.nall_hbm, ...), custom_call_target="tpu_custom_call" | custom-call | tf_op jit(solution)/shard_map/reduce_gradients/pallas_call | solution.py:1221
  160.0 6.3 %widen_gradients.1 = (bf16[512,768]{1,0:T(8,128)(2,1)}, bf16[512,768]{1,0:T(8,128)(2,1)}, f32[576,768]{1,0:T(8,128)}, f32[192,768]{1,0:T(8,128)}, f32[768,768]{1...) custom-call(bf16[8,192,768]{2,1,0:T(8,128)(2,1)} %bitcast.17, ...), custom_call_target="tpu_custom_call" | custom-call | tf_op jit(solution)/shard_map/widen_gradients/pallas_call | solution.py:1342
Async XLA Ops:
  48.8 23.4 %collective-permute-start.1 = (bf16[2,64,768]{2,1,0:T(8,128)(2,1)}, bf16[2,64,768]{2,1,0:T(8,128)(2,1)S(1)}, u32[]{:S(2)}, u32[]{:S(2)}) collective-permute-start(bf16[2,64,768]{2,1,0:T(8,128)(2,1)} %get-tuple-element.64), channel_id=1, source_target_pairs={{0,8},{4,12},{8,16},{12,20},{16,24},{20,28},{24,0},{28,4},{1,9},{5... | collective-permute-start | bytes 589832 | tf_op jit(solution)/shard_map/ppermute | solution.py:1387
  50.4 21.8 %collective-permute-start.2 = (bf16[2,64,768]{2,1,0:T(8,128)(2,1)}, bf16[2,64,768]{2,1,0:T(8,128)(2,1)S(1)}, u32[]{:S(2)}, u32[]{:S(2)}) collective-permute-start(bf16[2,64,768]{2,1,0:T(8,128)(2,1)} %get-tuple-element.65), channel_id=1, source_target_pairs={{0,16},{4,20},{8,24},{12,28},{16,0},{20,4},{24,8},{28,12},{1,17},{... | collective-permute-start | bytes 589832 | tf_op jit(solution)/shard_map/ppermute | solution.py:1387
  53.1 19.1 %collective-permute-start.3 = (bf16[2,64,768]{2,1,0:T(8,128)(2,1)}, bf16[2,64,768]{2,1,0:T(8,128)(2,1)S(1)}, u32[]{:S(2)}, u32[]{:S(2)}) collective-permute-start(bf16[2,64,768]{2,1,0:T(8,128)(2,1)} %get-tuple-element.66), channel_id=1, source_target_pairs={{0,24},{4,28},{8,0},{12,4},{16,8},{20,12},{24,16},{28,20},{1,25},{... | collective-permute-start | bytes 589832 | tf_op jit(solution)/shard_map/ppermute | solution.py:1387
  54.4 19.2 %collective-permute-start = (bf16[4,128,768]{2,1,0:T(8,128)(2,1)}, bf16[4,128,768]{2,1,0:T(8,128)(2,1)S(1)}, u32[]{:S(2)}, u32[]{:S(2)}) collective-permute-start(bf16[4,128,768]{2,1,0:T(8,128)(2,1)} %get-tuple-element.62), channel_id=1, source_target_pairs={{0,4},{4,0},{8,12},{12,8},{16,20},{20,16},{24,28},{28,24},{1,5},{5... | collective-permute-start | bytes 2359304 | tf_op jit(solution)/shard_map/ppermute | solution.py:1383
  55.9 16.4 %copy-start.1 = (bf16[2,64,768]{2,1,0:T(8,128)(2,1)S(1)}, bf16[2,64,768]{2,1,0:T(8,128)(2,1)}, u32[]{:S(2)}) copy-start(bf16[2,64,768]{2,1,0:T(8,128)(2,1)} %get-tuple-element.63) | copy-start | bytes 589828
  55.9 17.7 %copy-start = (bf16[4,128,768]{2,1,0:T(8,128)(2,1)S(1)}, bf16[4,128,768]{2,1,0:T(8,128)(2,1)}, u32[]{:S(2)}) copy-start(bf16[4,128,768]{2,1,0:T(8,128)(2,1)} %get-tuple-element.61) | copy-start | bytes 2359300
  73.8 26.5 %collective-permute-start.7 = (bf16[64,768]{1,0:T(8,128)(2,1)S(1)}, bf16[64,768]{1,0:T(8,128)(2,1)S(1)}, u32[]{:S(2)}, u32[]{:S(2)}) collective-permute-start(bf16[64,768]{1,0:T(8,128)(2,1)S(1)} %get-tuple-element.82), channel_id=1, source_target_pairs={{0,4},{4,0},{8,12},{12,8},{16,20},{20,16},{24,28},{28,24},{1,5},{5... | collective-permute-start | bytes 294920 | tf_op jit(solution)/shard_map/ppermute | solution.py:1383
  75.3 25.6 %collective-permute-start.4 = (bf16[128,768]{1,0:T(8,128)(2,1)S(1)}, bf16[128,768]{1,0:T(8,128)(2,1)S(1)}, u32[]{:S(2)}, u32[]{:S(2)}) collective-permute-start(bf16[128,768]{1,0:T(8,128)(2,1)S(1)} %get-tuple-element.78), channel_id=1, source_target_pairs={{0,8},{4,12},{8,16},{12,20},{16,24},{20,28},{24,0},{28,4},{1,9},{5... | collective-permute-start | bytes 589832 | tf_op jit(solution)/shard_map/ppermute | solution.py:1387
  76.1 24.8 %collective-permute-start.5 = (bf16[128,768]{1,0:T(8,128)(2,1)S(1)}, bf16[128,768]{1,0:T(8,128)(2,1)S(1)}, u32[]{:S(2)}, u32[]{:S(2)}) collective-permute-start(bf16[128,768]{1,0:T(8,128)(2,1)S(1)} %get-tuple-element.79), channel_id=1, source_target_pairs={{0,16},{4,20},{8,24},{12,28},{16,0},{20,4},{24,8},{28,12},{1,17},{... | collective-permute-start | bytes 589832 | tf_op jit(solution)/shard_map/ppermute | solution.py:1387
  76.4 24.6 %collective-permute-start.6 = (bf16[128,768]{1,0:T(8,128)(2,1)S(1)}, bf16[128,768]{1,0:T(8,128)(2,1)S(1)}, u32[]{:S(2)}, u32[]{:S(2)}) collective-permute-start(bf16[128,768]{1,0:T(8,128)(2,1)S(1)} %get-tuple-element.80), channel_id=1, source_target_pairs={{0,24},{4,28},{8,0},{12,4},{16,8},{20,12},{24,16},{28,20},{1,25},{... | collective-permute-start | bytes 589832 | tf_op jit(solution)/shard_map/ppermute | solution.py:1387
